TPU v7x, 32 devices: a whole 2x2x4 slice. The times are simulated.
32 devices in a mesh: groups: 2 (over y), dp: 4 (over x, core), tensor: 4 (over z).
Axes of the slice: x: 2, y: 2, z: 4, core: 2. Of those that a mesh axis runs over, the one named last changes fastest.
Arguments:
- activations: bfloat16 [15360, 14336], P(('groups', 'dp'), 'tensor'), parts along dimension 0, may hold values from -6 to 6
- out_grads: bfloat16 [15360, 4096], P(('groups', 'dp'), 'tensor'), parts along dimension 0, may hold values from -6 to 6
- proj_in: bfloat16 [64, 14336], P(None, 'tensor'), may hold values from -0.046875 to 0.046875
- proj_out: bfloat16 [64, 4096], P(None, 'tensor'), may hold values from -0.09375 to 0.09375
- hess_inv: float32 [4096, 4096], P('dp', 'tensor'), may hold values from -1 to 2, as said below
- queries: bfloat16 [1536, 4096], P('dp', 'tensor'), may hold values from -6 to 6
Outputs:
- scores: float32 [120, 1536], P(('groups', 'dp'), 'tensor'), parts along dimension 0
There are 2 independent parts, one for each index of `groups`. A program takes and returns all parts, laid end to end along the dimension named above; an argument that names none is the same for every part. Nothing has to cross between parts.
Inputs may be any that keep to these rules, and one draw needn't show every extreme that they name: hess_inv is exactly symmetric.
All inputs are finite; a program needn't handle non-finite values.
Results may differ from a plain program's by a relative error of at most 0.0003.
Values may be sent and summed in bfloat16 or wider, within the bound.
No kernel may reach another device: no remote copies, remote signals or barrier semaphores. Data moves between devices by JAX's collectives and lax.ppermute only.
A program may use at most 128 MiB of HBM per device.

v0:
```python
import math

import jax
import jax.numpy as jnp
from jax import lax
from jax.sharding import PartitionSpec as P

R = 64
SEQ = 128


def sum_both(left, right):
    return lax.psum(jnp.concatenate([left, right], 1), "tensor")


def local(activations, out_grads, proj_in, proj_out, hess_inv, queries):
    contract = (((1,), (1,)), ((), ()))
    highest = lax.Precision.HIGHEST
    left = lax.dot_general(out_grads, proj_out, contract, preferred_element_type=jnp.float32)
    right = lax.dot_general(activations, proj_in, contract, preferred_element_type=jnp.float32)
    examples = left.shape[0] // SEQ
    width = hess_inv.shape[1]
    share = width // R
    scale = 1.0 / math.sqrt(SEQ)
    columns = lax.all_gather(hess_inv, "dp", axis=0, tiled=True)
    first = lax.axis_index("tensor") * share
    stacked = sum_both(left, right).reshape(examples, SEQ, 2 * R)
    left_full = stacked[:, :, :R]
    right_full = stacked[:, :, R:]
    own_left = lax.dynamic_slice_in_dim(left_full, first, share, 2)
    local_grads = (
        jnp.einsum("esa,esb->eab", own_left, right_full, precision=highest).reshape(examples, width)
        * scale
    )
    folded = jnp.dot(
        lax.all_gather(queries, "tensor", axis=1, tiled=True).astype(jnp.float32),
        columns,
        precision=highest,
    )
    partial_scores = lax.dot_general(
        local_grads, lax.all_gather(folded, "dp", axis=0, tiled=True), contract, precision=highest
    )
    shares = lax.psum_scatter(partial_scores, "tensor", scatter_dimension=1, tiled=True)
    return shares * (1.0 / math.sqrt(R * R))


def solution(mesh):
    return jax.shard_map(
        local,
        mesh=mesh,
        in_specs=(
            P(("groups", "dp"), "tensor"),
            P(("groups", "dp"), "tensor"),
            P(None, "tensor"),
            P(None, "tensor"),
            P("dp", "tensor"),
            P("dp", "tensor"),
        ),
        out_specs=P(("groups", "dp"), "tensor"),
        check_vma=False,
    )
```

profile of v0, /device:TPU:0, one launch (start us, length us, event | category | flops | bytes accessed | tf_op | source)
XLA Modules:
  0.0 316.5 jit_solution(3331522000373300326)
XLA Ops:
  6.5 0.0 copy-start
  6.5 0.0 all-gather.4.cloned.1.call-start
  6.5 0.7 all-gather.4.cloned.1.call-update
  7.3 0.0 all-gather.6.cloned.1.call-start
  7.3 0.7 all-gather.6.cloned.1.call-update
  8.0 0.0 all-reduce.2.cloned.1.call-start
  8.1 3.4 %fusion.3 = f32[1920,64]{0,1:T(8,128)S(1)} fusion(bf16[1920,1024]{1,0:T(8,128)(2,1)} %param.7, bf16[64,1024]{1,0:T(8,128)(2,1)} %param.9), kind=kOutput, calls=%fused_computation.6 | convolution fusion | flops 251658240 | bytes 4554752 | tf_op jit(solution)/shard_map/dot_general | solution.py:19
  11.5 0.0 copy-done
  11.5 9.2 %fusion.4 = f32[1920,64]{0,1:T(8,128)S(1)} fusion(bf16[1920,3584]{1,0:T(8,128)(2,1)} %param.6, bf16[64,3584]{1,0:T(8,128)(2,1)S(1)} %copy-done), kind=kOutput, calls=%fused_computation.7 | convolution fusion | flops 880803840 | bytes 14712832 | tf_op jit(solution)/shard_map/dot_general | solution.py:20
  20.6 0.1 pad_maximum_fusion
  20.7 0.3 copy.8
  21.1 1.3 copy.9
  22.4 0.0 all-reduce.2.cloned.1.call-update
  22.4 0.0 all-gather.8.cloned.1.call-start
  22.4 52.7 %all-gather.4.cloned.1.call-done = bf16[384,4096]{1,0:T(8,128)(2,1)} async-done(((bf16[384,1024]{1,0:T(8,128)(2,1)}), bf16[384,4096]{1,0:T(8,128)(2,1)}) %all-gather.4.cloned.1.call-update) | async-done | bytes 3145744 | tf_op jit(solution)/shard_map/all_gather | solution.py:36
  75.1 106.2 %all-gather.6.cloned.1.call-done = f32[4096,1024]{1,0:T(8,128)} async-done(((f32[1024,1024]{1,0:T(8,128)}), f32[4096,1024]{1,0:T(8,128)}) %all-gather.6.cloned.1.call-update) | async-done | bytes 16777232 | tf_op jit(solution)/shard_map/all_gather | solution.py:25
  181.3 15.8 %fusion.5 = f32[384,1024]{1,0:T(8,128)} fusion(bf16[384,4096]{1,0:T(8,128)(2,1)} %all-gather.4.cloned.1.call-done, f32[4096,1024]{1,0:T(8,128)} %all-gather.6.cloned.1.call-done), kind=kOutput, calls=%fused_computation.8 | convolution fusion | flops 19327352832 | bytes 21495808 | tf_op jit(solution)/shard_map/dot_general | solution.py:35
  197.1 0.0 all-gather.8.cloned.1.call-update
  197.2 0.2 reduce-scatter.2.cloned.1.call-start
  197.4 36.1 %all-reduce.2.cloned.1.call-done = f32[15,128,128]{1,2,0:T(8,128)} async-done(((f32[15,128,128]{1,2,0:T(8,128)}), f32[15,128,128]{1,2,0:T(8,128)}) %all-reduce.2.cloned.1.call-update) | async-done | bytes 983056 | tf_op jit(solution)/shard_map/psum | solution.py:13
  233.5 1.1 slice.8
  234.6 1.9 convolution_multiply_fusion
  236.5 0.1 mul.21
  236.6 44.1 %all-gather.8.cloned.1.call-done = f32[1536,1024]{1,0:T(8,128)} async-done(((f32[384,1024]{1,0:T(8,128)}), f32[1536,1024]{1,0:T(8,128)}) %all-gather.8.cloned.1.call-update) | async-done | bytes 6291472 | tf_op jit(solution)/shard_map/all_gather | solution.py:41
  280.8 8.6 %fusion.6 = f32[15,1536]{1,0:T(8,128)} fusion(f32[15,1024]{1,0:T(8,128)S(1)} %mul.21, f32[1536,1024]{1,0:T(8,128)} %all-gather.8.cloned.1.call-done), kind=kOutput, calls=%fused_computation.9 | convolution fusion | flops 283115520 | bytes 6445056 | tf_op jit(solution)/shard_map/dot_general | solution.py:40
  289.3 0.0 reduce-scatter.2.cloned.1.call-update
  289.4 19.3 %reduce-scatter.2.cloned.1.call-done = f32[15,384]{1,0:T(8,128)} async-done(((f32[15,1536]{1,0:T(8,128)}), f32[15,384]{1,0:T(8,128)}) %reduce-scatter.2.cloned.1.call-update) | async-done | bytes 23056 | tf_op jit(solution)/shard_map/reduce_scatter | solution.py:43
  308.6 1.3 broadcast_multiply_fusion
Async XLA Ops:
  6.5 4.9 %copy-start = (bf16[64,3584]{1,0:T(8,128)(2,1)S(1)}, bf16[64,3584]{1,0:T(8,128)(2,1)}, u32[]{:S(2)}) copy-start(bf16[64,3584]{1,0:T(8,128)(2,1)} %param.8) | copy-start | bytes 1376260
  6.5 68.6 %all-gather.4.cloned.1.call-start = ((), (), s32[]{:S(2)}) async-start(), calls=%async_computation.2 | async-start | bytes 3932160 | tf_op jit(solution)/shard_map/all_gather | solution.py:36
  7.3 174.1 %all-gather.6.cloned.1.call-start = ((), (), s32[]{:S(2)}) async-start(), calls=%async_computation.3 | async-start | bytes 20971520 | tf_op jit(solution)/shard_map/all_gather | solution.py:25
  8.0 225.5 %all-reduce.2.cloned.1.call-start = ((), (), s32[]{:S(2)}) async-start(), calls=%async_computation.1 | async-start | bytes 1966080 | tf_op jit(solution)/shard_map/psum | solution.py:13
  22.4 258.4 %all-gather.8.cloned.1.call-start = ((), (), s32[]{:S(2)}) async-start(), calls=%async_computation.4 | async-start | bytes 7864320 | tf_op jit(solution)/shard_map/all_gather | solution.py:41
  197.2 111.5 %reduce-scatter.2.cloned.1.call-start = ((), (), s32[]{:S(2)}) async-start(), calls=%async_computation.5 | async-start | bytes 122880 | tf_op jit(solution)/shard_map/reduce_scatter | solution.py:43
Sparse Core Ops, SparseCore 0:
  8.9 66.1 all-gather.3
  76.7 104.5 all-gather.5
  183.7 49.7 all-reduce.1
  235.0 45.6 all-gather.7
  289.5 19.1 reduce-scatter.1
where the time goes:
time: 317 us
  waiting for transfers between devices  260 us (82%)
  matrix products  38.9 us (12%)
  between operations  13.2 us (4%)
    all_gather x1, waiting for transfers between devices, local(): columns = lax.all_gather(hess_inv, 'dp', axis=0, tiled=True)  106 us
    all_gather x1, waiting for transfers between devices, local(): lax.all_gather(queries, 'tensor', axis=1, tiled=True).astype(jnp.float32)  52.7 us
    all_gather x1, waiting for transfers between devices, local(): lax.all_gather(folded, 'dp', axis=0, tiled=True)  44.1 us
    psum x1, waiting for transfers between devices, sum_both(): return lax.psum(jnp.concatenate([left, right], 1), 'tensor')  36.1 us
    reduce_scatter x1, waiting for transfers between devices, local(): lax.psum_scatter(partial_scores, 'tensor', scatter_dimension=1, tiled=True)  19.3 us
    dot_general x1, matrix products, local(): jnp.dot(lax.all_gather(queries, 'tensor', axis=1, tiled=True).astype(jnp....  15.8 us
    dot_general x1, matrix products, local(): lax.dot_general(activations, proj_in, contract, preferred_element_type=jn...  9.16 us
    dot_general x1, matrix products, local(): lax.dot_general(local_grads, lax.all_gather(folded, 'dp', axis=0, tiled=T...  8.59 us
  transfers between devices with their start and end apart: 5, of which 5 were waited for; matrix products, arithmetic and copies ran while one was open for 10% of the time, Pallas kernels for 0%

commit v1 on v0

v1 whole, which is shorter than its diff:
```python
import functools
import math

import jax
import jax.numpy as jnp
from jax import lax
from jax.experimental import pallas as pl
from jax.experimental.pallas import tpu as pltpu
from jax.sharding import PartitionSpec as P

R = 64
SEQ = 128
LANES = 128
TOP = 128.0
ROWS_CONTRACT = (((1,), (1,)), ((), ()))


def params(mib):
    return pltpu.CompilerParams(vmem_limit_bytes=mib << 20)


def first_example(owner, m, examples):
    return jnp.minimum(owner * m, examples - m)


def bitrev(v, bits):
    out = 0
    for b in range(bits):
        out = out + ((v >> b) & 1) * (1 << (bits - 1 - b))
    return out


def project_kernel(steps, coded, pos, acts, outs, p_in, p_out, y_ref, acc):
    k = pl.program_id(1)
    right = lax.dot_general(acts[...], p_in[...], ROWS_CONTRACT, preferred_element_type=jnp.float32)
    left = lax.dot_general(outs[...], p_out[...], ROWS_CONTRACT, preferred_element_type=jnp.float32)
    both = jnp.concatenate([left, right], 1)

    @pl.when(k == 0)
    def _():
        acc[...] = both

    @pl.when(k > 0)
    def _():
        acc[...] += both

    @pl.when(k == steps - 1)
    def _():
        x = acc[...]
        if not coded:
            y_ref[0] = x
        else:
            rows = x.shape[0]
            top = jnp.maximum(jnp.max(jnp.abs(x), axis=0, keepdims=True), 1e-30)
            top = top.astype(jnp.bfloat16).astype(jnp.float32)
            w = x * (TOP / top)
            s = w * w
            s = s * s
            s = s * s
            s = s * s
            y = jnp.where(x < 0, -s, s)
            y_ref[0, pl.ds(0, rows), :] = y.astype(jnp.bfloat16)
            y_ref[0, pl.ds(rows, 16), :] = jnp.broadcast_to(top, (16, LANES)).astype(jnp.bfloat16)


def project(pos, acts, outs, p_in, p_out, shifts, coded, n, m):
    examples = acts.shape[0] // SEQ
    rows = m * SEQ
    steps = 1
    for c in (8, 4, 2):
        if acts.shape[1] % (c * LANES) == 0 and outs.shape[1] % (c * LANES) == 0:
            steps = c
            break
    wide_in, wide_out = acts.shape[1] // steps, outs.shape[1] // steps
    first, stride = shifts[0], (shifts[1] - shifts[0] if len(shifts) > 1 else 0)

    def start(i, pos):
        owner = lax.rem(pos[1] + first + stride * i, n)
        return first_example(owner, m, examples) * SEQ

    out_rows = rows + 16 if coded else rows
    dtype = jnp.bfloat16 if coded else jnp.float32
    count = len(shifts)
    return pl.pallas_call(
        functools.partial(project_kernel, steps, coded),
        grid_spec=pltpu.PrefetchScalarGridSpec(
            num_scalar_prefetch=1,
            grid=(count, steps),
            in_specs=[
                pl.BlockSpec((pl.Element(rows), pl.Element(wide_in)), lambda i, k, pos: (start(i, pos), k * wide_in)),
                pl.BlockSpec((pl.Element(rows), pl.Element(wide_out)), lambda i, k, pos: (start(i, pos), k * wide_out)),
                pl.BlockSpec((R, wide_in), lambda i, k, pos: (0, k)),
                pl.BlockSpec((R, wide_out), lambda i, k, pos: (0, k)),
            ],
            out_specs=pl.BlockSpec((1, out_rows, LANES), lambda i, k, pos: (i, 0, 0)),
            scratch_shapes=[pltpu.VMEM((rows, LANES), jnp.float32)],
        ),
        out_shape=jax.ShapeDtypeStruct((count, out_rows, LANES), dtype),
        compiler_params=params(24),
        cost_estimate=pl.CostEstimate(
            flops=8 * count * rows * (acts.shape[1] + outs.shape[1]) * R,
            bytes_accessed=2 * count * rows * (acts.shape[1] + outs.shape[1]),
            transcendentals=0,
        ),
    )(pos, acts, outs, p_in, p_out)


def grads_kernel(n, m, bits, pos, own, *refs):
    coded, out, z = refs[: n - 1], refs[n - 1], refs[n]
    rows = m * SEQ
    x = own[...]
    for ref in coded:
        y = ref[pl.ds(0, rows), :].astype(jnp.float32)
        top = ref[pl.ds(rows, 1), :].astype(jnp.float32) * (1.0 / TOP)
        w = jnp.sqrt(jnp.sqrt(jnp.sqrt(jnp.sqrt(jnp.abs(y)))))
        x = x + jnp.where(y < 0, -w, w) * top
    half = R // n // 2
    d = pos[0]
    for e in range(m):
        xe = x[e * SEQ : (e + 1) * SEQ, :]
        z[...] = lax.dot_general(
            xe.T, xe, (((1,), (0,)), ((), ())), precision=lax.Precision.HIGHEST, preferred_element_type=jnp.float32
        )
        for j in range(n):
            at = bitrev(lax.bitwise_xor(d, j), bits)
            even = z[pl.ds(2 * half * j, half, stride=2), :]
            odd = z[pl.ds(2 * half * j + 1, half, stride=2), :]
            out[at, :, e, :] = jnp.concatenate([even[:, R:], odd[:, R:]], 1)


def grads_of(pos, own, coded, n, m, bits):
    half = R // n // 2
    return pl.pallas_call(
        functools.partial(grads_kernel, n, m, bits),
        in_specs=[pl.BlockSpec(memory_space=pltpu.SMEM)] + [pl.BlockSpec(memory_space=pltpu.VMEM)] * n,
        out_specs=pl.BlockSpec(memory_space=pltpu.VMEM),
        out_shape=jax.ShapeDtypeStruct((n, half, m, LANES), jnp.float32),
        scratch_shapes=[pltpu.VMEM((SEQ, LANES), jnp.float32)],
        compiler_params=params(24),
    )(pos, own, *coded)


def split(v):
    hi = v.astype(jnp.bfloat16)
    return hi, (v - hi.astype(jnp.float32)).astype(jnp.bfloat16)


def scores_kernel(n, m, bits, pos, h_hi, h_lo, queries, *refs):
    grads, out, a = refs[:n], refs[n], refs[n + 1]
    half = grads[0].shape[0]
    group = n * m
    rows = n * group
    for p in range(n):
        for r in range(half):
            a[pl.ds(p * group, group), pl.ds(r * LANES, LANES)] = grads[p][r]
    contract = (((1,), (0,)), ((), ()))
    hi, lo = split(a[...])
    top = lax.dot_general(jnp.concatenate([hi, lo], 0), h_hi[...], contract, preferred_element_type=jnp.float32)
    low = lax.dot_general(hi, h_lo[...], contract, preferred_element_type=jnp.float32)
    hi, lo = split(top[:rows] + top[rows:] + low)
    both = jnp.concatenate([hi, lo], 0)
    d, t = pos[0], pos[1]

    def one(u):
        block = bitrev(lax.bitwise_xor(d, lax.rem(t + u, n)), bits)
        s = lax.dot_general(both, queries[block], ROWS_CONTRACT, preferred_element_type=jnp.float32)
        s = s[:rows] + s[rows:]
        for p in range(n):
            owner = lax.rem(t - p + n, n)
            for b in range(n):
                at = p * group + b * m
                out[b, u, owner] = s[at : at + m]

    if n <= 4:
        for u in range(n):
            one(u)
    else:
        lax.fori_loop(0, n, lambda u, c: (one(u), c)[1], 0)


def scores_of(pos, h_hi, h_lo, queries, grads, n, m, bits):
    half, group, _ = grads[0].shape
    width = queries.shape[1]
    rows = n * group
    return pl.pallas_call(
        functools.partial(scores_kernel, n, m, bits),
        in_specs=[pl.BlockSpec(memory_space=pltpu.SMEM)] + [pl.BlockSpec(memory_space=pltpu.VMEM)] * (3 + n),
        out_specs=pl.BlockSpec(memory_space=pltpu.VMEM),
        out_shape=jax.ShapeDtypeStruct((n, n, n, m, width), jnp.float32),
        scratch_shapes=[pltpu.VMEM((rows, half * LANES), jnp.float32)],
        compiler_params=params(40),
    )(pos, h_hi, h_lo, queries, *grads)


def local(n, activations, out_grads, proj_in, proj_out, hess_inv, queries):
    bits = n.bit_length() - 1
    examples = activations.shape[0] // SEQ
    m = -(-examples // n)
    pos = jnp.stack([lax.axis_index("dp"), lax.axis_index("tensor")]).astype(jnp.int32)

    def shift(v, s):
        return lax.ppermute(v, "tensor", [(i, (i + s) % n) for i in range(n)])

    def flip(v, mask):
        return lax.ppermute(v, "dp", [(i, i ^ mask) for i in range(n)])

    all_q = queries[None]
    for b in reversed(range(bits)):
        all_q = jnp.concatenate([all_q, flip(all_q, 1 << b)], 0)

    order = sorted(range(1, n), key=lambda s: -min(s, n - s))
    sent = {}
    for s in order:
        y = project(pos, activations, out_grads, proj_in, proj_out, (s,), True, n, m)
        sent[s] = shift(y[0], s)
    own = project(pos, activations, out_grads, proj_in, proj_out, (0,), False, n, m)[0]

    h_top = lax.reduce_precision(hess_inv, 8, 7)
    h_hi = h_top.astype(jnp.bfloat16)
    h_lo = (hess_inv - h_top).astype(jnp.bfloat16)

    grads = grads_of(pos, own, [sent[s] for s in order], n, m, bits)
    parts = [grads[0]] + [flip(grads[p], bitrev(p, bits)) for p in range(1, n)]
    group = jnp.concatenate(parts, 1)
    groups = [group] + [shift(group, s) for s in range(1, n)]

    out = scores_of(pos, h_hi, h_lo, all_q, groups, n, m, bits)
    for b in range(bits):
        half = out.shape[0] // 2
        out = out[:half] + flip(out[half:], 1 << b)
    out = out[0]
    total = out[0]
    for s in range(1, n):
        total = total + shift(out[s], s)
    width = total.shape[-1]
    total = total.reshape(n * m, width)
    rows, i = [], 0
    while i < examples:
        owner = min(i // m, n - 1)
        begin = min(owner * m, examples - m)
        stop = begin + m
        rows.append(total[owner * m + i - begin : owner * m + stop - begin])
        i = stop
    scale = (1.0 / math.sqrt(SEQ)) * (1.0 / math.sqrt(R * R))
    return jnp.concatenate(rows, 0)[:examples] * scale


def solution(mesh):
    n = mesh.shape["tensor"]
    return jax.shard_map(
        functools.partial(local, n),
        mesh=mesh,
        in_specs=(
            P(("groups", "dp"), "tensor"),
            P(("groups", "dp"), "tensor"),
            P(None, "tensor"),
            P(None, "tensor"),
            P("dp", "tensor"),
            P("dp", "tensor"),
        ),
        out_specs=P(("groups", "dp"), "tensor"),
        check_vma=False,
    )
```

time: 317 us -> 87.1 us (0.27)
  waiting for transfers between devices: 260 us -> 38.3 us
  matrix products: 38.9 us -> 0 us
  Pallas kernels: 0 us -> 18.5 us
  starting transfers between devices: 0.34 us -> 18 us
  between operations: 13.2 us -> 0.2 us
  local copies, waits for them, and re-layouts: 2.81 us -> 7.11 us
  other arithmetic: 1.41 us -> 4.73 us
    all_gather x3 -> x0, waiting for transfers between devices: 203 us -> none  [the longest x1 106 us: local(): columns = lax.all_gather(hess_inv, 'dp', axis=0, tiled=True)]
    dot_general x5 -> x0, matrix products: 38.9 us -> none  [the longest x1 15.8 us: local(): jnp.dot(lax.all_gather(queries, 'tensor', axis=1, tiled=True).astype(jnp....]
    ppermute x0 -> x16, waiting for transfers between devices: none -> 38.3 us  [the longest x7 25.7 us: flip(): return lax.ppermute(v, 'dp', [(i, i ^ mask) for i in range(n)])]
    psum x1 -> x0, waiting for transfers between devices: 36.1 us -> none  [sum_both(): return lax.psum(jnp.concatenate([left, right], 1), 'tensor')]
    reduce_scatter x1 -> x0, waiting for transfers between devices: 19.3 us -> none  [local(): lax.psum_scatter(partial_scores, 'tensor', scatter_dimension=1, tiled=True)]
    pallas_call x0 -> x6, Pallas kernels: none -> 18.5 us  [the longest x4 14.4 us: project(): pl.pallas_call(functools.partial(project_kernel, steps, coded), grid_spec...]
    ppermute x0 -> x16, starting transfers between devices: none -> 18 us  [the longest x9 12.1 us: shift(): return lax.ppermute(v, 'tensor', [(i, (i + s) % n) for i in range(n)])]
    unnamed x2 -> x12, local copies, waits for them, and re-layouts: 0.01 us -> 7.04 us
  transfers between devices with their start and end apart: 5 -> 16, of which waited for: 5 -> 10; matrix products, arithmetic and copies ran while one was open for 10% -> 3% of each run, Pallas kernels for 0% -> 19%
where the time goes in v1:
time: 87.1 us; the launch traced here: 86.8 us
  waiting for transfers between devices  38.3 us (44%)
  Pallas kernels  18.5 us (21%)
  starting transfers between devices  18 us (21%)
  local copies, waits for them, and re-layouts  7.11 us (8%)
  other arithmetic  4.73 us (5%)
    ppermute x7, waiting for transfers between devices, flip(): return lax.ppermute(v, 'dp', [(i, i ^ mask) for i in range(n)])  25.7 us
    pallas_call x4, Pallas kernels, project(): pl.pallas_call(functools.partial(project_kernel, steps, coded), grid_spec...  14.4 us
    ppermute x9, waiting for transfers between devices, shift(): return lax.ppermute(v, 'tensor', [(i, (i + s) % n) for i in range(n)])  12.5 us
    ppermute x9, starting transfers between devices, shift(): return lax.ppermute(v, 'tensor', [(i, (i + s) % n) for i in range(n)])  12.1 us
    unnamed x12, local copies, waits for them, and re-layouts  7.04 us
    ppermute x7, starting transfers between devices, flip(): return lax.ppermute(v, 'dp', [(i, i ^ mask) for i in range(n)])  5.88 us
    concatenate x2, other arithmetic, local(): all_q = jnp.concatenate([all_q, flip(all_q, 1 << b)], 0)  2.99 us
    pallas_call x1, Pallas kernels, scores_of(): pl.pallas_call(functools.partial(scores_kernel, n, m, bits), in_specs=[pl...  2.25 us
  transfers between devices with their start and end apart: 16, of which 10 were waited for; matrix products, arithmetic and copies ran while one was open for 3% of the time, Pallas kernels for 19%

profile of v1, /device:TPU:0, one launch (start us, length us, event | category | flops | bytes accessed | tf_op | source)
XLA Modules:
  0.0 86.8 jit_solution(4873528995599744419)
XLA Ops:
  0.0 2.9 %collective-permute-start = (bf16[1,384,1024]{2,1,0:T(8,128)(2,1)}, bf16[1,384,1024]{2,1,0:T(8,128)(2,1)S(1)}, u32[]{:S(2)}, u32[]{:S(2)}) collective-permute-start(bf16[1,384,1024]{2,1,0:T(8,128)(2,1)} %bitcast.39), channel_id=1, source_target_pairs={{0,8},{4,12},{8,0},{12,4},{1,9},{5,13},{9,1},{13,5},{2,10},{6,14},... | collective-permute-start | bytes 2359304 | tf_op jit(solution)/shard_map/ppermute | solution.py:205
  2.9 17.7 %collective-permute-done = bf16[1,384,1024]{2,1,0:T(8,128)(2,1)S(1)} collective-permute-done((bf16[1,384,1024]{2,1,0:T(8,128)(2,1)}, bf16[1,384,1024]{2,1,0:T(8,128)(2,1)S(1)}, u32[]{:S(2)}, u32[]{:S(2)}) %collective-permute-start) | collective-permute-done | bytes 786464 | tf_op jit(solution)/shard_map/ppermute | solution.py:205
  20.7 1.3 %pad_maximum_fusion.1 = bf16[2,384,1024]{2,1,0:T(8,128)(2,1)S(1)} fusion(bf16[1,384,1024]{2,1,0:T(8,128)(2,1)S(1)} %collective-permute-done, bf16[1,384,1024]{2,1,0:T(8,128)(2,1)} %bitcast.40), kind=kLoop, calls=%fused_computation.4 | loop fusion | flops 786432 | bytes 3145728 | tf_op jit(solution)/shard_map/concatenate | solution.py:209
  22.1 4.9 %copy-done = bf16[1920,3584]{1,0:T(8,128)(2,1)S(1)} copy-done((bf16[1920,3584]{1,0:T(8,128)(2,1)S(1)}, bf16[1920,3584]{1,0:T(8,128)(2,1)}, u32[]{:S(2)}) %copy-start) | copy-done | bytes 13762584
  27.1 2.1 %copy-done.1 = bf16[1920,1024]{1,0:T(8,128)(2,1)S(1)} copy-done((bf16[1920,1024]{1,0:T(8,128)(2,1)S(1)}, bf16[1920,1024]{1,0:T(8,128)(2,1)}, u32[]{:S(2)}) %copy-start.1) | copy-done | bytes 3932184
  29.2 3.6 %shard_map.66 = bf16[1,528,128]{2,1,0:T(8,128)(2,1)S(1)} custom-call(s32[2]{0:T(128)S(1)} %pad_add_fusion.pos, bf16[1920,3584]{1,0:T(8,128)(2,1)S(1)} %copy-done, bf16[1920,1024]{1,0:T(8,128)(2,1)S(1)} %copy-done.1, bf16[64,3584]{1,0:T(8,128)(2,1)S(1)} %copy-done.2, bf16[64,1024]{1,0:T(8,128)(2,1)S(1)} %copy-done.3), custom_call_target="tpu_custom_call" | custom-call | flops 1207959552 | bytes 4718592 | tf_op jit(solution)/shard_map/pallas_call | solution.py:84
  32.8 1.9 %collective-permute-start.3 = (bf16[528,128]{1,0:T(8,128)(2,1)S(1)}, bf16[528,128]{1,0:T(8,128)(2,1)S(1)}, u32[]{:S(2)}, u32[]{:S(2)}) collective-permute-start(bf16[528,128]{1,0:T(8,128)(2,1)S(1)} %bitcast.36), channel_id=1, source_target_pairs={{0,1},{1,2},{2,3},{3,0},{4,5},{5,6},{6,7},{7,4},{8,9},{9,10},{10,1... | collective-permute-start | bytes 405512 | tf_op jit(solution)/shard_map/ppermute | solution.py:202
  34.7 3.6 %shard_map.67 = bf16[1,528,128]{2,1,0:T(8,128)(2,1)S(1)} custom-call(s32[2]{0:T(128)S(1)} %pad_add_fusion.pos, bf16[1920,3584]{1,0:T(8,128)(2,1)S(1)} %copy-done, bf16[1920,1024]{1,0:T(8,128)(2,1)S(1)} %copy-done.1, bf16[64,3584]{1,0:T(8,128)(2,1)S(1)} %copy-done.2, bf16[64,1024]{1,0:T(8,128)(2,1)S(1)} %copy-done.3), custom_call_target="tpu_custom_call" | custom-call | flops 1207959552 | bytes 4718592 | tf_op jit(solution)/shard_map/pallas_call | solution.py:84
  38.3 2.1 %collective-permute-start.4 = (bf16[528,128]{1,0:T(8,128)(2,1)S(1)}, bf16[528,128]{1,0:T(8,128)(2,1)S(1)}, u32[]{:S(2)}, u32[]{:S(2)}) collective-permute-start(bf16[528,128]{1,0:T(8,128)(2,1)S(1)} %bitcast.37), channel_id=1, source_target_pairs={{0,3},{1,0},{2,1},{3,2},{4,7},{5,4},{6,5},{7,6},{8,11},{9,8},{10,9... | collective-permute-start | bytes 405512 | tf_op jit(solution)/shard_map/ppermute | solution.py:202
  40.4 3.6 %shard_map.65 = bf16[1,528,128]{2,1,0:T(8,128)(2,1)S(1)} custom-call(s32[2]{0:T(128)S(1)} %pad_add_fusion.pos, bf16[1920,3584]{1,0:T(8,128)(2,1)S(1)} %copy-done, bf16[1920,1024]{1,0:T(8,128)(2,1)S(1)} %copy-done.1, bf16[64,3584]{1,0:T(8,128)(2,1)S(1)} %copy-done.2, bf16[64,1024]{1,0:T(8,128)(2,1)S(1)} %copy-done.3), custom_call_target="tpu_custom_call" | custom-call | flops 1207959552 | bytes 4718592 | tf_op jit(solution)/shard_map/pallas_call | solution.py:84
  44.0 1.0 %collective-permute-start.2 = (bf16[528,128]{1,0:T(8,128)(2,1)S(1)}, bf16[528,128]{1,0:T(8,128)(2,1)S(1)}, u32[]{:S(2)}, u32[]{:S(2)}) collective-permute-start(bf16[528,128]{1,0:T(8,128)(2,1)S(1)} %bitcast.38), channel_id=1, source_target_pairs={{0,2},{1,3},{2,0},{3,1},{4,6},{5,7},{6,4},{7,5},{8,10},{9,11},{10,... | collective-permute-start | bytes 405512 | tf_op jit(solution)/shard_map/ppermute | solution.py:202
  45.1 3.5 %shard_map.64 = f32[1,512,128]{2,1,0:T(8,128)S(1)} custom-call(s32[2]{0:T(128)S(1)} %pad_add_fusion.pos, bf16[1920,3584]{1,0:T(8,128)(2,1)S(1)} %copy-done, bf16[1920,1024]{1,0:T(8,128)(2,1)S(1)} %copy-done.1, bf16[64,3584]{1,0:T(8,128)(2,1)S(1)} %copy-done.2, bf16[64,1024]{1,0:T(8,128)(2,1)S(1)} %copy-done.3), custom_call_target="tpu_custom_call" | custom-call | flops 1207959552 | bytes 4718592 | tf_op jit(solution)/shard_map/pallas_call | solution.py:84
  48.6 4.1 %collective-permute-done.2.refs_0_ = bf16[528,128]{1,0:T(8,128)(2,1)S(1)} collective-permute-done((bf16[528,128]{1,0:T(8,128)(2,1)S(1)}, bf16[528,128]{1,0:T(8,128)(2,1)S(1)}, u32[]{:S(2)}, u32[]{:S(2)}) %collective-permute-start.2) | collective-permute-done | bytes 135200 | tf_op jit(solution)/shard_map/ppermute | solution.py:202
  52.8 1.9 %shard_map.68 = f32[4,8,4,128]{3,2,1,0:T(4,128)S(1)} custom-call(s32[2]{0:T(128)S(1)} %pad_add_fusion.pos, f32[512,128]{1,0:T(8,128)S(1)} %bitcast.35, bf16[528,128]{1,0:T(8,128)(2,1)S(1)} %collective-permute-done.2.refs_0_, bf16[528,128]{1,0:T(8,128)(2,1)S(1)} %collective-permute-done.3.refs_1_, bf16[528,128]{1,0:T(8,128)(2,1)S(1)} %collective-permute-done.4.refs_2_), custom_call_target="tpu_custom_call" | custom-call | tf_op jit(solution)/shard_map/pallas_call | solution.py:133
  54.7 1.2 %collective-permute-start.7 = (f32[8,4,128]{2,1,0:T(4,128)S(1)}, f32[8,4,128]{2,1,0:T(4,128)S(1)}, u32[]{:S(2)}, u32[]{:S(2)}) collective-permute-start(f32[8,4,128]{2,1,0:T(4,128)S(1)} %get-tuple-element.11), channel_id=1, source_target_pairs={{0,12},{4,8},{8,4},{12,0},{1,13},{5,9},{9,5},{13,1},{2,14},{6,10},... | collective-permute-start | bytes 49160 | tf_op jit(solution)/shard_map/ppermute | solution.py:205
  55.9 0.5 collective-permute-start.6
  56.4 0.5 collective-permute-start.5
  56.9 0.9 %fusion = (bf16[1024,1024]{1,0:T(8,128)(2,1)S(1)}, bf16[1024,1024]{1,0:T(8,128)(2,1)S(1)}) fusion(f32[1024,1024]{1,0:T(8,128)S(1)} %copy-done.4), kind=kLoop, calls=%fused_computation.2 | loop fusion | flops 4194304 | bytes 8388608 | tf_op jit(solution)/shard_map/convert_element_type | solution.py:220
  57.9 2.2 %collective-permute-done.5 = f32[8,4,128]{2,1,0:T(4,128)S(1)} collective-permute-done((f32[8,4,128]{2,1,0:T(4,128)S(1)}, f32[8,4,128]{2,1,0:T(4,128)S(1)}, u32[]{:S(2)}, u32[]{:S(2)}) %collective-permute-start.5) | collective-permute-done | bytes 16416 | tf_op jit(solution)/shard_map/ppermute | solution.py:205
  60.1 2.5 %collective-permute-start.10 = (f32[8,16,128]{2,1,0:T(8,128)S(1)}, f32[8,16,128]{2,1,0:T(8,128)S(1)}, u32[]{:S(2)}, u32[]{:S(2)}) collective-permute-start(f32[8,16,128]{2,1,0:T(8,128)S(1)} %pad_maximum_fusion.2.refs_0_), channel_id=1, source_target_pairs={{0,3},{1,0},{2,1},{3,2},{4,7},{5,4},{6,5},{7,6},{8,11},{9,8},{10,9... | collective-permute-start | bytes 196616 | tf_op jit(solution)/shard_map/ppermute | solution.py:202
  62.6 0.6 collective-permute-start.8
  63.3 1.7 %pad_maximum_fusion.queries = bf16[4,384,1024]{2,1,0:T(8,128)(2,1)S(1)} fusion(bf16[2,384,1024]{2,1,0:T(8,128)(2,1)} %collective-permute-done.1, bf16[1,384,1024]{2,1,0:T(8,128)(2,1)S(1)} %collective-permute-done, bf16[1,384,1024]{2,1,0:T(8,128)(2,1)S(1)} %bitcast.41), kind=kLoop, calls=%fused_computation.3 | loop fusion | flops 3145728 | bytes 6291456 | tf_op jit(solution)/shard_map/concatenate | solution.py:209
  65.0 2.8 %collective-permute-done.9.refs_2_ = f32[8,16,128]{2,1,0:T(8,128)S(1)} collective-permute-done((f32[8,16,128]{2,1,0:T(8,128)S(1)}, f32[8,16,128]{2,1,0:T(8,128)S(1)}, u32[]{:S(2)}, u32[]{:S(2)}) %collective-permute-start.9) | collective-permute-done | bytes 65568 | tf_op jit(solution)/shard_map/ppermute | solution.py:202
  67.8 0.9 %collective-permute-done.8.refs_1_ = f32[8,16,128]{2,1,0:T(8,128)S(1)} collective-permute-done((f32[8,16,128]{2,1,0:T(8,128)S(1)}, f32[8,16,128]{2,1,0:T(8,128)S(1)}, u32[]{:S(2)}, u32[]{:S(2)}) %collective-permute-start.8) | collective-permute-done | bytes 65568 | tf_op jit(solution)/shard_map/ppermute | solution.py:202
  68.7 2.2 %shard_map.69 = f32[4,4,4,4,384]{4,3,2,1,0:T(4,128)S(1)} custom-call(s32[2]{0:T(128)S(1)} %pad_add_fusion.pos, bf16[1024,1024]{1,0:T(8,128)(2,1)S(1)} %get-tuple-element.6.h_hi, bf16[1024,1024]{1,0:T(8,128)(2,1)S(1)} %get-tuple-element.5.h_lo, bf16[4,384,1024]{2,1,0:T(8,128)(2,1)S(1)} %pad_maximum_fusion.queries, ...), custom_call_target="tpu_custom_call" | custom-call | tf_op jit(solution)/shard_map/pallas_call | solution.py:185
  71.1 1.4 %collective-permute-done.11 = f32[2,4,4,4,384]{4,3,2,1,0:T(4,128)S(1)} collective-permute-done((f32[2,4,4,4,384]{4,3,2,1,0:T(4,128)S(1)}, f32[2,4,4,4,384]{4,3,2,1,0:T(4,128)S(1)}, u32[]{:S(2)}, u32[]{:S(2)}) %collective-permute-start.11) | collective-permute-done | bytes 196640 | tf_op jit(solution)/shard_map/ppermute | solution.py:205
  72.6 0.6 collective-permute-start.12
  73.2 4.3 %collective-permute-done.12 = f32[1,4,4,4,384]{4,3,2,1,0:T(4,128)S(1)} collective-permute-done((f32[1,4,4,4,384]{4,3,2,1,0:T(4,128)S(1)}, f32[1,4,4,4,384]{4,3,2,1,0:T(4,128)S(1)}, u32[]{:S(2)}, u32[]{:S(2)}) %collective-permute-start.12) | collective-permute-done | bytes 98336 | tf_op jit(solution)/shard_map/ppermute | solution.py:205
  77.6 3.8 %collective-permute-start.15 = (f32[4,4,384]{2,1,0:T(4,128)S(1)}, f32[4,4,384]{2,1,0:T(4,128)S(1)}, u32[]{:S(2)}, u32[]{:S(2)}) collective-permute-start(f32[4,4,384]{2,1,0:T(4,128)S(1)} %get-tuple-element.8), channel_id=1, source_target_pairs={{0,3},{1,0},{2,1},{3,2},{4,7},{5,4},{6,5},{7,6},{8,11},{9,8},{10,9... | collective-permute-start | bytes 73736 | tf_op jit(solution)/shard_map/ppermute | solution.py:202
  81.4 1.8 %collective-permute-done.13 = f32[4,4,384]{2,1,0:T(4,128)S(1)} collective-permute-done((f32[4,4,384]{2,1,0:T(4,128)S(1)}, f32[4,4,384]{2,1,0:T(4,128)S(1)}, u32[]{:S(2)}, u32[]{:S(2)}) %collective-permute-start.13) | collective-permute-done | bytes 24608 | tf_op jit(solution)/shard_map/ppermute | solution.py:202
  83.2 2.9 %collective-permute-done.14 = f32[4,4,384]{2,1,0:T(4,128)S(1)} collective-permute-done((f32[4,4,384]{2,1,0:T(4,128)S(1)}, f32[4,4,384]{2,1,0:T(4,128)S(1)}, u32[]{:S(2)}, u32[]{:S(2)}) %collective-permute-start.14) | collective-permute-done | bytes 24608 | tf_op jit(solution)/shard_map/ppermute | solution.py:202
  86.2 0.6 maximum_multiply_fusion
  (34 shorter events, 0.6 us)
Async XLA Ops:
  0.0 22.1 %copy-start.3 = (bf16[64,1024]{1,0:T(8,128)(2,1)S(1)}, bf16[64,1024]{1,0:T(8,128)(2,1)}, u32[]{:S(2)}) copy-start(bf16[64,1024]{1,0:T(8,128)(2,1)} %p_out.7) | copy-start | bytes 393220
  0.0 22.1 %copy-start.2 = (bf16[64,3584]{1,0:T(8,128)(2,1)S(1)}, bf16[64,3584]{1,0:T(8,128)(2,1)}, u32[]{:S(2)}) copy-start(bf16[64,3584]{1,0:T(8,128)(2,1)} %p_in.7) | copy-start | bytes 1376260
  0.0 20.7 %collective-permute-start = (bf16[1,384,1024]{2,1,0:T(8,128)(2,1)}, bf16[1,384,1024]{2,1,0:T(8,128)(2,1)S(1)}, u32[]{:S(2)}, u32[]{:S(2)}) collective-permute-start(bf16[1,384,1024]{2,1,0:T(8,128)(2,1)} %bitcast.39), channel_id=1, source_target_pairs={{0,8},{4,12},{8,0},{12,4},{1,9},{5,13},{9,1},{13,5},{2,10},{6,14},... | collective-permute-start | bytes 2359304 | tf_op jit(solution)/shard_map/ppermute | solution.py:205
  22.0 41.3 %collective-permute-start.1 = (bf16[2,384,1024]{2,1,0:T(8,128)(2,1)S(1)}, bf16[2,384,1024]{2,1,0:T(8,128)(2,1)}, u32[]{:S(2)}, u32[]{:S(2)}) collective-permute-start(bf16[2,384,1024]{2,1,0:T(8,128)(2,1)S(1)} %pad_maximum_fusion.1), channel_id=1, source_target_pairs={{0,4},{4,0},{8,12},{12,8},{1,5},{5,1},{9,13},{13,9},{2,6},{6,2},{1... | collective-permute-start | bytes 4718600 | tf_op jit(solution)/shard_map/ppermute | solution.py:205
  22.1 4.9 %copy-start = (bf16[1920,3584]{1,0:T(8,128)(2,1)S(1)}, bf16[1920,3584]{1,0:T(8,128)(2,1)}, u32[]{:S(2)}) copy-start(bf16[1920,3584]{1,0:T(8,128)(2,1)} %acts.7) | copy-start | bytes 41287684
  27.1 2.1 %copy-start.1 = (bf16[1920,1024]{1,0:T(8,128)(2,1)S(1)}, bf16[1920,1024]{1,0:T(8,128)(2,1)}, u32[]{:S(2)}) copy-start(bf16[1920,1024]{1,0:T(8,128)(2,1)} %outs.7) | copy-start | bytes 11796484
  32.8 15.8 %collective-permute-start.3 = (bf16[528,128]{1,0:T(8,128)(2,1)S(1)}, bf16[528,128]{1,0:T(8,128)(2,1)S(1)}, u32[]{:S(2)}, u32[]{:S(2)}) collective-permute-start(bf16[528,128]{1,0:T(8,128)(2,1)S(1)} %bitcast.36), channel_id=1, source_target_pairs={{0,1},{1,2},{2,3},{3,0},{4,5},{5,6},{6,7},{7,4},{8,9},{9,10},{10,1... | collective-permute-start | bytes 405512 | tf_op jit(solution)/shard_map/ppermute | solution.py:202
  38.3 10.3 %collective-permute-start.4 = (bf16[528,128]{1,0:T(8,128)(2,1)S(1)}, bf16[528,128]{1,0:T(8,128)(2,1)S(1)}, u32[]{:S(2)}, u32[]{:S(2)}) collective-permute-start(bf16[528,128]{1,0:T(8,128)(2,1)S(1)} %bitcast.37), channel_id=1, source_target_pairs={{0,3},{1,0},{2,1},{3,2},{4,7},{5,4},{6,5},{7,6},{8,11},{9,8},{10,9... | collective-permute-start | bytes 405512 | tf_op jit(solution)/shard_map/ppermute | solution.py:202
  44.0 8.7 %collective-permute-start.2 = (bf16[528,128]{1,0:T(8,128)(2,1)S(1)}, bf16[528,128]{1,0:T(8,128)(2,1)S(1)}, u32[]{:S(2)}, u32[]{:S(2)}) collective-permute-start(bf16[528,128]{1,0:T(8,128)(2,1)S(1)} %bitcast.38), channel_id=1, source_target_pairs={{0,2},{1,3},{2,0},{3,1},{4,6},{5,7},{6,4},{7,5},{8,10},{9,11},{10,... | collective-permute-start | bytes 405512 | tf_op jit(solution)/shard_map/ppermute | solution.py:202
  45.1 11.8 %copy-start.4 = (f32[1024,1024]{1,0:T(8,128)S(1)}, f32[1024,1024]{1,0:T(8,128)}, u32[]{:S(2)}) copy-start(f32[1024,1024]{1,0:T(8,128)} %param.10) | copy-start | bytes 12582916
  54.7 3.2 %collective-permute-start.7 = (f32[8,4,128]{2,1,0:T(4,128)S(1)}, f32[8,4,128]{2,1,0:T(4,128)S(1)}, u32[]{:S(2)}, u32[]{:S(2)}) collective-permute-start(f32[8,4,128]{2,1,0:T(4,128)S(1)} %get-tuple-element.11), channel_id=1, source_target_pairs={{0,12},{4,8},{8,4},{12,0},{1,13},{5,9},{9,5},{13,1},{2,14},{6,10},... | collective-permute-start | bytes 49160 | tf_op jit(solution)/shard_map/ppermute | solution.py:205
  55.9 2.1 %collective-permute-start.6 = (f32[8,4,128]{2,1,0:T(4,128)S(1)}, f32[8,4,128]{2,1,0:T(4,128)S(1)}, u32[]{:S(2)}, u32[]{:S(2)}) collective-permute-start(f32[8,4,128]{2,1,0:T(4,128)S(1)} %get-tuple-element.12), channel_id=1, source_target_pairs={{0,4},{4,0},{8,12},{12,8},{1,5},{5,1},{9,13},{13,9},{2,6},{6,2},{1... | collective-permute-start | bytes 49160 | tf_op jit(solution)/shard_map/ppermute | solution.py:205
  56.4 6.9 %copy-start.5 = (bf16[384,1024]{1,0:T(8,128)(2,1)S(1)}, bf16[384,1024]{1,0:T(8,128)(2,1)}, u32[]{:S(2)}) copy-start(bf16[384,1024]{1,0:T(8,128)(2,1)} %param.11) | copy-start | bytes 2359300
  56.4 3.7 %collective-permute-start.5 = (f32[8,4,128]{2,1,0:T(4,128)S(1)}, f32[8,4,128]{2,1,0:T(4,128)S(1)}, u32[]{:S(2)}, u32[]{:S(2)}) collective-permute-start(f32[8,4,128]{2,1,0:T(4,128)S(1)} %get-tuple-element.13), channel_id=1, source_target_pairs={{0,8},{4,12},{8,0},{12,4},{1,9},{5,13},{9,1},{13,5},{2,10},{6,14},... | collective-permute-start | bytes 49160 | tf_op jit(solution)/shard_map/ppermute | solution.py:205
  60.1 4.9 %collective-permute-start.10 = (f32[8,16,128]{2,1,0:T(8,128)S(1)}, f32[8,16,128]{2,1,0:T(8,128)S(1)}, u32[]{:S(2)}, u32[]{:S(2)}) collective-permute-start(f32[8,16,128]{2,1,0:T(8,128)S(1)} %pad_maximum_fusion.2.refs_0_), channel_id=1, source_target_pairs={{0,3},{1,0},{2,1},{3,2},{4,7},{5,4},{6,5},{7,6},{8,11},{9,8},{10,9... | collective-permute-start | bytes 196616 | tf_op jit(solution)/shard_map/ppermute | solution.py:202
  62.6 5.2 %collective-permute-start.9 = (f32[8,16,128]{2,1,0:T(8,128)S(1)}, f32[8,16,128]{2,1,0:T(8,128)S(1)}, u32[]{:S(2)}, u32[]{:S(2)}) collective-permute-start(f32[8,16,128]{2,1,0:T(8,128)S(1)} %pad_maximum_fusion.2.refs_0_), channel_id=1, source_target_pairs={{0,2},{1,3},{2,0},{3,1},{4,6},{5,7},{6,4},{7,5},{8,10},{9,11},{10,... | collective-permute-start | bytes 196616 | tf_op jit(solution)/shard_map/ppermute | solution.py:202
  62.6 6.1 %collective-permute-start.8 = (f32[8,16,128]{2,1,0:T(8,128)S(1)}, f32[8,16,128]{2,1,0:T(8,128)S(1)}, u32[]{:S(2)}, u32[]{:S(2)}) collective-permute-start(f32[8,16,128]{2,1,0:T(8,128)S(1)} %pad_maximum_fusion.2.refs_0_), channel_id=1, source_target_pairs={{0,1},{1,2},{2,3},{3,0},{4,5},{5,6},{6,7},{7,4},{8,9},{9,10},{10,1... | collective-permute-start | bytes 196616 | tf_op jit(solution)/shard_map/ppermute | solution.py:202
  71.0 1.5 %collective-permute-start.11 = (f32[2,4,4,4,384]{4,3,2,1,0:T(4,128)S(1)}, f32[2,4,4,4,384]{4,3,2,1,0:T(4,128)S(1)}, u32[]{:S(2)}, u32[]{:S(2)}) collective-permute-start(f32[2,4,4,4,384]{4,3,2,1,0:T(4,128)S(1)} %slice.85), channel_id=1, source_target_pairs={{0,4},{4,0},{8,12},{12,8},{1,5},{5,1},{9,13},{13,9},{2,6},{6,2},{1... | collective-permute-start | bytes 589832 | tf_op jit(solution)/shard_map/ppermute | solution.py:205
  72.6 4.9 %collective-permute-start.12 = (f32[1,4,4,4,384]{4,3,2,1,0:T(4,128)S(1)}, f32[1,4,4,4,384]{4,3,2,1,0:T(4,128)S(1)}, u32[]{:S(2)}, u32[]{:S(2)}) collective-permute-start(f32[1,4,4,4,384]{4,3,2,1,0:T(4,128)S(1)} %slice.87), channel_id=1, source_target_pairs={{0,8},{4,12},{8,0},{12,4},{1,9},{5,13},{9,1},{13,5},{2,10},{6,14},... | collective-permute-start | bytes 294920 | tf_op jit(solution)/shard_map/ppermute | solution.py:205
  77.5 5.7 %collective-permute-start.13 = (f32[4,4,384]{2,1,0:T(4,128)S(1)}, f32[4,4,384]{2,1,0:T(4,128)S(1)}, u32[]{:S(2)}, u32[]{:S(2)}) collective-permute-start(f32[4,4,384]{2,1,0:T(4,128)S(1)} %get-tuple-element.7), channel_id=1, source_target_pairs={{0,1},{1,2},{2,3},{3,0},{4,5},{5,6},{6,7},{7,4},{8,9},{9,10},{10,1... | collective-permute-start | bytes 73736 | tf_op jit(solution)/shard_map/ppermute | solution.py:202
  77.6 5.6 %collective-permute-start.15 = (f32[4,4,384]{2,1,0:T(4,128)S(1)}, f32[4,4,384]{2,1,0:T(4,128)S(1)}, u32[]{:S(2)}, u32[]{:S(2)}) collective-permute-start(f32[4,4,384]{2,1,0:T(4,128)S(1)} %get-tuple-element.8), channel_id=1, source_target_pairs={{0,3},{1,0},{2,1},{3,2},{4,7},{5,4},{6,5},{7,6},{8,11},{9,8},{10,9... | collective-permute-start | bytes 73736 | tf_op jit(solution)/shard_map/ppermute | solution.py:202
  81.4 4.7 %collective-permute-start.14 = (f32[4,4,384]{2,1,0:T(4,128)S(1)}, f32[4,4,384]{2,1,0:T(4,128)S(1)}, u32[]{:S(2)}, u32[]{:S(2)}) collective-permute-start(f32[4,4,384]{2,1,0:T(4,128)S(1)} %get-tuple-element.9), channel_id=1, source_target_pairs={{0,2},{1,3},{2,0},{3,1},{4,6},{5,7},{6,4},{7,5},{8,10},{9,11},{10,... | collective-permute-start | bytes 73736 | tf_op jit(solution)/shard_map/ppermute | solution.py:202

commit v2 on v0

v2 whole, which is shorter than its diff:
```python
import functools
import math

import jax
import jax.numpy as jnp
from jax import lax
from jax.experimental import pallas as pl
from jax.experimental.pallas import tpu as pltpu
from jax.sharding import PartitionSpec as P

R = 64
SEQ = 128
LANES = 128
TOP = 128.0
ROWS_CONTRACT = (((1,), (1,)), ((), ()))


def params(mib):
    return pltpu.CompilerParams(vmem_limit_bytes=mib << 20)


def first_example(owner, m, examples):
    return jnp.minimum(owner * m, examples - m)


def bitrev(v, bits):
    out = 0
    for b in range(bits):
        out = out + ((v >> b) & 1) * (1 << (bits - 1 - b))
    return out


def encode(x, y_ref):
    rows = x.shape[0]
    top = jnp.maximum(jnp.max(jnp.abs(x), axis=0, keepdims=True), 1e-30)
    top = top.astype(jnp.bfloat16).astype(jnp.float32)
    w = x * (TOP / top)
    s = w * w
    s = s * s
    s = s * s
    s = s * s
    y = jnp.where(x < 0, -s, s)
    y_ref[pl.ds(0, rows), :] = y.astype(jnp.bfloat16)
    y_ref[pl.ds(rows, 16), :] = jnp.broadcast_to(top, (16, LANES)).astype(jnp.bfloat16)


def project_kernel(masks, acts, outs, p_in, p_out, *refs):
    y_refs, acc = refs[:-1], refs[-1]
    right = lax.dot_general(acts[...], p_in[...], ROWS_CONTRACT, preferred_element_type=jnp.float32)
    left = lax.dot_general(outs[...], p_out[...], ROWS_CONTRACT, preferred_element_type=jnp.float32)
    acc[...] = jnp.concatenate([left, right], 1)

    def finish(mask, y_ref):
        if mask == 0:
            y_ref[...] = acc[...]
        else:
            encode(acc[...], y_ref)

    for i, (mask, y_ref) in enumerate(zip(masks, y_refs)):
        pl.when(pl.program_id(0) == i)(functools.partial(finish, mask, y_ref))


def project(acts, outs, p_in, p_out, masks, m):
    examples = acts.shape[0] // SEQ
    rows = m * SEQ
    first = masks[0]

    def start(i):
        return first_example(lax.bitwise_xor(lax.axis_index("tensor"), first - i), m, examples) * SEQ

    shapes = [
        jax.ShapeDtypeStruct((rows + 16, LANES), jnp.bfloat16) if k else jax.ShapeDtypeStruct((rows, LANES), jnp.float32)
        for k in masks
    ]
    return pl.pallas_call(
        functools.partial(project_kernel, masks),
        grid=(len(masks),),
        in_specs=[
            pl.BlockSpec((pl.Element(rows), pl.Element(acts.shape[1])), lambda i: (start(i), 0)),
            pl.BlockSpec((pl.Element(rows), pl.Element(outs.shape[1])), lambda i: (start(i), 0)),
            pl.BlockSpec(p_in.shape, lambda i: (0, 0)),
            pl.BlockSpec(p_out.shape, lambda i: (0, 0)),
        ],
        out_specs=[pl.BlockSpec(s.shape, lambda i: (0, 0)) for s in shapes],
        scratch_shapes=[pltpu.VMEM((rows, LANES), jnp.float32)],
        out_shape=shapes,
        compiler_params=params(59),
        cost_estimate=pl.CostEstimate(flops=1, bytes_accessed=1, transcendentals=0),
    )(acts, outs, p_in, p_out)


def split(v):
    hi = v.astype(jnp.bfloat16)
    return hi, (v - hi.astype(jnp.float32)).astype(jnp.bfloat16)


def grads_kernel(n, m, bits, own, *refs):
    coded, out, z = refs[: n - 1], refs[n - 1], refs[n]
    rows = m * SEQ
    x = own[...]
    for ref in coded:
        y = ref[pl.ds(0, rows), :].astype(jnp.float32)
        top = ref[pl.ds(rows, 16), :].astype(jnp.float32)[:1] * (1.0 / TOP)
        w = lax.rsqrt(lax.rsqrt(lax.rsqrt(lax.rsqrt(jnp.abs(y)))))
        x = x + jnp.where(y < 0, -w, w) * top
    half = R // n // 2
    d = lax.axis_index("dp")
    contract = (((1,), (0,)), ((), ()))
    for e in range(m):
        xe = x[e * SEQ : (e + 1) * SEQ, :]
        hi, lo = split(xe)
        hi_t, lo_t = split(xe.T)
        first = lax.dot_general(jnp.concatenate([hi_t, lo_t], 0), hi, contract, preferred_element_type=jnp.float32)
        last = lax.dot_general(hi_t, lo, contract, preferred_element_type=jnp.float32)
        z[e] = first[:LANES] + first[LANES:] + last
    for e in range(m):
        for j in range(n):
            at = bitrev(lax.bitwise_xor(d, j), bits)
            even = z[e, pl.ds(2 * half * j, half, stride=2), :]
            odd = z[e, pl.ds(2 * half * j + 1, half, stride=2), :]
            out[at, :, e, :] = jnp.concatenate([even[:, R:], odd[:, R:]], 1)


def grads_of(own, coded, n, m, bits):
    half = R // n // 2
    return pl.pallas_call(
        functools.partial(grads_kernel, n, m, bits),
        in_specs=[pl.BlockSpec(memory_space=pltpu.VMEM)] * n,
        out_specs=pl.BlockSpec(memory_space=pltpu.VMEM),
        out_shape=jax.ShapeDtypeStruct((n, half, m, LANES), jnp.float32),
        scratch_shapes=[pltpu.VMEM((m, SEQ, LANES), jnp.float32)],
        compiler_params=params(24),
    )(own, *coded)


def scores_kernel(n, m, masks, h_hi, h_lo, *refs):
    queries, grads, out, a = refs[:n], refs[n : 2 * n], refs[2 * n], refs[2 * n + 1]
    half = grads[0].shape[0]
    group = n * m
    rows = n * group
    for p in range(n):
        for r in range(half):
            a[pl.ds(p * group, group), pl.ds(r * LANES, LANES)] = grads[p][r]
    contract = (((1,), (0,)), ((), ()))
    hi, lo = split(a[...])
    top = lax.dot_general(jnp.concatenate([hi, lo], 0), h_hi[...], contract, preferred_element_type=jnp.float32)
    low = lax.dot_general(hi, h_lo[...], contract, preferred_element_type=jnp.float32)
    hi, lo = split(top[:rows] + top[rows:] + low)
    both = jnp.concatenate([hi, lo], 0)
    d, t = lax.axis_index("dp"), lax.axis_index("tensor")
    for mask, ref in zip(masks, queries):
        to = lax.bitwise_xor(lax.bitwise_xor(d, mask), t)
        s = lax.dot_general(both, ref[...], ROWS_CONTRACT, preferred_element_type=jnp.float32)
        s = s[:rows] + s[rows:]
        for p in range(n):
            for b in range(n):
                at = p * group + b * m
                out[b, to, lax.bitwise_xor(t, p)] = s[at : at + m]


def scores_of(h_hi, h_lo, queries, grads, n, m):
    half, group, _ = grads[0].shape
    masks = sorted(queries)
    blocks = [queries[k] for k in masks]
    width = blocks[0].shape[0]
    rows = n * group
    return pl.pallas_call(
        functools.partial(scores_kernel, n, m, masks),
        in_specs=[pl.BlockSpec(memory_space=pltpu.VMEM)] * (2 + 2 * n),
        out_specs=pl.BlockSpec(memory_space=pltpu.VMEM),
        out_shape=jax.ShapeDtypeStruct((n, n, n, m, width), jnp.float32),
        scratch_shapes=[pltpu.VMEM((rows, half * LANES), jnp.float32)],
        compiler_params=params(40),
    )(h_hi, h_lo, *blocks, *grads)


def local(n, activations, out_grads, proj_in, proj_out, hess_inv, queries):
    bits = n.bit_length() - 1
    examples = activations.shape[0] // SEQ
    m = -(-examples // n)
    def along(v, mask):
        return lax.ppermute(v, "tensor", [(i, i ^ mask) for i in range(n)])

    def flip(v, mask):
        return lax.ppermute(v, "dp", [(i, i ^ mask) for i in range(n)])

    def after(v, first):
        return lax.optimization_barrier((v, first))[0]

    all_q = {0: queries}
    all_q[n // 2] = flip(queries, n // 2)

    far = list(range(n - 1, 1, -1))
    y = project(activations, out_grads, proj_in, proj_out, far, m)
    near, own = project(activations, after(out_grads, y), proj_in, proj_out, [1, 0], m)
    coded = [along(v, mask) for v, mask in zip(y, far)] + [along(near, 1)]

    own, all_q[n // 2] = lax.optimization_barrier((own, all_q[n // 2]))
    grads = grads_of(own, coded, n, m, bits)
    parts = [flip(grads[p], bitrev(p, bits)) for p in range(1, n)]
    hess_inv = after(hess_inv, grads)
    h_top = lax.reduce_precision(hess_inv, 8, 7)
    h_hi = h_top.astype(jnp.bfloat16)
    h_lo = (hess_inv - h_top).astype(jnp.bfloat16)
    first, h_hi, h_lo = lax.optimization_barrier((grads[0], h_hi, h_lo))
    parts = [first] + parts
    group = jnp.concatenate(parts, 1)
    groups = [group] + [along(group, s) for s in range(1, n)]

    for b in reversed(range(bits - 1)):
        keys = list(all_q)
        all_q = dict(zip(keys, after(tuple(all_q.values()), group)))
        all_q.update({k | (1 << b): flip(v, 1 << b) for k, v in all_q.items()})

    out = scores_of(h_hi, h_lo, all_q, groups, n, m)
    for b in range(bits):
        half = out.shape[0] // 2
        out = out[:half] + flip(out[half:], 1 << b)
    out = out[0]
    total = out[0]
    for s in range(1, n):
        total = total + along(out[s], s)
    width = total.shape[-1]
    total = total.reshape(n * m, width)
    rows, i = [], 0
    while i < examples:
        owner = min(i // m, n - 1)
        begin = min(owner * m, examples - m)
        stop = begin + m
        rows.append(total[owner * m + i - begin : owner * m + stop - begin])
        i = stop
    scale = (1.0 / math.sqrt(SEQ)) * (1.0 / math.sqrt(R * R))
    return jnp.concatenate(rows, 0)[:examples] * scale


def solution(mesh):
    n = mesh.shape["tensor"]
    return jax.shard_map(
        functools.partial(local, n),
        mesh=mesh,
        in_specs=(
            P(("groups", "dp"), "tensor"),
            P(("groups", "dp"), "tensor"),
            P(None, "tensor"),
            P(None, "tensor"),
            P("dp", "tensor"),
            P("dp", "tensor"),
        ),
        out_specs=P(("groups", "dp"), "tensor"),
        check_vma=False,
    )
```

time: 317 us -> 59.2 us (0.19)
  waiting for transfers between devices: 260 us -> 20.2 us
  matrix products: 38.9 us -> 0 us
  starting transfers between devices: 0.34 us -> 18.7 us
  Pallas kernels: 0 us -> 15.2 us
  between operations: 13.2 us -> 0.15 us
    all_gather x3 -> x0, waiting for transfers between devices: 203 us -> none  [the longest x1 106 us: local(): columns = lax.all_gather(hess_inv, 'dp', axis=0, tiled=True)]
    dot_general x5 -> x0, matrix products: 38.9 us -> none  [the longest x1 15.8 us: local(): jnp.dot(lax.all_gather(queries, 'tensor', axis=1, tiled=True).astype(jnp....]
    psum x1 -> x0, waiting for transfers between devices: 36.1 us -> none  [sum_both(): return lax.psum(jnp.concatenate([left, right], 1), 'tensor')]
    ppermute x0 -> x17, waiting for transfers between devices: none -> 20.2 us  [the longest x9 13.8 us: along(): return lax.ppermute(v, 'tensor', [(i, i ^ mask) for i in range(n)])]
    reduce_scatter x1 -> x0, waiting for transfers between devices: 19.3 us -> none  [local(): lax.psum_scatter(partial_scores, 'tensor', scatter_dimension=1, tiled=True)]
    ppermute x0 -> x17, starting transfers between devices: none -> 18.7 us  [the longest x9 12.3 us: along(): return lax.ppermute(v, 'tensor', [(i, i ^ mask) for i in range(n)])]
    pallas_call x0 -> x4, Pallas kernels: none -> 15.2 us  [the longest x2 12.7 us: project(): pl.pallas_call(functools.partial(project_kernel, masks), grid=(len(masks)...]
  transfers between devices with their start and end apart: 5 -> 17, of which waited for: 5 -> 10; matrix products, arithmetic and copies ran while one was open for 10% -> 5% of each run, Pallas kernels for 0% -> 21%
where the time goes in v2:
time: 59.2 us; the launch traced here: 59.1 us
  waiting for transfers between devices  20.2 us (34%)
  starting transfers between devices  18.7 us (32%)
  Pallas kernels  15.2 us (26%)
  other arithmetic  3.84 us (6%)
  local copies, waits for them, and re-layouts  1.03 us (2%)
    ppermute x9, waiting for transfers between devices, along(): return lax.ppermute(v, 'tensor', [(i, i ^ mask) for i in range(n)])  13.8 us
    pallas_call x2, Pallas kernels, project(): pl.pallas_call(functools.partial(project_kernel, masks), grid=(len(masks)...  12.7 us
    ppermute x9, starting transfers between devices, along(): return lax.ppermute(v, 'tensor', [(i, i ^ mask) for i in range(n)])  12.3 us
    ppermute x8, waiting for transfers between devices, flip(): return lax.ppermute(v, 'dp', [(i, i ^ mask) for i in range(n)])  6.4 us
    ppermute x8, starting transfers between devices, flip(): return lax.ppermute(v, 'dp', [(i, i ^ mask) for i in range(n)])  6.4 us
    convert_element_type x1, other arithmetic, local(): h_lo = (hess_inv - h_top).astype(jnp.bfloat16)  3.1 us
    pallas_call x1, Pallas kernels, scores_of(): pl.pallas_call(functools.partial(scores_kernel, n, m, masks), in_specs=[p...  1.72 us
  transfers between devices with their start and end apart: 17, of which 10 were waited for; matrix products, arithmetic and copies ran while one was open for 5% of the time, Pallas kernels for 21%

profile of v2, /device:TPU:0, one launch (start us, length us, event | category | flops | bytes accessed | tf_op | source)
XLA Modules:
  0.0 59.1 jit_solution(420973308375144246)
XLA Ops:
  0.0 2.9 %collective-permute-start = (bf16[384,1024]{1,0:T(8,128)(2,1)}, bf16[384,1024]{1,0:T(8,128)(2,1)S(1)}, u32[]{:S(2)}, u32[]{:S(2)}) collective-permute-start(bf16[384,1024]{1,0:T(8,128)(2,1)} %refs_0_), channel_id=1, source_target_pairs={{0,8},{4,12},{8,0},{12,4},{1,9},{5,13},{9,1},{13,5},{2,10},{6,14},... | collective-permute-start | bytes 2359304 | tf_op jit(solution)/shard_map/ppermute | solution.py:185
  2.9 6.4 %shard_map.64 = (bf16[528,128]{1,0:T(8,128)(2,1)}, bf16[528,128]{1,0:T(8,128)(2,1)}) custom-call(bf16[1920,3584]{1,0:T(8,128)(2,1)} %acts.3, bf16[1920,1024]{1,0:T(8,128)(2,1)} %outs.2, bf16[64,3584]{1,0:T(8,128)(2,1)} %p_in.3, bf16[64,1024]{1,0:T(8,128)(2,1)} %p_out.3), custom_call_target="tpu_custom_call" | custom-call | flops 1 | bytes 1 | tf_op jit(solution)/shard_map/pallas_call | solution.py:75
  9.3 3.6 %collective-permute-start.1 = (bf16[528,128]{1,0:T(8,128)(2,1)}, bf16[528,128]{1,0:T(8,128)(2,1)S(1)}, u32[]{:S(2)}, u32[]{:S(2)}) collective-permute-start(bf16[528,128]{1,0:T(8,128)(2,1)} %get-tuple-element.18), channel_id=1, source_target_pairs={{0,3},{1,2},{2,1},{3,0},{4,7},{5,6},{6,5},{7,4},{8,11},{9,10},{10,... | collective-permute-start | bytes 405512 | tf_op jit(solution)/shard_map/ppermute | solution.py:182
  12.9 6.3 %shard_map.65 = (bf16[528,128]{1,0:T(8,128)(2,1)}, f32[512,128]{1,0:T(8,128)}) custom-call(bf16[1920,3584]{1,0:T(8,128)(2,1)} %acts.3, bf16[1920,1024]{1,0:T(8,128)(2,1)} %outs.2, bf16[64,3584]{1,0:T(8,128)(2,1)} %p_in.3, bf16[64,1024]{1,0:T(8,128)(2,1)} %p_out.3), custom_call_target="tpu_custom_call" | custom-call | flops 1 | bytes 1 | tf_op jit(solution)/shard_map/pallas_call | solution.py:75
  19.2 0.8 %collective-permute-start.3 = (bf16[528,128]{1,0:T(8,128)(2,1)}, bf16[528,128]{1,0:T(8,128)(2,1)S(1)}, u32[]{:S(2)}, u32[]{:S(2)}) collective-permute-start(bf16[528,128]{1,0:T(8,128)(2,1)} %get-tuple-element.23), channel_id=1, source_target_pairs={{0,1},{1,0},{2,3},{3,2},{4,5},{5,4},{6,7},{7,6},{8,9},{9,8},{10,11... | collective-permute-start | bytes 405512 | tf_op jit(solution)/shard_map/ppermute | solution.py:182
  20.0 0.7 %collective-permute-done.refs_2_ = bf16[384,1024]{1,0:T(8,128)(2,1)S(1)} collective-permute-done((bf16[384,1024]{1,0:T(8,128)(2,1)}, bf16[384,1024]{1,0:T(8,128)(2,1)S(1)}, u32[]{:S(2)}, u32[]{:S(2)}) %collective-permute-start) | collective-permute-done | bytes 786464 | tf_op jit(solution)/shard_map/ppermute | solution.py:185
  20.7 3.7 %collective-permute-done.2.refs_1_ = bf16[528,128]{1,0:T(8,128)(2,1)S(1)} collective-permute-done((bf16[528,128]{1,0:T(8,128)(2,1)}, bf16[528,128]{1,0:T(8,128)(2,1)S(1)}, u32[]{:S(2)}, u32[]{:S(2)}) %collective-permute-start.2) | collective-permute-done | bytes 135200 | tf_op jit(solution)/shard_map/ppermute | solution.py:182
  24.4 2.3 %collective-permute-done.3.refs_2_ = bf16[528,128]{1,0:T(8,128)(2,1)S(1)} collective-permute-done((bf16[528,128]{1,0:T(8,128)(2,1)}, bf16[528,128]{1,0:T(8,128)(2,1)S(1)}, u32[]{:S(2)}, u32[]{:S(2)}) %collective-permute-start.3) | collective-permute-done | bytes 135200 | tf_op jit(solution)/shard_map/ppermute | solution.py:182
  26.6 0.9 %copy-done.1 = f32[512,128]{1,0:T(8,128)S(1)} copy-done((f32[512,128]{1,0:T(8,128)S(1)}, f32[512,128]{1,0:T(8,128)}, u32[]{:S(2)}) %copy-start.1) | copy-done | bytes 262168
  27.6 0.8 %shard_map.66 = f32[4,8,4,128]{3,2,1,0:T(4,128)S(1)} custom-call(f32[512,128]{1,0:T(8,128)S(1)} %copy-done.1, bf16[528,128]{1,0:T(8,128)(2,1)S(1)} %collective-permute-done.1.refs_0_, bf16[528,128]{1,0:T(8,128)(2,1)S(1)} %collective-permute-done.2.refs_1_, bf16[528,128]{1,0:T(8,128)(2,1)S(1)} %collective-permute-done.3.refs_2_), custom_call_target="tpu_custom_call" | custom-call | tf_op jit(solution)/shard_map/pallas_call | solution.py:126
  28.4 0.6 %collective-permute-start.4 = (f32[8,4,128]{2,1,0:T(4,128)S(1)}, f32[8,4,128]{2,1,0:T(4,128)S(1)}, u32[]{:S(2)}, u32[]{:S(2)}) collective-permute-start(f32[8,4,128]{2,1,0:T(4,128)S(1)} %get-tuple-element.36), channel_id=1, source_target_pairs={{0,8},{4,12},{8,0},{12,4},{1,9},{5,13},{9,1},{13,5},{2,10},{6,14},... | collective-permute-start | bytes 49160 | tf_op jit(solution)/shard_map/ppermute | solution.py:185
  29.0 0.2 collective-permute-start.6
  29.2 1.4 %collective-permute-start.5 = (f32[8,4,128]{2,1,0:T(4,128)S(1)}, f32[8,4,128]{2,1,0:T(4,128)S(1)}, u32[]{:S(2)}, u32[]{:S(2)}) collective-permute-start(f32[8,4,128]{2,1,0:T(4,128)S(1)} %get-tuple-element.38), channel_id=1, source_target_pairs={{0,4},{4,0},{8,12},{12,8},{1,5},{5,1},{9,13},{13,9},{2,6},{6,2},{1... | collective-permute-start | bytes 49160 | tf_op jit(solution)/shard_map/ppermute | solution.py:185
  30.6 3.1 %fusion = (bf16[1024,1024]{1,0:T(8,128)(2,1)S(1)}, bf16[1024,1024]{1,0:T(8,128)(2,1)S(1)}) fusion(f32[1024,1024]{1,0:T(8,128)} %param.10), kind=kLoop, calls=%fused_computation.2 | loop fusion | flops 4194304 | bytes 8388608 | tf_op jit(solution)/shard_map/convert_element_type | solution.py:204
  33.7 0.1 collective-permute-start.7
  33.9 0.4 collective-permute-start.8
  34.3 2.2 %collective-permute-start.11 = (f32[8,16,128]{2,1,0:T(8,128)S(1)}, f32[8,16,128]{2,1,0:T(8,128)S(1)}, u32[]{:S(2)}, u32[]{:S(2)}) collective-permute-start(f32[8,16,128]{2,1,0:T(8,128)S(1)} %pad_maximum_fusion.refs_4_), channel_id=1, source_target_pairs={{0,3},{1,2},{2,1},{3,0},{4,7},{5,6},{6,5},{7,4},{8,11},{9,10},{10,... | collective-permute-start | bytes 196616 | tf_op jit(solution)/shard_map/ppermute | solution.py:182
  36.5 2.2 %collective-permute-start.9 = (f32[8,16,128]{2,1,0:T(8,128)S(1)}, f32[8,16,128]{2,1,0:T(8,128)S(1)}, u32[]{:S(2)}, u32[]{:S(2)}) collective-permute-start(f32[8,16,128]{2,1,0:T(8,128)S(1)} %pad_maximum_fusion.refs_4_), channel_id=1, source_target_pairs={{0,1},{1,0},{2,3},{3,2},{4,5},{5,4},{6,7},{7,6},{8,9},{9,8},{10,11... | collective-permute-start | bytes 196616 | tf_op jit(solution)/shard_map/ppermute | solution.py:182
  38.7 2.3 %collective-permute-done.11.refs_7_ = f32[8,16,128]{2,1,0:T(8,128)S(1)} collective-permute-done((f32[8,16,128]{2,1,0:T(8,128)S(1)}, f32[8,16,128]{2,1,0:T(8,128)S(1)}, u32[]{:S(2)}, u32[]{:S(2)}) %collective-permute-start.11) | collective-permute-done | bytes 65568 | tf_op jit(solution)/shard_map/ppermute | solution.py:182
  41.0 2.0 %collective-permute-done.10.refs_6_ = f32[8,16,128]{2,1,0:T(8,128)S(1)} collective-permute-done((f32[8,16,128]{2,1,0:T(8,128)S(1)}, f32[8,16,128]{2,1,0:T(8,128)S(1)}, u32[]{:S(2)}, u32[]{:S(2)}) %collective-permute-start.10) | collective-permute-done | bytes 65568 | tf_op jit(solution)/shard_map/ppermute | solution.py:182
  43.0 1.7 %shard_map.67 = f32[4,4,4,4,384]{4,3,2,1,0:T(4,128)S(1)} custom-call(bf16[1024,1024]{1,0:T(8,128)(2,1)S(1)} %get-tuple-element.25.h_hi, bf16[1024,1024]{1,0:T(8,128)(2,1)S(1)} %get-tuple-element.26.h_lo, bf16[384,1024]{1,0:T(8,128)(2,1)S(1)} %copy-done, bf16[384,1024]{1,0:T(8,128)(2,1)S(1)} %collective-permute-done.7.refs_1_, ...), custom_call_target="tpu_custom_call" | custom-call | tf_op jit(solution)/shard_map/pallas_call | solution.py:167
  44.8 0.1 collective-permute-start.12
  44.8 1.4 %collective-permute-done.12 = f32[2,4,4,4,384]{4,3,2,1,0:T(4,128)S(1)} collective-permute-done((f32[2,4,4,4,384]{4,3,2,1,0:T(4,128)S(1)}, f32[2,4,4,4,384]{4,3,2,1,0:T(4,128)S(1)}, u32[]{:S(2)}, u32[]{:S(2)}) %collective-permute-start.12) | collective-permute-done | bytes 196640 | tf_op jit(solution)/shard_map/ppermute | solution.py:185
  46.4 0.6 %collective-permute-start.13 = (f32[1,4,4,4,384]{4,3,2,1,0:T(4,128)S(1)}, f32[1,4,4,4,384]{4,3,2,1,0:T(4,128)S(1)}, u32[]{:S(2)}, u32[]{:S(2)}) collective-permute-start(f32[1,4,4,4,384]{4,3,2,1,0:T(4,128)S(1)} %slice.87), channel_id=1, source_target_pairs={{0,8},{4,12},{8,0},{12,4},{1,9},{5,13},{9,1},{13,5},{2,10},{6,14},... | collective-permute-start | bytes 294920 | tf_op jit(solution)/shard_map/ppermute | solution.py:185
  47.0 4.3 %collective-permute-done.13 = f32[1,4,4,4,384]{4,3,2,1,0:T(4,128)S(1)} collective-permute-done((f32[1,4,4,4,384]{4,3,2,1,0:T(4,128)S(1)}, f32[1,4,4,4,384]{4,3,2,1,0:T(4,128)S(1)}, u32[]{:S(2)}, u32[]{:S(2)}) %collective-permute-start.13) | collective-permute-done | bytes 98336 | tf_op jit(solution)/shard_map/ppermute | solution.py:185
  51.3 0.5 collective-permute-start.14
  51.8 1.9 %collective-permute-start.16 = (f32[4,4,384]{2,1,0:T(4,128)S(1)}, f32[4,4,384]{2,1,0:T(4,128)S(1)}, u32[]{:S(2)}, u32[]{:S(2)}) collective-permute-start(f32[4,4,384]{2,1,0:T(4,128)S(1)} %get-tuple-element.34), channel_id=1, source_target_pairs={{0,3},{1,2},{2,1},{3,0},{4,7},{5,6},{6,5},{7,4},{8,11},{9,10},{10,... | collective-permute-start | bytes 73736 | tf_op jit(solution)/shard_map/ppermute | solution.py:182
  53.7 1.2 %collective-permute-start.15 = (f32[4,4,384]{2,1,0:T(4,128)S(1)}, f32[4,4,384]{2,1,0:T(4,128)S(1)}, u32[]{:S(2)}, u32[]{:S(2)}) collective-permute-start(f32[4,4,384]{2,1,0:T(4,128)S(1)} %get-tuple-element.35), channel_id=1, source_target_pairs={{0,2},{1,3},{2,0},{3,1},{4,6},{5,7},{6,4},{7,5},{8,10},{9,11},{10,... | collective-permute-start | bytes 73736 | tf_op jit(solution)/shard_map/ppermute | solution.py:182
  54.9 0.3 collective-permute-done.14
  55.2 2.2 %collective-permute-done.16 = f32[4,4,384]{2,1,0:T(4,128)S(1)} collective-permute-done((f32[4,4,384]{2,1,0:T(4,128)S(1)}, f32[4,4,384]{2,1,0:T(4,128)S(1)}, u32[]{:S(2)}, u32[]{:S(2)}) %collective-permute-start.16) | collective-permute-done | bytes 24608 | tf_op jit(solution)/shard_map/ppermute | solution.py:182
  57.4 1.0 %collective-permute-done.15 = f32[4,4,384]{2,1,0:T(4,128)S(1)} collective-permute-done((f32[4,4,384]{2,1,0:T(4,128)S(1)}, f32[4,4,384]{2,1,0:T(4,128)S(1)}, u32[]{:S(2)}, u32[]{:S(2)}) %collective-permute-start.15) | collective-permute-done | bytes 24608 | tf_op jit(solution)/shard_map/ppermute | solution.py:182
  58.4 0.6 %maximum_multiply_fusion = f32[15,384]{1,0:T(8,128)} fusion(f32[3,384]{1,0:T(4,128)S(1)} %slice.95, f32[4,384]{1,0:T(4,128)S(1)} %get-tuple-element.41, f32[4,384]{1,0:T(4,128)S(1)} %get-tuple-element.42, f32[4,384]{1,0:T(4,128)S(1)} %get-tuple-element.40), kind=kLoop, calls=%fused_computation.13 | loop fusion | flops 23040 | bytes 46080 | tf_op jit(solution)/shard_map/mul | solution.py:233
  (23 shorter events, 0.2 us)
Async XLA Ops:
  0.0 20.7 %collective-permute-start = (bf16[384,1024]{1,0:T(8,128)(2,1)}, bf16[384,1024]{1,0:T(8,128)(2,1)S(1)}, u32[]{:S(2)}, u32[]{:S(2)}) collective-permute-start(bf16[384,1024]{1,0:T(8,128)(2,1)} %refs_0_), channel_id=1, source_target_pairs={{0,8},{4,12},{8,0},{12,4},{1,9},{5,13},{9,1},{13,5},{2,10},{6,14},... | collective-permute-start | bytes 2359304 | tf_op jit(solution)/shard_map/ppermute | solution.py:185
  9.3 11.4 %collective-permute-start.1 = (bf16[528,128]{1,0:T(8,128)(2,1)}, bf16[528,128]{1,0:T(8,128)(2,1)S(1)}, u32[]{:S(2)}, u32[]{:S(2)}) collective-permute-start(bf16[528,128]{1,0:T(8,128)(2,1)} %get-tuple-element.18), channel_id=1, source_target_pairs={{0,3},{1,2},{2,1},{3,0},{4,7},{5,6},{6,5},{7,4},{8,11},{9,10},{10,... | collective-permute-start | bytes 405512 | tf_op jit(solution)/shard_map/ppermute | solution.py:182
  12.9 11.4 %collective-permute-start.2 = (bf16[528,128]{1,0:T(8,128)(2,1)}, bf16[528,128]{1,0:T(8,128)(2,1)S(1)}, u32[]{:S(2)}, u32[]{:S(2)}) collective-permute-start(bf16[528,128]{1,0:T(8,128)(2,1)} %get-tuple-element.19), channel_id=1, source_target_pairs={{0,2},{1,3},{2,0},{3,1},{4,6},{5,7},{6,4},{7,5},{8,10},{9,11},{10,... | collective-permute-start | bytes 405512 | tf_op jit(solution)/shard_map/ppermute | solution.py:182
  19.2 7.4 %collective-permute-start.3 = (bf16[528,128]{1,0:T(8,128)(2,1)}, bf16[528,128]{1,0:T(8,128)(2,1)S(1)}, u32[]{:S(2)}, u32[]{:S(2)}) collective-permute-start(bf16[528,128]{1,0:T(8,128)(2,1)} %get-tuple-element.23), channel_id=1, source_target_pairs={{0,1},{1,0},{2,3},{3,2},{4,5},{5,4},{6,7},{7,6},{8,9},{9,8},{10,11... | collective-permute-start | bytes 405512 | tf_op jit(solution)/shard_map/ppermute | solution.py:182
  26.6 1.0 %copy-start.1 = (f32[512,128]{1,0:T(8,128)S(1)}, f32[512,128]{1,0:T(8,128)}, u32[]{:S(2)}) copy-start(f32[512,128]{1,0:T(8,128)} %get-tuple-element.22.own) | copy-start | bytes 786436
  28.4 5.3 %collective-permute-start.4 = (f32[8,4,128]{2,1,0:T(4,128)S(1)}, f32[8,4,128]{2,1,0:T(4,128)S(1)}, u32[]{:S(2)}, u32[]{:S(2)}) collective-permute-start(f32[8,4,128]{2,1,0:T(4,128)S(1)} %get-tuple-element.36), channel_id=1, source_target_pairs={{0,8},{4,12},{8,0},{12,4},{1,9},{5,13},{9,1},{13,5},{2,10},{6,14},... | collective-permute-start | bytes 49160 | tf_op jit(solution)/shard_map/ppermute | solution.py:185
  29.0 4.7 %collective-permute-start.6 = (f32[8,4,128]{2,1,0:T(4,128)S(1)}, f32[8,4,128]{2,1,0:T(4,128)S(1)}, u32[]{:S(2)}, u32[]{:S(2)}) collective-permute-start(f32[8,4,128]{2,1,0:T(4,128)S(1)} %get-tuple-element.37), channel_id=1, source_target_pairs={{0,12},{4,8},{8,4},{12,0},{1,13},{5,9},{9,5},{13,1},{2,14},{6,10},... | collective-permute-start | bytes 49160 | tf_op jit(solution)/shard_map/ppermute | solution.py:185
  29.2 4.5 %copy-start = (bf16[384,1024]{1,0:T(8,128)(2,1)S(1)}, bf16[384,1024]{1,0:T(8,128)(2,1)}, u32[]{:S(2)}) copy-start(bf16[384,1024]{1,0:T(8,128)(2,1)} %refs_0_) | copy-start | bytes 2359300
  29.2 4.5 %collective-permute-start.5 = (f32[8,4,128]{2,1,0:T(4,128)S(1)}, f32[8,4,128]{2,1,0:T(4,128)S(1)}, u32[]{:S(2)}, u32[]{:S(2)}) collective-permute-start(f32[8,4,128]{2,1,0:T(4,128)S(1)} %get-tuple-element.38), channel_id=1, source_target_pairs={{0,4},{4,0},{8,12},{12,8},{1,5},{5,1},{9,13},{13,9},{2,6},{6,2},{1... | collective-permute-start | bytes 49160 | tf_op jit(solution)/shard_map/ppermute | solution.py:185
  33.7 9.3 %collective-permute-start.7 = (bf16[384,1024]{1,0:T(8,128)(2,1)S(1)}, bf16[384,1024]{1,0:T(8,128)(2,1)S(1)}, u32[]{:S(2)}, u32[]{:S(2)}) collective-permute-start(bf16[384,1024]{1,0:T(8,128)(2,1)S(1)} %copy-done), channel_id=1, source_target_pairs={{0,4},{4,0},{8,12},{12,8},{1,5},{5,1},{9,13},{13,9},{2,6},{6,2},{1... | collective-permute-start | bytes 2359304 | tf_op jit(solution)/shard_map/ppermute | solution.py:185
  33.9 9.1 %collective-permute-start.8 = (bf16[384,1024]{1,0:T(8,128)(2,1)S(1)}, bf16[384,1024]{1,0:T(8,128)(2,1)S(1)}, u32[]{:S(2)}, u32[]{:S(2)}) collective-permute-start(bf16[384,1024]{1,0:T(8,128)(2,1)S(1)} %collective-permute-done.refs_2_), channel_id=1, source_target_pairs={{0,4},{4,0},{8,12},{12,8},{1,5},{5,1},{9,13},{13,9},{2,6},{6,2},{1... | collective-permute-start | bytes 2359304 | tf_op jit(solution)/shard_map/ppermute | solution.py:185
  34.3 6.7 %collective-permute-start.11 = (f32[8,16,128]{2,1,0:T(8,128)S(1)}, f32[8,16,128]{2,1,0:T(8,128)S(1)}, u32[]{:S(2)}, u32[]{:S(2)}) collective-permute-start(f32[8,16,128]{2,1,0:T(8,128)S(1)} %pad_maximum_fusion.refs_4_), channel_id=1, source_target_pairs={{0,3},{1,2},{2,1},{3,0},{4,7},{5,6},{6,5},{7,4},{8,11},{9,10},{10,... | collective-permute-start | bytes 196616 | tf_op jit(solution)/shard_map/ppermute | solution.py:182
  36.5 6.5 %collective-permute-start.10 = (f32[8,16,128]{2,1,0:T(8,128)S(1)}, f32[8,16,128]{2,1,0:T(8,128)S(1)}, u32[]{:S(2)}, u32[]{:S(2)}) collective-permute-start(f32[8,16,128]{2,1,0:T(8,128)S(1)} %pad_maximum_fusion.refs_4_), channel_id=1, source_target_pairs={{0,2},{1,3},{2,0},{3,1},{4,6},{5,7},{6,4},{7,5},{8,10},{9,11},{10,... | collective-permute-start | bytes 196616 | tf_op jit(solution)/shard_map/ppermute | solution.py:182
  36.5 6.5 %collective-permute-start.9 = (f32[8,16,128]{2,1,0:T(8,128)S(1)}, f32[8,16,128]{2,1,0:T(8,128)S(1)}, u32[]{:S(2)}, u32[]{:S(2)}) collective-permute-start(f32[8,16,128]{2,1,0:T(8,128)S(1)} %pad_maximum_fusion.refs_4_), channel_id=1, source_target_pairs={{0,1},{1,0},{2,3},{3,2},{4,5},{5,4},{6,7},{7,6},{8,9},{9,8},{10,11... | collective-permute-start | bytes 196616 | tf_op jit(solution)/shard_map/ppermute | solution.py:182
  44.8 1.5 %collective-permute-start.12 = (f32[2,4,4,4,384]{4,3,2,1,0:T(4,128)S(1)}, f32[2,4,4,4,384]{4,3,2,1,0:T(4,128)S(1)}, u32[]{:S(2)}, u32[]{:S(2)}) collective-permute-start(f32[2,4,4,4,384]{4,3,2,1,0:T(4,128)S(1)} %slice.85), channel_id=1, source_target_pairs={{0,4},{4,0},{8,12},{12,8},{1,5},{5,1},{9,13},{13,9},{2,6},{6,2},{1... | collective-permute-start | bytes 589832 | tf_op jit(solution)/shard_map/ppermute | solution.py:185
  46.4 4.9 %collective-permute-start.13 = (f32[1,4,4,4,384]{4,3,2,1,0:T(4,128)S(1)}, f32[1,4,4,4,384]{4,3,2,1,0:T(4,128)S(1)}, u32[]{:S(2)}, u32[]{:S(2)}) collective-permute-start(f32[1,4,4,4,384]{4,3,2,1,0:T(4,128)S(1)} %slice.87), channel_id=1, source_target_pairs={{0,8},{4,12},{8,0},{12,4},{1,9},{5,13},{9,1},{13,5},{2,10},{6,14},... | collective-permute-start | bytes 294920 | tf_op jit(solution)/shard_map/ppermute | solution.py:185
  51.3 3.9 %collective-permute-start.14 = (f32[4,4,384]{2,1,0:T(4,128)S(1)}, f32[4,4,384]{2,1,0:T(4,128)S(1)}, u32[]{:S(2)}, u32[]{:S(2)}) collective-permute-start(f32[4,4,384]{2,1,0:T(4,128)S(1)} %get-tuple-element.33), channel_id=1, source_target_pairs={{0,1},{1,0},{2,3},{3,2},{4,5},{5,4},{6,7},{7,6},{8,9},{9,8},{10,11... | collective-permute-start | bytes 73736 | tf_op jit(solution)/shard_map/ppermute | solution.py:182
  51.8 5.6 %collective-permute-start.16 = (f32[4,4,384]{2,1,0:T(4,128)S(1)}, f32[4,4,384]{2,1,0:T(4,128)S(1)}, u32[]{:S(2)}, u32[]{:S(2)}) collective-permute-start(f32[4,4,384]{2,1,0:T(4,128)S(1)} %get-tuple-element.34), channel_id=1, source_target_pairs={{0,3},{1,2},{2,1},{3,0},{4,7},{5,6},{6,5},{7,4},{8,11},{9,10},{10,... | collective-permute-start | bytes 73736 | tf_op jit(solution)/shard_map/ppermute | solution.py:182
  53.7 4.7 %collective-permute-start.15 = (f32[4,4,384]{2,1,0:T(4,128)S(1)}, f32[4,4,384]{2,1,0:T(4,128)S(1)}, u32[]{:S(2)}, u32[]{:S(2)}) collective-permute-start(f32[4,4,384]{2,1,0:T(4,128)S(1)} %get-tuple-element.35), channel_id=1, source_target_pairs={{0,2},{1,3},{2,0},{3,1},{4,6},{5,7},{6,4},{7,5},{8,10},{9,11},{10,... | collective-permute-start | bytes 73736 | tf_op jit(solution)/shard_map/ppermute | solution.py:182

commit v3 on v2

--- a/solution.py
+++ b/solution.py
@@ -30,17 +30,29 @@
     return out
 
 
-def encode(x, y_ref):
-    rows = x.shape[0]
-    top = jnp.maximum(jnp.max(jnp.abs(x), axis=0, keepdims=True), 1e-30)
-    top = top.astype(jnp.bfloat16).astype(jnp.float32)
+def power(x, top):
     w = x * (TOP / top)
     s = w * w
     s = s * s
     s = s * s
     s = s * s
-    y = jnp.where(x < 0, -s, s)
-    y_ref[pl.ds(0, rows), :] = y.astype(jnp.bfloat16)
+    return jnp.where(x < 0, -s, s)
+
+
+def root(y):
+    w = lax.rsqrt(lax.rsqrt(lax.rsqrt(lax.rsqrt(jnp.abs(y)))))
+    return jnp.where(y < 0, -w, w)
+
+
+def column_top(x):
+    top = jnp.maximum(jnp.max(jnp.abs(x), axis=0, keepdims=True), 1e-30)
+    return top.astype(jnp.bfloat16).astype(jnp.float32)
+
+
+def encode(x, y_ref):
+    rows = x.shape[0]
+    top = column_top(x)
+    y_ref[pl.ds(0, rows), :] = power(x, top).astype(jnp.bfloat16)
     y_ref[pl.ds(rows, 16), :] = jnp.broadcast_to(top, (16, LANES)).astype(jnp.bfloat16)
 
 
@@ -60,7 +72,7 @@
         pl.when(pl.program_id(0) == i)(functools.partial(finish, mask, y_ref))
 
 
-def project(acts, outs, p_in, p_out, masks, m):
+def project(acts, outs, p_in, p_out, masks, m, mib):
     examples = acts.shape[0] // SEQ
     rows = m * SEQ
     first = masks[0]
@@ -84,7 +96,7 @@
         out_specs=[pl.BlockSpec(s.shape, lambda i: (0, 0)) for s in shapes],
         scratch_shapes=[pltpu.VMEM((rows, LANES), jnp.float32)],
         out_shape=shapes,
-        compiler_params=params(59),
+        compiler_params=params(mib),
         cost_estimate=pl.CostEstimate(flops=1, bytes_accessed=1, transcendentals=0),
     )(acts, outs, p_in, p_out)
 
@@ -95,14 +107,12 @@
 
 
 def grads_kernel(n, m, bits, own, *refs):
-    coded, out, z = refs[: n - 1], refs[n - 1], refs[n]
+    coded, out, z, block = refs[: n - 1], *refs[-3:]
     rows = m * SEQ
     x = own[...]
     for ref in coded:
-        y = ref[pl.ds(0, rows), :].astype(jnp.float32)
-        top = ref[pl.ds(rows, 16), :].astype(jnp.float32)[:1] * (1.0 / TOP)
-        w = lax.rsqrt(lax.rsqrt(lax.rsqrt(lax.rsqrt(jnp.abs(y)))))
-        x = x + jnp.where(y < 0, -w, w) * top
+        y = ref[...].astype(jnp.float32)
+        x = x + root(y[:rows]) * y[rows : rows + 1]
     half = R // n // 2
     d = lax.axis_index("dp")
     contract = (((1,), (0,)), ((), ()))
@@ -113,34 +123,61 @@
         first = lax.dot_general(jnp.concatenate([hi_t, lo_t], 0), hi, contract, preferred_element_type=jnp.float32)
         last = lax.dot_general(hi_t, lo, contract, preferred_element_type=jnp.float32)
         z[e] = first[:LANES] + first[LANES:] + last
-    for e in range(m):
-        for j in range(n):
-            at = bitrev(lax.bitwise_xor(d, j), bits)
+    for j in range(n):
+        for e in range(m):
             even = z[e, pl.ds(2 * half * j, half, stride=2), :]
             odd = z[e, pl.ds(2 * half * j + 1, half, stride=2), :]
-            out[at, :, e, :] = jnp.concatenate([even[:, R:], odd[:, R:]], 1)
+            g = jnp.concatenate([even[:, R:], odd[:, R:]], 1)
+            top = column_top(g)
+            block[pl.ds(e, half, stride=m), :] = power(g, top)
+            block[pl.ds(half * m + e, 1), :] = top
+        out[bitrev(lax.bitwise_xor(d, j), bits)] = block[...].astype(jnp.bfloat16)
 
 
 def grads_of(own, coded, n, m, bits):
-    half = R // n // 2
+    rows = (R // n // 2 + 1) * m
     return pl.pallas_call(
         functools.partial(grads_kernel, n, m, bits),
         in_specs=[pl.BlockSpec(memory_space=pltpu.VMEM)] * n,
         out_specs=pl.BlockSpec(memory_space=pltpu.VMEM),
-        out_shape=jax.ShapeDtypeStruct((n, half, m, LANES), jnp.float32),
-        scratch_shapes=[pltpu.VMEM((m, SEQ, LANES), jnp.float32)],
+        out_shape=jax.ShapeDtypeStruct((n, rows, LANES), jnp.bfloat16),
+        scratch_shapes=[pltpu.VMEM((m, SEQ, LANES), jnp.float32), pltpu.VMEM((rows, LANES), jnp.float32)],
         compiler_params=params(24),
+        cost_estimate=pl.CostEstimate(flops=1, bytes_accessed=1, transcendentals=0),
     )(own, *coded)
+
+
+def halves_kernel(h, *refs):
+    hi, lo = split(h[...])
+    refs[-2][...] = hi
+    refs[-1][...] = lo
+
+
+def halves(h, wait_for):
+    rows = h.shape[0] // 4 if h.shape[0] % 64 == 0 else h.shape[0]
+    spec = pl.BlockSpec((rows, h.shape[1]), lambda i: (i, 0))
+    shape = jax.ShapeDtypeStruct(h.shape, jnp.bfloat16)
+    return pl.pallas_call(
+        halves_kernel,
+        grid=(h.shape[0] // rows,),
+        in_specs=[spec] + [pl.BlockSpec(memory_space=pl.ANY)] * len(wait_for),
+        out_specs=[spec, spec],
+        out_shape=[shape, shape],
+        compiler_params=params(24),
+        cost_estimate=pl.CostEstimate(flops=1, bytes_accessed=1, transcendentals=0),
+    )(h, *wait_for)
 
 
 def scores_kernel(n, m, masks, h_hi, h_lo, *refs):
     queries, grads, out, a = refs[:n], refs[n : 2 * n], refs[2 * n], refs[2 * n + 1]
-    half = grads[0].shape[0]
-    group = n * m
-    rows = n * group
-    for p in range(n):
+    half = R // n // 2
+    rows = n * n * m
+    for s in range(n * n):
+        y = grads[s // n][s % n].astype(jnp.float32)
+        top = y[half * m :]
+        w = root(y[: half * m]) * (1.0 / TOP)
         for r in range(half):
-            a[pl.ds(p * group, group), pl.ds(r * LANES, LANES)] = grads[p][r]
+            a[pl.ds(s * m, m), pl.ds(r * LANES, LANES)] = w[r * m : (r + 1) * m] * top
     contract = (((1,), (0,)), ((), ()))
     hi, lo = split(a[...])
     top = lax.dot_general(jnp.concatenate([hi, lo], 0), h_hi[...], contract, preferred_element_type=jnp.float32)
@@ -154,22 +191,20 @@
         s = s[:rows] + s[rows:]
         for p in range(n):
             for b in range(n):
-                at = p * group + b * m
+                at = (p * n + b) * m
                 out[b, to, lax.bitwise_xor(t, p)] = s[at : at + m]
 
 
 def scores_of(h_hi, h_lo, queries, grads, n, m):
-    half, group, _ = grads[0].shape
     masks = sorted(queries)
     blocks = [queries[k] for k in masks]
     width = blocks[0].shape[0]
-    rows = n * group
     return pl.pallas_call(
         functools.partial(scores_kernel, n, m, masks),
         in_specs=[pl.BlockSpec(memory_space=pltpu.VMEM)] * (2 + 2 * n),
         out_specs=pl.BlockSpec(memory_space=pltpu.VMEM),
         out_shape=jax.ShapeDtypeStruct((n, n, n, m, width), jnp.float32),
-        scratch_shapes=[pltpu.VMEM((rows, half * LANES), jnp.float32)],
+        scratch_shapes=[pltpu.VMEM((n * n * m, R // n // 2 * LANES), jnp.float32)],
         compiler_params=params(40),
     )(h_hi, h_lo, *blocks, *grads)
 
@@ -191,25 +226,17 @@
     all_q[n // 2] = flip(queries, n // 2)
 
     far = list(range(n - 1, 1, -1))
-    y = project(activations, out_grads, proj_in, proj_out, far, m)
-    near, own = project(activations, after(out_grads, y), proj_in, proj_out, [1, 0], m)
+    y = project(activations, out_grads, proj_in, proj_out, far, m, 59)
+    near, own = project(activations, after(out_grads, y), proj_in, proj_out, [1, 0], m, 58)
     coded = [along(v, mask) for v, mask in zip(y, far)] + [along(near, 1)]
-
-    own, all_q[n // 2] = lax.optimization_barrier((own, all_q[n // 2]))
-    grads = grads_of(own, coded, n, m, bits)
+    grads = grads_of(own * TOP, coded, n, m, bits)
+    h_hi, h_lo = halves(hess_inv, [grads, all_q[n // 2]])
     parts = [flip(grads[p], bitrev(p, bits)) for p in range(1, n)]
-    hess_inv = after(hess_inv, grads)
-    h_top = lax.reduce_precision(hess_inv, 8, 7)
-    h_hi = h_top.astype(jnp.bfloat16)
-    h_lo = (hess_inv - h_top).astype(jnp.bfloat16)
     first, h_hi, h_lo = lax.optimization_barrier((grads[0], h_hi, h_lo))
-    parts = [first] + parts
-    group = jnp.concatenate(parts, 1)
+    group = jnp.stack([first] + parts)
     groups = [group] + [along(group, s) for s in range(1, n)]
-
     for b in reversed(range(bits - 1)):
-        keys = list(all_q)
-        all_q = dict(zip(keys, after(tuple(all_q.values()), group)))
+        all_q = dict(zip(all_q, after(tuple(all_q.values()), group)))
         all_q.update({k | (1 << b): flip(v, 1 << b) for k, v in all_q.items()})
 
     out = scores_of(h_hi, h_lo, all_q, groups, n, m)
@@ -229,7 +256,7 @@
         stop = begin + m
         rows.append(total[owner * m + i - begin : owner * m + stop - begin])
         i = stop
-    scale = (1.0 / math.sqrt(SEQ)) * (1.0 / math.sqrt(R * R))
+    scale = (1.0 / math.sqrt(SEQ)) * (1.0 / math.sqrt(R * R)) / (TOP * TOP)
     return jnp.concatenate(rows, 0)[:examples] * scale
 
 

time: 59.2 us -> 56.6 us (0.956)
  other arithmetic: 3.84 us -> 1.69 us
  waiting for transfers between devices: 20.2 us -> 18.9 us
  local copies, waits for them, and re-layouts: 1.03 us -> 0.08 us
  Pallas kernels: 15.2 us -> 16.1 us
  starting transfers between devices: 18.7 us -> 19.5 us
    convert_element_type x1 -> x0, other arithmetic: 3.1 us -> none  [local(): h_lo = (hess_inv - h_top).astype(jnp.bfloat16)]
    mul x0 -> x1, other arithmetic: none -> 0.97 us  [local(): grads = grads_of(own * TOP, coded, n, m, bits)]
    unnamed x4, local copies, waits for them, and re-layouts: 0.95 us -> 0.01 us
    ppermute x8, starting transfers between devices: 6.4 us -> 7.2 us  [flip(): return lax.ppermute(v, 'dp', [(i, i ^ mask) for i in range(n)])]
    ppermute x9, waiting for transfers between devices: 13.8 us -> 13 us  [along(): return lax.ppermute(v, 'tensor', [(i, i ^ mask) for i in range(n)])]
    pallas_call x0 -> x1, Pallas kernels: none -> 0.6 us  [halves(): pl.pallas_call(halves_kernel, grid=(h.shape[0] // rows,), in_specs=[spec]...]
  transfers between devices with their start and end apart: 17 -> 17, of which waited for: 10 -> 10; matrix products, arithmetic and copies ran while one was open for 5% -> 2% of each run, Pallas kernels for 21% -> 25%
where the time goes in v3:
time: 56.6 us; the launch traced here: 56.4 us
  starting transfers between devices  19.5 us (34%)
  waiting for transfers between devices  18.9 us (33%)
  Pallas kernels  16.1 us (28%)
  other arithmetic  1.69 us (3%)
    ppermute x9, waiting for transfers between devices, along(): return lax.ppermute(v, 'tensor', [(i, i ^ mask) for i in range(n)])  13 us
    pallas_call x2, Pallas kernels, project(): pl.pallas_call(functools.partial(project_kernel, masks), grid=(len(masks)...  12.9 us
    ppermute x9, starting transfers between devices, along(): return lax.ppermute(v, 'tensor', [(i, i ^ mask) for i in range(n)])  12.3 us
    ppermute x8, starting transfers between devices, flip(): return lax.ppermute(v, 'dp', [(i, i ^ mask) for i in range(n)])  7.2 us
    ppermute x8, waiting for transfers between devices, flip(): return lax.ppermute(v, 'dp', [(i, i ^ mask) for i in range(n)])  5.94 us
    pallas_call x1, Pallas kernels, scores_of(): pl.pallas_call(functools.partial(scores_kernel, n, m, masks), in_specs=[p...  1.81 us
  transfers between devices with their start and end apart: 17, of which 10 were waited for; matrix products, arithmetic and copies ran while one was open for 2% of the time, Pallas kernels for 25%

profile of v3, /device:TPU:0, one launch (start us, length us, event | category | flops | bytes accessed | tf_op | source)
XLA Modules:
  0.0 56.4 jit_solution(7507692254693018260)
XLA Ops:
  0.0 2.9 %collective-permute-start.3 = (bf16[384,1024]{1,0:T(8,128)(2,1)}, bf16[384,1024]{1,0:T(8,128)(2,1)S(1)}, u32[]{:S(2)}, u32[]{:S(2)}) collective-permute-start(bf16[384,1024]{1,0:T(8,128)(2,1)} %refs_0_), channel_id=1, source_target_pairs={{0,8},{4,12},{8,0},{12,4},{1,9},{5,13},{9,1},{13,5},{2,10},{6,14},... | collective-permute-start | bytes 2359304 | tf_op jit(solution)/shard_map/ppermute | solution.py:220
  2.9 6.4 %shard_map.64 = (bf16[528,128]{1,0:T(8,128)(2,1)}, bf16[528,128]{1,0:T(8,128)(2,1)}) custom-call(bf16[1920,3584]{1,0:T(8,128)(2,1)} %acts.3, bf16[1920,1024]{1,0:T(8,128)(2,1)} %outs.2, bf16[64,3584]{1,0:T(8,128)(2,1)} %p_in.3, bf16[64,1024]{1,0:T(8,128)(2,1)} %p_out.3), custom_call_target="tpu_custom_call" | custom-call | flops 1 | bytes 1 | tf_op jit(solution)/shard_map/pallas_call | solution.py:87
  9.3 3.6 %collective-permute-start = (bf16[528,128]{1,0:T(8,128)(2,1)}, bf16[528,128]{1,0:T(8,128)(2,1)S(1)}, u32[]{:S(2)}, u32[]{:S(2)}) collective-permute-start(bf16[528,128]{1,0:T(8,128)(2,1)} %get-tuple-element.17), channel_id=1, source_target_pairs={{0,3},{1,2},{2,1},{3,0},{4,7},{5,6},{6,5},{7,4},{8,11},{9,10},{10,... | collective-permute-start | bytes 405512 | tf_op jit(solution)/shard_map/ppermute | solution.py:217
  12.9 6.5 %shard_map.65 = (bf16[528,128]{1,0:T(8,128)(2,1)}, f32[512,128]{1,0:T(8,128)}) custom-call(bf16[1920,3584]{1,0:T(8,128)(2,1)} %acts.3, bf16[1920,1024]{1,0:T(8,128)(2,1)} %outs.2, bf16[64,3584]{1,0:T(8,128)(2,1)} %p_in.3, bf16[64,1024]{1,0:T(8,128)(2,1)} %p_out.3), custom_call_target="tpu_custom_call" | custom-call | flops 1 | bytes 1 | tf_op jit(solution)/shard_map/pallas_call | solution.py:87
  19.4 0.8 %collective-permute-start.2 = (bf16[528,128]{1,0:T(8,128)(2,1)}, bf16[528,128]{1,0:T(8,128)(2,1)S(1)}, u32[]{:S(2)}, u32[]{:S(2)}) collective-permute-start(bf16[528,128]{1,0:T(8,128)(2,1)} %get-tuple-element.21), channel_id=1, source_target_pairs={{0,1},{1,0},{2,3},{3,2},{4,5},{5,4},{6,7},{7,6},{8,9},{9,8},{10,11... | collective-permute-start | bytes 405512 | tf_op jit(solution)/shard_map/ppermute | solution.py:217
  20.2 1.0 %broadcast_multiply_fusion.own = f32[512,128]{1,0:T(8,128)S(1)} fusion(f32[512,128]{1,0:T(8,128)} %get-tuple-element.20), kind=kLoop, calls=%fused_computation.1 | loop fusion | flops 65536 | bytes 524288 | tf_op jit(solution)/shard_map/mul | solution.py:232
  21.2 3.2 %collective-permute-done.1.refs_1_ = bf16[528,128]{1,0:T(8,128)(2,1)S(1)} collective-permute-done((bf16[528,128]{1,0:T(8,128)(2,1)}, bf16[528,128]{1,0:T(8,128)(2,1)S(1)}, u32[]{:S(2)}, u32[]{:S(2)}) %collective-permute-start.1) | collective-permute-done | bytes 135200 | tf_op jit(solution)/shard_map/ppermute | solution.py:217
  24.4 2.4 %collective-permute-done.2.refs_2_ = bf16[528,128]{1,0:T(8,128)(2,1)S(1)} collective-permute-done((bf16[528,128]{1,0:T(8,128)(2,1)}, bf16[528,128]{1,0:T(8,128)(2,1)S(1)}, u32[]{:S(2)}, u32[]{:S(2)}) %collective-permute-start.2) | collective-permute-done | bytes 135200 | tf_op jit(solution)/shard_map/ppermute | solution.py:217
  26.7 0.8 %shard_map.66.refs_0_ = bf16[4,36,128]{2,1,0:T(8,128)(2,1)S(1)} custom-call(f32[512,128]{1,0:T(8,128)S(1)} %broadcast_multiply_fusion.own, bf16[528,128]{1,0:T(8,128)(2,1)S(1)} %collective-permute-done.refs_0_, bf16[528,128]{1,0:T(8,128)(2,1)S(1)} %collective-permute-done.1.refs_1_, bf16[528,128]{1,0:T(8,128)(2,1)S(1)} %collective-permute-done.2.refs_2_), custom_call_target="tpu_custom_call" | custom-call | flops 1 | bytes 1 | tf_op jit(solution)/shard_map/pallas_call | solution.py:139
  27.5 0.6 %collective-permute-start.4 = (bf16[36,128]{1,0:T(8,128)(2,1)S(1)}, bf16[36,128]{1,0:T(8,128)(2,1)S(1)}, u32[]{:S(2)}, u32[]{:S(2)}) collective-permute-start(bf16[36,128]{1,0:T(8,128)(2,1)S(1)} %get-tuple-element.32), channel_id=1, source_target_pairs={{0,8},{4,12},{8,0},{12,4},{1,9},{5,13},{9,1},{13,5},{2,10},{6,14},... | collective-permute-start | bytes 27656 | tf_op jit(solution)/shard_map/ppermute | solution.py:220
  28.2 0.3 collective-permute-start.6
  28.5 1.3 %collective-permute-start.5 = (bf16[36,128]{1,0:T(8,128)(2,1)S(1)}, bf16[36,128]{1,0:T(8,128)(2,1)S(1)}, u32[]{:S(2)}, u32[]{:S(2)}) collective-permute-start(bf16[36,128]{1,0:T(8,128)(2,1)S(1)} %get-tuple-element.34), channel_id=1, source_target_pairs={{0,4},{4,0},{8,12},{12,8},{1,5},{5,1},{9,13},{13,9},{2,6},{6,2},{1... | collective-permute-start | bytes 27656 | tf_op jit(solution)/shard_map/ppermute | solution.py:220
  29.8 0.6 %shard_map.67 = (bf16[1024,1024]{1,0:T(8,128)(2,1)S(1)}, bf16[1024,1024]{1,0:T(8,128)(2,1)S(1)}) custom-call(f32[1024,1024]{1,0:T(8,128)S(1)} %copy-done, bf16[4,36,128]{2,1,0:T(8,128)(2,1)S(1)} %shard_map.66.refs_0_, bf16[384,1024]{1,0:T(8,128)(2,1)S(1)} %collective-permute-done.3.refs_1_.refs_2_), custom_call_target="tpu_custom_call" | custom-call | flops 1 | bytes 1 | tf_op jit(solution)/shard_map/pallas_call | solution.py:160
  30.4 1.0 %collective-permute-done.4 = bf16[36,128]{1,0:T(8,128)(2,1)S(1)} collective-permute-done((bf16[36,128]{1,0:T(8,128)(2,1)S(1)}, bf16[36,128]{1,0:T(8,128)(2,1)S(1)}, u32[]{:S(2)}, u32[]{:S(2)}) %collective-permute-start.4) | collective-permute-done | bytes 9248 | tf_op jit(solution)/shard_map/ppermute | solution.py:220
  31.4 0.2 collective-permute-start.7
  31.6 0.4 collective-permute-start.8
  32.0 2.2 %collective-permute-start.11 = (bf16[4,36,128]{2,1,0:T(8,128)(2,1)S(1)}, bf16[4,36,128]{2,1,0:T(8,128)(2,1)S(1)}, u32[]{:S(2)}, u32[]{:S(2)}) collective-permute-start(bf16[4,36,128]{2,1,0:T(8,128)(2,1)S(1)} %pad_maximum_fusion.refs_4_), channel_id=1, source_target_pairs={{0,3},{1,2},{2,1},{3,0},{4,7},{5,6},{6,5},{7,4},{8,11},{9,10},{10,... | collective-permute-start | bytes 110600 | tf_op jit(solution)/shard_map/ppermute | solution.py:217
  34.2 2.2 %collective-permute-start.9 = (bf16[4,36,128]{2,1,0:T(8,128)(2,1)S(1)}, bf16[4,36,128]{2,1,0:T(8,128)(2,1)S(1)}, u32[]{:S(2)}, u32[]{:S(2)}) collective-permute-start(bf16[4,36,128]{2,1,0:T(8,128)(2,1)S(1)} %pad_maximum_fusion.refs_4_), channel_id=1, source_target_pairs={{0,1},{1,0},{2,3},{3,2},{4,5},{5,4},{6,7},{7,6},{8,9},{9,8},{10,11... | collective-permute-start | bytes 110600 | tf_op jit(solution)/shard_map/ppermute | solution.py:217
  36.4 1.5 %collective-permute-done.11.refs_7_ = bf16[4,36,128]{2,1,0:T(8,128)(2,1)S(1)} collective-permute-done((bf16[4,36,128]{2,1,0:T(8,128)(2,1)S(1)}, bf16[4,36,128]{2,1,0:T(8,128)(2,1)S(1)}, u32[]{:S(2)}, u32[]{:S(2)}) %collective-permute-start.11) | collective-permute-done | bytes 36896 | tf_op jit(solution)/shard_map/ppermute | solution.py:217
  37.8 1.3 %collective-permute-done.10.refs_6_ = bf16[4,36,128]{2,1,0:T(8,128)(2,1)S(1)} collective-permute-done((bf16[4,36,128]{2,1,0:T(8,128)(2,1)S(1)}, bf16[4,36,128]{2,1,0:T(8,128)(2,1)S(1)}, u32[]{:S(2)}, u32[]{:S(2)}) %collective-permute-start.10) | collective-permute-done | bytes 36896 | tf_op jit(solution)/shard_map/ppermute | solution.py:217
  39.2 1.8 %shard_map.68 = f32[4,4,4,4,384]{4,3,2,1,0:T(4,128)S(1)} custom-call(bf16[1024,1024]{1,0:T(8,128)(2,1)S(1)} %get-tuple-element.24.h_hi, bf16[1024,1024]{1,0:T(8,128)(2,1)S(1)} %get-tuple-element.25.h_lo, bf16[384,1024]{1,0:T(8,128)(2,1)S(1)} %copy-done.1, bf16[384,1024]{1,0:T(8,128)(2,1)S(1)} %collective-permute-done.7.refs_1_, ...), custom_call_target="tpu_custom_call" | custom-call | tf_op jit(solution)/shard_map/pallas_call | solution.py:202
  41.0 0.1 collective-permute-start.12
  41.1 1.4 %collective-permute-done.12 = f32[2,4,4,4,384]{4,3,2,1,0:T(4,128)S(1)} collective-permute-done((f32[2,4,4,4,384]{4,3,2,1,0:T(4,128)S(1)}, f32[2,4,4,4,384]{4,3,2,1,0:T(4,128)S(1)}, u32[]{:S(2)}, u32[]{:S(2)}) %collective-permute-start.12) | collective-permute-done | bytes 196640 | tf_op jit(solution)/shard_map/ppermute | solution.py:220
  42.6 1.4 %collective-permute-start.13 = (f32[1,4,4,4,384]{4,3,2,1,0:T(4,128)S(1)}, f32[1,4,4,4,384]{4,3,2,1,0:T(4,128)S(1)}, u32[]{:S(2)}, u32[]{:S(2)}) collective-permute-start(f32[1,4,4,4,384]{4,3,2,1,0:T(4,128)S(1)} %slice.87), channel_id=1, source_target_pairs={{0,8},{4,12},{8,0},{12,4},{1,9},{5,13},{9,1},{13,5},{2,10},{6,14},... | collective-permute-start | bytes 294920 | tf_op jit(solution)/shard_map/ppermute | solution.py:220
  44.0 3.5 %collective-permute-done.13 = f32[1,4,4,4,384]{4,3,2,1,0:T(4,128)S(1)} collective-permute-done((f32[1,4,4,4,384]{4,3,2,1,0:T(4,128)S(1)}, f32[1,4,4,4,384]{4,3,2,1,0:T(4,128)S(1)}, u32[]{:S(2)}, u32[]{:S(2)}) %collective-permute-start.13) | collective-permute-done | bytes 98336 | tf_op jit(solution)/shard_map/ppermute | solution.py:220
  47.6 1.3 %collective-permute-start.14 = (f32[4,4,384]{2,1,0:T(4,128)S(1)}, f32[4,4,384]{2,1,0:T(4,128)S(1)}, u32[]{:S(2)}, u32[]{:S(2)}) collective-permute-start(f32[4,4,384]{2,1,0:T(4,128)S(1)} %get-tuple-element.29), channel_id=1, source_target_pairs={{0,1},{1,0},{2,3},{3,2},{4,5},{5,4},{6,7},{7,6},{8,9},{9,8},{10,11... | collective-permute-start | bytes 73736 | tf_op jit(solution)/shard_map/ppermute | solution.py:217
  48.8 2.2 %collective-permute-start.16 = (f32[4,4,384]{2,1,0:T(4,128)S(1)}, f32[4,4,384]{2,1,0:T(4,128)S(1)}, u32[]{:S(2)}, u32[]{:S(2)}) collective-permute-start(f32[4,4,384]{2,1,0:T(4,128)S(1)} %get-tuple-element.30), channel_id=1, source_target_pairs={{0,3},{1,2},{2,1},{3,0},{4,7},{5,6},{6,5},{7,4},{8,11},{9,10},{10,... | collective-permute-start | bytes 73736 | tf_op jit(solution)/shard_map/ppermute | solution.py:217
  51.0 0.1 collective-permute-start.15
  51.1 0.3 collective-permute-done.14
  51.5 3.0 %collective-permute-done.16 = f32[4,4,384]{2,1,0:T(4,128)S(1)} collective-permute-done((f32[4,4,384]{2,1,0:T(4,128)S(1)}, f32[4,4,384]{2,1,0:T(4,128)S(1)}, u32[]{:S(2)}, u32[]{:S(2)}) %collective-permute-start.16) | collective-permute-done | bytes 24608 | tf_op jit(solution)/shard_map/ppermute | solution.py:217
  54.5 1.3 %collective-permute-done.15 = f32[4,4,384]{2,1,0:T(4,128)S(1)} collective-permute-done((f32[4,4,384]{2,1,0:T(4,128)S(1)}, f32[4,4,384]{2,1,0:T(4,128)S(1)}, u32[]{:S(2)}, u32[]{:S(2)}) %collective-permute-start.15) | collective-permute-done | bytes 24608 | tf_op jit(solution)/shard_map/ppermute | solution.py:217
  55.8 0.6 %maximum_multiply_fusion = f32[15,384]{1,0:T(8,128)} fusion(f32[3,384]{1,0:T(4,128)S(1)} %slice.95, f32[4,384]{1,0:T(4,128)S(1)} %get-tuple-element.37, f32[4,384]{1,0:T(4,128)S(1)} %get-tuple-element.38, f32[4,384]{1,0:T(4,128)S(1)} %get-tuple-element.36), kind=kLoop, calls=%fused_computation.11 | loop fusion | flops 23040 | bytes 46080 | tf_op jit(solution)/shard_map/mul | solution.py:260
  (24 shorter events, 0.2 us)
Async XLA Ops:
  0.0 29.8 %collective-permute-start.3 = (bf16[384,1024]{1,0:T(8,128)(2,1)}, bf16[384,1024]{1,0:T(8,128)(2,1)S(1)}, u32[]{:S(2)}, u32[]{:S(2)}) collective-permute-start(bf16[384,1024]{1,0:T(8,128)(2,1)} %refs_0_), channel_id=1, source_target_pairs={{0,8},{4,12},{8,0},{12,4},{1,9},{5,13},{9,1},{13,5},{2,10},{6,14},... | collective-permute-start | bytes 2359304 | tf_op jit(solution)/shard_map/ppermute | solution.py:220
  9.3 11.8 %collective-permute-start = (bf16[528,128]{1,0:T(8,128)(2,1)}, bf16[528,128]{1,0:T(8,128)(2,1)S(1)}, u32[]{:S(2)}, u32[]{:S(2)}) collective-permute-start(bf16[528,128]{1,0:T(8,128)(2,1)} %get-tuple-element.17), channel_id=1, source_target_pairs={{0,3},{1,2},{2,1},{3,0},{4,7},{5,6},{6,5},{7,4},{8,11},{9,10},{10,... | collective-permute-start | bytes 405512 | tf_op jit(solution)/shard_map/ppermute | solution.py:217
  12.9 11.4 %collective-permute-start.1 = (bf16[528,128]{1,0:T(8,128)(2,1)}, bf16[528,128]{1,0:T(8,128)(2,1)S(1)}, u32[]{:S(2)}, u32[]{:S(2)}) collective-permute-start(bf16[528,128]{1,0:T(8,128)(2,1)} %get-tuple-element.18), channel_id=1, source_target_pairs={{0,2},{1,3},{2,0},{3,1},{4,6},{5,7},{6,4},{7,5},{8,10},{9,11},{10,... | collective-permute-start | bytes 405512 | tf_op jit(solution)/shard_map/ppermute | solution.py:217
  12.9 16.8 %copy-start = (f32[1024,1024]{1,0:T(8,128)S(1)}, f32[1024,1024]{1,0:T(8,128)}, u32[]{:S(2)}) copy-start(f32[1024,1024]{1,0:T(8,128)} %h.1) | copy-start | bytes 12582916
  19.4 12.0 %copy-start.1 = (bf16[384,1024]{1,0:T(8,128)(2,1)S(1)}, bf16[384,1024]{1,0:T(8,128)(2,1)}, u32[]{:S(2)}) copy-start(bf16[384,1024]{1,0:T(8,128)(2,1)} %refs_0_) | copy-start | bytes 2359300
  19.4 7.3 %collective-permute-start.2 = (bf16[528,128]{1,0:T(8,128)(2,1)}, bf16[528,128]{1,0:T(8,128)(2,1)S(1)}, u32[]{:S(2)}, u32[]{:S(2)}) collective-permute-start(bf16[528,128]{1,0:T(8,128)(2,1)} %get-tuple-element.21), channel_id=1, source_target_pairs={{0,1},{1,0},{2,3},{3,2},{4,5},{5,4},{6,7},{7,6},{8,9},{9,8},{10,11... | collective-permute-start | bytes 405512 | tf_op jit(solution)/shard_map/ppermute | solution.py:217
  27.5 3.8 %collective-permute-start.4 = (bf16[36,128]{1,0:T(8,128)(2,1)S(1)}, bf16[36,128]{1,0:T(8,128)(2,1)S(1)}, u32[]{:S(2)}, u32[]{:S(2)}) collective-permute-start(bf16[36,128]{1,0:T(8,128)(2,1)S(1)} %get-tuple-element.32), channel_id=1, source_target_pairs={{0,8},{4,12},{8,0},{12,4},{1,9},{5,13},{9,1},{13,5},{2,10},{6,14},... | collective-permute-start | bytes 27656 | tf_op jit(solution)/shard_map/ppermute | solution.py:220
  28.2 3.2 %collective-permute-start.6 = (bf16[36,128]{1,0:T(8,128)(2,1)S(1)}, bf16[36,128]{1,0:T(8,128)(2,1)S(1)}, u32[]{:S(2)}, u32[]{:S(2)}) collective-permute-start(bf16[36,128]{1,0:T(8,128)(2,1)S(1)} %get-tuple-element.33), channel_id=1, source_target_pairs={{0,12},{4,8},{8,4},{12,0},{1,13},{5,9},{9,5},{13,1},{2,14},{6,10},... | collective-permute-start | bytes 27656 | tf_op jit(solution)/shard_map/ppermute | solution.py:220
  28.5 2.9 %collective-permute-start.5 = (bf16[36,128]{1,0:T(8,128)(2,1)S(1)}, bf16[36,128]{1,0:T(8,128)(2,1)S(1)}, u32[]{:S(2)}, u32[]{:S(2)}) collective-permute-start(bf16[36,128]{1,0:T(8,128)(2,1)S(1)} %get-tuple-element.34), channel_id=1, source_target_pairs={{0,4},{4,0},{8,12},{12,8},{1,5},{5,1},{9,13},{13,9},{2,6},{6,2},{1... | collective-permute-start | bytes 27656 | tf_op jit(solution)/shard_map/ppermute | solution.py:220
  31.4 7.8 %collective-permute-start.7 = (bf16[384,1024]{1,0:T(8,128)(2,1)S(1)}, bf16[384,1024]{1,0:T(8,128)(2,1)S(1)}, u32[]{:S(2)}, u32[]{:S(2)}) collective-permute-start(bf16[384,1024]{1,0:T(8,128)(2,1)S(1)} %copy-done.1), channel_id=1, source_target_pairs={{0,4},{4,0},{8,12},{12,8},{1,5},{5,1},{9,13},{13,9},{2,6},{6,2},{1... | collective-permute-start | bytes 2359304 | tf_op jit(solution)/shard_map/ppermute | solution.py:220
  31.6 7.6 %collective-permute-start.8 = (bf16[384,1024]{1,0:T(8,128)(2,1)S(1)}, bf16[384,1024]{1,0:T(8,128)(2,1)S(1)}, u32[]{:S(2)}, u32[]{:S(2)}) collective-permute-start(bf16[384,1024]{1,0:T(8,128)(2,1)S(1)} %collective-permute-done.3.refs_1_.refs_2_), channel_id=1, source_target_pairs={{0,4},{4,0},{8,12},{12,8},{1,5},{5,1},{9,13},{13,9},{2,6},{6,2},{1... | collective-permute-start | bytes 2359304 | tf_op jit(solution)/shard_map/ppermute | solution.py:220
  32.0 5.9 %collective-permute-start.11 = (bf16[4,36,128]{2,1,0:T(8,128)(2,1)S(1)}, bf16[4,36,128]{2,1,0:T(8,128)(2,1)S(1)}, u32[]{:S(2)}, u32[]{:S(2)}) collective-permute-start(bf16[4,36,128]{2,1,0:T(8,128)(2,1)S(1)} %pad_maximum_fusion.refs_4_), channel_id=1, source_target_pairs={{0,3},{1,2},{2,1},{3,0},{4,7},{5,6},{6,5},{7,4},{8,11},{9,10},{10,... | collective-permute-start | bytes 110600 | tf_op jit(solution)/shard_map/ppermute | solution.py:217
  34.2 5.0 %collective-permute-start.10 = (bf16[4,36,128]{2,1,0:T(8,128)(2,1)S(1)}, bf16[4,36,128]{2,1,0:T(8,128)(2,1)S(1)}, u32[]{:S(2)}, u32[]{:S(2)}) collective-permute-start(bf16[4,36,128]{2,1,0:T(8,128)(2,1)S(1)} %pad_maximum_fusion.refs_4_), channel_id=1, source_target_pairs={{0,2},{1,3},{2,0},{3,1},{4,6},{5,7},{6,4},{7,5},{8,10},{9,11},{10,... | collective-permute-start | bytes 110600 | tf_op jit(solution)/shard_map/ppermute | solution.py:217
  34.2 5.0 %collective-permute-start.9 = (bf16[4,36,128]{2,1,0:T(8,128)(2,1)S(1)}, bf16[4,36,128]{2,1,0:T(8,128)(2,1)S(1)}, u32[]{:S(2)}, u32[]{:S(2)}) collective-permute-start(bf16[4,36,128]{2,1,0:T(8,128)(2,1)S(1)} %pad_maximum_fusion.refs_4_), channel_id=1, source_target_pairs={{0,1},{1,0},{2,3},{3,2},{4,5},{5,4},{6,7},{7,6},{8,9},{9,8},{10,11... | collective-permute-start | bytes 110600 | tf_op jit(solution)/shard_map/ppermute | solution.py:217
  41.0 1.5 %collective-permute-start.12 = (f32[2,4,4,4,384]{4,3,2,1,0:T(4,128)S(1)}, f32[2,4,4,4,384]{4,3,2,1,0:T(4,128)S(1)}, u32[]{:S(2)}, u32[]{:S(2)}) collective-permute-start(f32[2,4,4,4,384]{4,3,2,1,0:T(4,128)S(1)} %slice.85), channel_id=1, source_target_pairs={{0,4},{4,0},{8,12},{12,8},{1,5},{5,1},{9,13},{13,9},{2,6},{6,2},{1... | collective-permute-start | bytes 589832 | tf_op jit(solution)/shard_map/ppermute | solution.py:220
  42.6 4.9 %collective-permute-start.13 = (f32[1,4,4,4,384]{4,3,2,1,0:T(4,128)S(1)}, f32[1,4,4,4,384]{4,3,2,1,0:T(4,128)S(1)}, u32[]{:S(2)}, u32[]{:S(2)}) collective-permute-start(f32[1,4,4,4,384]{4,3,2,1,0:T(4,128)S(1)} %slice.87), channel_id=1, source_target_pairs={{0,8},{4,12},{8,0},{12,4},{1,9},{5,13},{9,1},{13,5},{2,10},{6,14},... | collective-permute-start | bytes 294920 | tf_op jit(solution)/shard_map/ppermute | solution.py:220
  47.6 3.9 %collective-permute-start.14 = (f32[4,4,384]{2,1,0:T(4,128)S(1)}, f32[4,4,384]{2,1,0:T(4,128)S(1)}, u32[]{:S(2)}, u32[]{:S(2)}) collective-permute-start(f32[4,4,384]{2,1,0:T(4,128)S(1)} %get-tuple-element.29), channel_id=1, source_target_pairs={{0,1},{1,0},{2,3},{3,2},{4,5},{5,4},{6,7},{7,6},{8,9},{9,8},{10,11... | collective-permute-start | bytes 73736 | tf_op jit(solution)/shard_map/ppermute | solution.py:217
  48.8 5.6 %collective-permute-start.16 = (f32[4,4,384]{2,1,0:T(4,128)S(1)}, f32[4,4,384]{2,1,0:T(4,128)S(1)}, u32[]{:S(2)}, u32[]{:S(2)}) collective-permute-start(f32[4,4,384]{2,1,0:T(4,128)S(1)} %get-tuple-element.30), channel_id=1, source_target_pairs={{0,3},{1,2},{2,1},{3,0},{4,7},{5,6},{6,5},{7,4},{8,11},{9,10},{10,... | collective-permute-start | bytes 73736 | tf_op jit(solution)/shard_map/ppermute | solution.py:217
  51.0 4.7 %collective-permute-start.15 = (f32[4,4,384]{2,1,0:T(4,128)S(1)}, f32[4,4,384]{2,1,0:T(4,128)S(1)}, u32[]{:S(2)}, u32[]{:S(2)}) collective-permute-start(f32[4,4,384]{2,1,0:T(4,128)S(1)} %get-tuple-element.31), channel_id=1, source_target_pairs={{0,2},{1,3},{2,0},{3,1},{4,6},{5,7},{6,4},{7,5},{8,10},{9,11},{10,... | collective-permute-start | bytes 73736 | tf_op jit(solution)/shard_map/ppermute | solution.py:217

commit v4 on v3

--- a/solution.py
+++ b/solution.py
@@ -186,13 +186,14 @@
     both = jnp.concatenate([hi, lo], 0)
     d, t = lax.axis_index("dp"), lax.axis_index("tensor")
     for mask, ref in zip(masks, queries):
-        to = lax.bitwise_xor(lax.bitwise_xor(d, mask), t)
+        to = lax.bitwise_xor(d, mask)
         s = lax.dot_general(both, ref[...], ROWS_CONTRACT, preferred_element_type=jnp.float32)
         s = s[:rows] + s[rows:]
         for p in range(n):
             for b in range(n):
                 at = (p * n + b) * m
-                out[b, to, lax.bitwise_xor(t, p)] = s[at : at + m]
+                back = bitrev(b, n.bit_length() - 1)
+                out[back & 1, lax.bitwise_xor(d >> 1, back >> 1), to, lax.bitwise_xor(t, p)] = s[at : at + m]
 
 
 def scores_of(h_hi, h_lo, queries, grads, n, m):
@@ -203,7 +204,7 @@
         functools.partial(scores_kernel, n, m, masks),
         in_specs=[pl.BlockSpec(memory_space=pltpu.VMEM)] * (2 + 2 * n),
         out_specs=pl.BlockSpec(memory_space=pltpu.VMEM),
-        out_shape=jax.ShapeDtypeStruct((n, n, n, m, width), jnp.float32),
+        out_shape=jax.ShapeDtypeStruct((2, n // 2, n, n, m, width), jnp.float32),
         scratch_shapes=[pltpu.VMEM((n * n * m, R // n // 2 * LANES), jnp.float32)],
         compiler_params=params(40),
     )(h_hi, h_lo, *blocks, *grads)
@@ -227,7 +228,8 @@
 
     far = list(range(n - 1, 1, -1))
     y = project(activations, out_grads, proj_in, proj_out, far, m, 59)
-    near, own = project(activations, after(out_grads, y), proj_in, proj_out, [1, 0], m, 58)
+    (near,) = project(activations, after(out_grads, y), proj_in, proj_out, [1], m, 59)
+    (own,) = project(activations, after(out_grads, near), proj_in, proj_out, [0], m, 57)
     coded = [along(v, mask) for v, mask in zip(y, far)] + [along(near, 1)]
     grads = grads_of(own * TOP, coded, n, m, bits)
     h_hi, h_lo = halves(hess_inv, [grads, all_q[n // 2]])
@@ -236,17 +238,15 @@
     group = jnp.stack([first] + parts)
     groups = [group] + [along(group, s) for s in range(1, n)]
     for b in reversed(range(bits - 1)):
-        all_q = dict(zip(all_q, after(tuple(all_q.values()), group)))
+        all_q = dict(zip(all_q, after(tuple(all_q.values()), grads)))
         all_q.update({k | (1 << b): flip(v, 1 << b) for k, v in all_q.items()})
 
     out = scores_of(h_hi, h_lo, all_q, groups, n, m)
-    for b in range(bits):
-        half = out.shape[0] // 2
-        out = out[:half] + flip(out[half:], 1 << b)
-    out = out[0]
-    total = out[0]
-    for s in range(1, n):
-        total = total + along(out[s], s)
+    out = out[0] + flip(out[1], 1)
+    same_core = [[(2 * x + core) * n + t for x in range(n // 2) for t in range(n)] for core in range(2)]
+    out = out.reshape(n * n // 2, n, m, out.shape[-1])
+    out = lax.all_to_all(out, ("dp", "tensor"), 0, 0, tiled=True, axis_index_groups=same_core)
+    total = jnp.sum(out, 0)
     width = total.shape[-1]
     total = total.reshape(n * m, width)
     rows, i = [], 0

time: 56.6 us -> 55.2 us (0.975)
  blocking collectives: 0 us -> 12.9 us
  waiting for transfers between devices: 18.9 us -> 6.61 us
  starting transfers between devices: 19.5 us -> 14.6 us
  Pallas kernels: 16.1 us -> 19.1 us
    all_to_all x0 -> x1, blocking collectives: none -> 12.9 us  [local(): lax.all_to_all(out, ('dp', 'tensor'), 0, 0, tiled=True, axis_index_groups...]
    ppermute x9 -> x6, waiting for transfers between devices: 13 us -> 4.18 us  [along(): return lax.ppermute(v, 'tensor', [(i, i ^ mask) for i in range(n)])]
    ppermute x8 -> x7, waiting for transfers between devices: 5.94 us -> 2.42 us  [flip(): return lax.ppermute(v, 'dp', [(i, i ^ mask) for i in range(n)])]
    ppermute x9 -> x6, starting transfers between devices: 12.3 us -> 8.84 us  [along(): return lax.ppermute(v, 'tensor', [(i, i ^ mask) for i in range(n)])]
    pallas_call x2 -> x3, Pallas kernels: 12.9 us -> 15.9 us  [project(): pl.pallas_call(functools.partial(project_kernel, masks), grid=(len(masks)...]
    ppermute x8 -> x7, starting transfers between devices: 7.2 us -> 5.72 us  [flip(): return lax.ppermute(v, 'dp', [(i, i ^ mask) for i in range(n)])]
  transfers between devices with their start and end apart: 17 -> 13, of which waited for: 10 -> 5; matrix products, arithmetic and copies ran while one was open for 2% -> 2% of each run, Pallas kernels for 25% -> 31%
where the time goes in v4:
time: 55.2 us; the launch traced here: 55 us
  Pallas kernels  19.1 us (35%)
  starting transfers between devices  14.6 us (26%)
  blocking collectives  12.9 us (23%)
  waiting for transfers between devices  6.61 us (12%)
  other arithmetic  1.69 us (3%)
    pallas_call x3, Pallas kernels, project(): pl.pallas_call(functools.partial(project_kernel, masks), grid=(len(masks)...  15.9 us
    all_to_all x1, blocking collectives, local(): lax.all_to_all(out, ('dp', 'tensor'), 0, 0, tiled=True, axis_index_groups...  12.9 us
    ppermute x6, starting transfers between devices, along(): return lax.ppermute(v, 'tensor', [(i, i ^ mask) for i in range(n)])  8.84 us
    ppermute x7, starting transfers between devices, flip(): return lax.ppermute(v, 'dp', [(i, i ^ mask) for i in range(n)])  5.72 us
    ppermute x6, waiting for transfers between devices, along(): return lax.ppermute(v, 'tensor', [(i, i ^ mask) for i in range(n)])  4.18 us
    ppermute x7, waiting for transfers between devices, flip(): return lax.ppermute(v, 'dp', [(i, i ^ mask) for i in range(n)])  2.42 us
    pallas_call x1, Pallas kernels, scores_of(): pl.pallas_call(functools.partial(scores_kernel, n, m, masks), in_specs=[p...  1.81 us
  transfers between devices with their start and end apart: 13, of which 5 were waited for; matrix products, arithmetic and copies ran while one was open for 2% of the time, Pallas kernels for 31%

profile of v4, /device:TPU:0, one launch (start us, length us, event | category | flops | bytes accessed | tf_op | source)
XLA Modules:
  0.0 55.0 jit_solution(8429235638932452139)
XLA Ops:
  0.0 2.9 %collective-permute-start.3 = (bf16[384,1024]{1,0:T(8,128)(2,1)}, bf16[384,1024]{1,0:T(8,128)(2,1)S(1)}, u32[]{:S(2)}, u32[]{:S(2)}) collective-permute-start(bf16[384,1024]{1,0:T(8,128)(2,1)} %refs_0_), channel_id=1, source_target_pairs={{0,8},{4,12},{8,0},{12,4},{1,9},{5,13},{9,1},{13,5},{2,10},{6,14},... | collective-permute-start | bytes 2359304 | tf_op jit(solution)/shard_map/ppermute | solution.py:221
  2.9 6.4 %shard_map.64 = (bf16[528,128]{1,0:T(8,128)(2,1)}, bf16[528,128]{1,0:T(8,128)(2,1)}) custom-call(bf16[1920,3584]{1,0:T(8,128)(2,1)} %acts.5, bf16[1920,1024]{1,0:T(8,128)(2,1)} %outs.3, bf16[64,3584]{1,0:T(8,128)(2,1)} %p_in.5, bf16[64,1024]{1,0:T(8,128)(2,1)} %p_out.5), custom_call_target="tpu_custom_call" | custom-call | flops 1 | bytes 1 | tf_op jit(solution)/shard_map/pallas_call | solution.py:87
  9.3 3.6 %collective-permute-start = (bf16[528,128]{1,0:T(8,128)(2,1)}, bf16[528,128]{1,0:T(8,128)(2,1)S(1)}, u32[]{:S(2)}, u32[]{:S(2)}) collective-permute-start(bf16[528,128]{1,0:T(8,128)(2,1)} %get-tuple-element.16), channel_id=1, source_target_pairs={{0,3},{1,2},{2,1},{3,0},{4,7},{5,6},{6,5},{7,4},{8,11},{9,10},{10,... | collective-permute-start | bytes 405512 | tf_op jit(solution)/shard_map/ppermute | solution.py:218
  12.9 0.0 collective-permute-start.1
  12.9 4.7 %shard_map.65 = bf16[528,128]{1,0:T(8,128)(2,1)} custom-call(bf16[1920,3584]{1,0:T(8,128)(2,1)} %acts.5, bf16[1920,1024]{1,0:T(8,128)(2,1)} %outs.3, bf16[64,3584]{1,0:T(8,128)(2,1)} %p_in.5, bf16[64,1024]{1,0:T(8,128)(2,1)} %p_out.5), custom_call_target="tpu_custom_call" | custom-call | flops 1 | bytes 1 | tf_op jit(solution)/shard_map/pallas_call | solution.py:87
  17.6 0.8 %collective-permute-start.2 = (bf16[528,128]{1,0:T(8,128)(2,1)}, bf16[528,128]{1,0:T(8,128)(2,1)S(1)}, u32[]{:S(2)}, u32[]{:S(2)}) collective-permute-start(bf16[528,128]{1,0:T(8,128)(2,1)} %shard_map.65), channel_id=1, source_target_pairs={{0,1},{1,0},{2,3},{3,2},{4,5},{5,4},{6,7},{7,6},{8,9},{9,8},{10,11... | collective-permute-start | bytes 405512 | tf_op jit(solution)/shard_map/ppermute | solution.py:218
  18.4 4.8 %shard_map.66 = f32[512,128]{1,0:T(8,128)} custom-call(bf16[1920,3584]{1,0:T(8,128)(2,1)} %acts.5, bf16[1920,1024]{1,0:T(8,128)(2,1)} %outs.3, bf16[64,3584]{1,0:T(8,128)(2,1)} %p_in.5, bf16[64,1024]{1,0:T(8,128)(2,1)} %p_out.5), custom_call_target="tpu_custom_call" | custom-call | flops 1 | bytes 1 | tf_op jit(solution)/shard_map/pallas_call | solution.py:87
  23.2 1.0 %broadcast_multiply_fusion.own = f32[512,128]{1,0:T(8,128)S(1)} fusion(f32[512,128]{1,0:T(8,128)} %shard_map.66), kind=kLoop, calls=%fused_computation.3 | loop fusion | flops 65536 | bytes 524288 | tf_op jit(solution)/shard_map/mul | solution.py:234
  24.2 1.3 %collective-permute-done.2.refs_2_ = bf16[528,128]{1,0:T(8,128)(2,1)S(1)} collective-permute-done((bf16[528,128]{1,0:T(8,128)(2,1)}, bf16[528,128]{1,0:T(8,128)(2,1)S(1)}, u32[]{:S(2)}, u32[]{:S(2)}) %collective-permute-start.2) | collective-permute-done | bytes 135200 | tf_op jit(solution)/shard_map/ppermute | solution.py:218
  25.5 0.0 collective-permute-done.refs_0_
  25.5 0.8 %shard_map.67.refs_0_ = bf16[4,36,128]{2,1,0:T(8,128)(2,1)S(1)} custom-call(f32[512,128]{1,0:T(8,128)S(1)} %broadcast_multiply_fusion.own, bf16[528,128]{1,0:T(8,128)(2,1)S(1)} %collective-permute-done.refs_0_, bf16[528,128]{1,0:T(8,128)(2,1)S(1)} %collective-permute-done.1.refs_1_, bf16[528,128]{1,0:T(8,128)(2,1)S(1)} %collective-permute-done.2.refs_2_), custom_call_target="tpu_custom_call" | custom-call | flops 1 | bytes 1 | tf_op jit(solution)/shard_map/pallas_call | solution.py:139
  26.3 0.1 collective-permute-start.4
  26.4 0.5 collective-permute-start.5
  26.9 0.5 collective-permute-start.6
  27.5 0.9 %collective-permute-start.8 = (bf16[36,128]{1,0:T(8,128)(2,1)S(1)}, bf16[36,128]{1,0:T(8,128)(2,1)S(1)}, u32[]{:S(2)}, u32[]{:S(2)}) collective-permute-start(bf16[36,128]{1,0:T(8,128)(2,1)S(1)} %get-tuple-element.28), channel_id=1, source_target_pairs={{0,12},{4,8},{8,4},{12,0},{1,13},{5,9},{9,5},{13,1},{2,14},{6,10},... | collective-permute-start | bytes 27656 | tf_op jit(solution)/shard_map/ppermute | solution.py:221
  28.4 0.7 %collective-permute-start.7 = (bf16[36,128]{1,0:T(8,128)(2,1)S(1)}, bf16[36,128]{1,0:T(8,128)(2,1)S(1)}, u32[]{:S(2)}, u32[]{:S(2)}) collective-permute-start(bf16[36,128]{1,0:T(8,128)(2,1)S(1)} %get-tuple-element.29), channel_id=1, source_target_pairs={{0,4},{4,0},{8,12},{12,8},{1,5},{5,1},{9,13},{13,9},{2,6},{6,2},{1... | collective-permute-start | bytes 27656 | tf_op jit(solution)/shard_map/ppermute | solution.py:221
  29.1 0.6 %shard_map.68 = (bf16[1024,1024]{1,0:T(8,128)(2,1)S(1)}, bf16[1024,1024]{1,0:T(8,128)(2,1)S(1)}) custom-call(f32[1024,1024]{1,0:T(8,128)S(1)} %copy-done, bf16[4,36,128]{2,1,0:T(8,128)(2,1)S(1)} %shard_map.67.refs_0_, bf16[384,1024]{1,0:T(8,128)(2,1)S(1)} %collective-permute-done.3.refs_1_.refs_2_), custom_call_target="tpu_custom_call" | custom-call | flops 1 | bytes 1 | tf_op jit(solution)/shard_map/pallas_call | solution.py:160
  29.7 1.0 %collective-permute-done.6 = bf16[36,128]{1,0:T(8,128)(2,1)S(1)} collective-permute-done((bf16[36,128]{1,0:T(8,128)(2,1)S(1)}, bf16[36,128]{1,0:T(8,128)(2,1)S(1)}, u32[]{:S(2)}, u32[]{:S(2)}) %collective-permute-start.6) | collective-permute-done | bytes 9248 | tf_op jit(solution)/shard_map/ppermute | solution.py:221
  30.7 0.0 collective-permute-done.7
  30.7 2.3 %collective-permute-start.11 = (bf16[4,36,128]{2,1,0:T(8,128)(2,1)S(1)}, bf16[4,36,128]{2,1,0:T(8,128)(2,1)S(1)}, u32[]{:S(2)}, u32[]{:S(2)}) collective-permute-start(bf16[4,36,128]{2,1,0:T(8,128)(2,1)S(1)} %pad_maximum_fusion.refs_4_), channel_id=1, source_target_pairs={{0,3},{1,2},{2,1},{3,0},{4,7},{5,6},{6,5},{7,4},{8,11},{9,10},{10,... | collective-permute-start | bytes 110600 | tf_op jit(solution)/shard_map/ppermute | solution.py:218
  33.0 0.0 collective-permute-start.10
  33.0 2.1 %collective-permute-start.9 = (bf16[4,36,128]{2,1,0:T(8,128)(2,1)S(1)}, bf16[4,36,128]{2,1,0:T(8,128)(2,1)S(1)}, u32[]{:S(2)}, u32[]{:S(2)}) collective-permute-start(bf16[4,36,128]{2,1,0:T(8,128)(2,1)S(1)} %pad_maximum_fusion.refs_4_), channel_id=1, source_target_pairs={{0,1},{1,0},{2,3},{3,2},{4,5},{5,4},{6,7},{7,6},{8,9},{9,8},{10,11... | collective-permute-start | bytes 110600 | tf_op jit(solution)/shard_map/ppermute | solution.py:218
  35.1 1.5 %collective-permute-done.11.refs_7_ = bf16[4,36,128]{2,1,0:T(8,128)(2,1)S(1)} collective-permute-done((bf16[4,36,128]{2,1,0:T(8,128)(2,1)S(1)}, bf16[4,36,128]{2,1,0:T(8,128)(2,1)S(1)}, u32[]{:S(2)}, u32[]{:S(2)}) %collective-permute-start.11) | collective-permute-done | bytes 36896 | tf_op jit(solution)/shard_map/ppermute | solution.py:218
  36.6 1.4 %collective-permute-done.10.refs_6_ = bf16[4,36,128]{2,1,0:T(8,128)(2,1)S(1)} collective-permute-done((bf16[4,36,128]{2,1,0:T(8,128)(2,1)S(1)}, bf16[4,36,128]{2,1,0:T(8,128)(2,1)S(1)}, u32[]{:S(2)}, u32[]{:S(2)}) %collective-permute-start.10) | collective-permute-done | bytes 36896 | tf_op jit(solution)/shard_map/ppermute | solution.py:218
  38.0 0.0 collective-permute-done.9.refs_5_
  38.0 0.0 collective-permute-done.4.refs_1_
  38.0 1.8 %shard_map.69 = f32[2,2,4,4,4,384]{5,4,3,2,1,0:T(4,128)S(1)} custom-call(bf16[1024,1024]{1,0:T(8,128)(2,1)S(1)} %get-tuple-element.22.h_hi, bf16[1024,1024]{1,0:T(8,128)(2,1)S(1)} %get-tuple-element.23.h_lo, bf16[384,1024]{1,0:T(8,128)(2,1)S(1)} %copy-done.1, bf16[384,1024]{1,0:T(8,128)(2,1)S(1)} %collective-permute-done.4.refs_1_, ...), custom_call_target="tpu_custom_call" | custom-call | tf_op jit(solution)/shard_map/pallas_call | solution.py:203
  39.8 0.1 collective-permute-start.12
  39.9 1.4 %collective-permute-done.12 = f32[2,4,4,4,384]{4,3,2,1,0:T(4,128)S(1)} collective-permute-done((f32[2,4,4,4,384]{4,3,2,1,0:T(4,128)S(1)}, f32[2,4,4,4,384]{4,3,2,1,0:T(4,128)S(1)}, u32[]{:S(2)}, u32[]{:S(2)}) %collective-permute-start.12) | collective-permute-done | bytes 196640 | tf_op jit(solution)/shard_map/ppermute | solution.py:221
  41.3 0.1 fusion
  41.4 12.9 %all_to_all.5 = f32[8,4,4,384]{3,2,1,0:T(4,128)S(1)} all-to-all(f32[8,4,4,384]{3,2,1,0:T(4,128)S(1)} %bitcast.25), channel_id=1, replica_groups={{0,1,2,3,8,9,10,11},{4,5,6,7,12,13,14,15},{16,17,18,19,24,25,26,27},{20..., dimensions={0} | all-to-all | bytes 393216 | tf_op jit(solution)/shard_map/all_to_all | solution.py:248
  54.4 0.6 %maximum_multiply_fusion = f32[15,384]{1,0:T(8,128)} fusion(f32[3,384]{1,0:T(4,128)S(1)} %slice.61, f32[4,384]{1,0:T(4,128)S(1)} %get-tuple-element.32, f32[4,384]{1,0:T(4,128)S(1)} %get-tuple-element.33, f32[4,384]{1,0:T(4,128)S(1)} %get-tuple-element.31), kind=kLoop, calls=%fused_computation.5 | loop fusion | flops 23040 | bytes 46080 | tf_op jit(solution)/shard_map/mul | solution.py:260
  (15 shorter events, 0.1 us)
Async XLA Ops:
  0.0 26.3 %collective-permute-start.3 = (bf16[384,1024]{1,0:T(8,128)(2,1)}, bf16[384,1024]{1,0:T(8,128)(2,1)S(1)}, u32[]{:S(2)}, u32[]{:S(2)}) collective-permute-start(bf16[384,1024]{1,0:T(8,128)(2,1)} %refs_0_), channel_id=1, source_target_pairs={{0,8},{4,12},{8,0},{12,4},{1,9},{5,13},{9,1},{13,5},{2,10},{6,14},... | collective-permute-start | bytes 2359304 | tf_op jit(solution)/shard_map/ppermute | solution.py:221
  9.3 16.2 %collective-permute-start = (bf16[528,128]{1,0:T(8,128)(2,1)}, bf16[528,128]{1,0:T(8,128)(2,1)S(1)}, u32[]{:S(2)}, u32[]{:S(2)}) collective-permute-start(bf16[528,128]{1,0:T(8,128)(2,1)} %get-tuple-element.16), channel_id=1, source_target_pairs={{0,3},{1,2},{2,1},{3,0},{4,7},{5,6},{6,5},{7,4},{8,11},{9,10},{10,... | collective-permute-start | bytes 405512 | tf_op jit(solution)/shard_map/ppermute | solution.py:218
  12.9 12.6 %collective-permute-start.1 = (bf16[528,128]{1,0:T(8,128)(2,1)}, bf16[528,128]{1,0:T(8,128)(2,1)S(1)}, u32[]{:S(2)}, u32[]{:S(2)}) collective-permute-start(bf16[528,128]{1,0:T(8,128)(2,1)} %get-tuple-element.17), channel_id=1, source_target_pairs={{0,2},{1,3},{2,0},{3,1},{4,6},{5,7},{6,4},{7,5},{8,10},{9,11},{10,... | collective-permute-start | bytes 405512 | tf_op jit(solution)/shard_map/ppermute | solution.py:218
  17.6 8.7 %copy-start.1 = (bf16[384,1024]{1,0:T(8,128)(2,1)S(1)}, bf16[384,1024]{1,0:T(8,128)(2,1)}, u32[]{:S(2)}) copy-start(bf16[384,1024]{1,0:T(8,128)(2,1)} %refs_0_) | copy-start | bytes 2359300
  17.6 7.9 %collective-permute-start.2 = (bf16[528,128]{1,0:T(8,128)(2,1)}, bf16[528,128]{1,0:T(8,128)(2,1)S(1)}, u32[]{:S(2)}, u32[]{:S(2)}) collective-permute-start(bf16[528,128]{1,0:T(8,128)(2,1)} %shard_map.65), channel_id=1, source_target_pairs={{0,1},{1,0},{2,3},{3,2},{4,5},{5,4},{6,7},{7,6},{8,9},{9,8},{10,11... | collective-permute-start | bytes 405512 | tf_op jit(solution)/shard_map/ppermute | solution.py:218
  18.4 10.7 %copy-start = (f32[1024,1024]{1,0:T(8,128)S(1)}, f32[1024,1024]{1,0:T(8,128)}, u32[]{:S(2)}) copy-start(f32[1024,1024]{1,0:T(8,128)} %h.1) | copy-start | bytes 12582916
  26.3 11.6 %collective-permute-start.4 = (bf16[384,1024]{1,0:T(8,128)(2,1)S(1)}, bf16[384,1024]{1,0:T(8,128)(2,1)S(1)}, u32[]{:S(2)}, u32[]{:S(2)}) collective-permute-start(bf16[384,1024]{1,0:T(8,128)(2,1)S(1)} %copy-done.1), channel_id=1, source_target_pairs={{0,4},{4,0},{8,12},{12,8},{1,5},{5,1},{9,13},{13,9},{2,6},{6,2},{1... | collective-permute-start | bytes 2359304 | tf_op jit(solution)/shard_map/ppermute | solution.py:221
  26.4 11.6 %collective-permute-start.5 = (bf16[384,1024]{1,0:T(8,128)(2,1)S(1)}, bf16[384,1024]{1,0:T(8,128)(2,1)S(1)}, u32[]{:S(2)}, u32[]{:S(2)}) collective-permute-start(bf16[384,1024]{1,0:T(8,128)(2,1)S(1)} %collective-permute-done.3.refs_1_.refs_2_), channel_id=1, source_target_pairs={{0,4},{4,0},{8,12},{12,8},{1,5},{5,1},{9,13},{13,9},{2,6},{6,2},{1... | collective-permute-start | bytes 2359304 | tf_op jit(solution)/shard_map/ppermute | solution.py:221
  26.9 3.7 %collective-permute-start.6 = (bf16[36,128]{1,0:T(8,128)(2,1)S(1)}, bf16[36,128]{1,0:T(8,128)(2,1)S(1)}, u32[]{:S(2)}, u32[]{:S(2)}) collective-permute-start(bf16[36,128]{1,0:T(8,128)(2,1)S(1)} %get-tuple-element.27), channel_id=1, source_target_pairs={{0,8},{4,12},{8,0},{12,4},{1,9},{5,13},{9,1},{13,5},{2,10},{6,14},... | collective-permute-start | bytes 27656 | tf_op jit(solution)/shard_map/ppermute | solution.py:221
  27.5 3.2 %collective-permute-start.8 = (bf16[36,128]{1,0:T(8,128)(2,1)S(1)}, bf16[36,128]{1,0:T(8,128)(2,1)S(1)}, u32[]{:S(2)}, u32[]{:S(2)}) collective-permute-start(bf16[36,128]{1,0:T(8,128)(2,1)S(1)} %get-tuple-element.28), channel_id=1, source_target_pairs={{0,12},{4,8},{8,4},{12,0},{1,13},{5,9},{9,5},{13,1},{2,14},{6,10},... | collective-permute-start | bytes 27656 | tf_op jit(solution)/shard_map/ppermute | solution.py:221
  28.4 2.3 %collective-permute-start.7 = (bf16[36,128]{1,0:T(8,128)(2,1)S(1)}, bf16[36,128]{1,0:T(8,128)(2,1)S(1)}, u32[]{:S(2)}, u32[]{:S(2)}) collective-permute-start(bf16[36,128]{1,0:T(8,128)(2,1)S(1)} %get-tuple-element.29), channel_id=1, source_target_pairs={{0,4},{4,0},{8,12},{12,8},{1,5},{5,1},{9,13},{13,9},{2,6},{6,2},{1... | collective-permute-start | bytes 27656 | tf_op jit(solution)/shard_map/ppermute | solution.py:221
  30.7 5.9 %collective-permute-start.11 = (bf16[4,36,128]{2,1,0:T(8,128)(2,1)S(1)}, bf16[4,36,128]{2,1,0:T(8,128)(2,1)S(1)}, u32[]{:S(2)}, u32[]{:S(2)}) collective-permute-start(bf16[4,36,128]{2,1,0:T(8,128)(2,1)S(1)} %pad_maximum_fusion.refs_4_), channel_id=1, source_target_pairs={{0,3},{1,2},{2,1},{3,0},{4,7},{5,6},{6,5},{7,4},{8,11},{9,10},{10,... | collective-permute-start | bytes 110600 | tf_op jit(solution)/shard_map/ppermute | solution.py:218
  33.0 4.9 %collective-permute-start.10 = (bf16[4,36,128]{2,1,0:T(8,128)(2,1)S(1)}, bf16[4,36,128]{2,1,0:T(8,128)(2,1)S(1)}, u32[]{:S(2)}, u32[]{:S(2)}) collective-permute-start(bf16[4,36,128]{2,1,0:T(8,128)(2,1)S(1)} %pad_maximum_fusion.refs_4_), channel_id=1, source_target_pairs={{0,2},{1,3},{2,0},{3,1},{4,6},{5,7},{6,4},{7,5},{8,10},{9,11},{10,... | collective-permute-start | bytes 110600 | tf_op jit(solution)/shard_map/ppermute | solution.py:218
  33.0 4.9 %collective-permute-start.9 = (bf16[4,36,128]{2,1,0:T(8,128)(2,1)S(1)}, bf16[4,36,128]{2,1,0:T(8,128)(2,1)S(1)}, u32[]{:S(2)}, u32[]{:S(2)}) collective-permute-start(bf16[4,36,128]{2,1,0:T(8,128)(2,1)S(1)} %pad_maximum_fusion.refs_4_), channel_id=1, source_target_pairs={{0,1},{1,0},{2,3},{3,2},{4,5},{5,4},{6,7},{7,6},{8,9},{9,8},{10,11... | collective-permute-start | bytes 110600 | tf_op jit(solution)/shard_map/ppermute | solution.py:218
  39.8 1.5 %collective-permute-start.12 = (f32[2,4,4,4,384]{4,3,2,1,0:T(4,128)S(1)}, f32[2,4,4,4,384]{4,3,2,1,0:T(4,128)S(1)}, u32[]{:S(2)}, u32[]{:S(2)}) collective-permute-start(f32[2,4,4,4,384]{4,3,2,1,0:T(4,128)S(1)} %slice_bitcast_fusion), channel_id=1, source_target_pairs={{0,4},{4,0},{8,12},{12,8},{1,5},{5,1},{9,13},{13,9},{2,6},{6,2},{1... | collective-permute-start | bytes 589832 | tf_op jit(solution)/shard_map/ppermute | solution.py:221

commit v5 on v4

--- a/solution.py
+++ b/solution.py
@@ -11,7 +11,8 @@
 R = 64
 SEQ = 128
 LANES = 128
-TOP = 128.0
+TOP = 8.0
+FLOOR = 0.07
 ROWS_CONTRACT = (((1,), (1,)), ((), ()))
 
 
@@ -31,16 +32,18 @@
 
 
 def power(x, top):
-    w = x * (TOP / top)
+    w = jnp.abs(x) * (TOP / top) + FLOOR
     s = w * w
     s = s * s
     s = s * s
     s = s * s
+    s = s * s
     return jnp.where(x < 0, -s, s)
 
 
 def root(y):
-    w = lax.rsqrt(lax.rsqrt(lax.rsqrt(lax.rsqrt(jnp.abs(y)))))
+    s = lax.rsqrt(lax.rsqrt(lax.rsqrt(lax.rsqrt(jnp.abs(y)))))
+    w = s * lax.rsqrt(s) - FLOOR
     return jnp.where(y < 0, -w, w)
 
 
@@ -78,7 +81,7 @@
     first = masks[0]
 
     def start(i):
-        return first_example(lax.bitwise_xor(lax.axis_index("tensor"), first - i), m, examples) * SEQ
+        return first_example(lax.bitwise_xor(lax.axis_index("tensor"), first + i), m, examples) * SEQ
 
     shapes = [
         jax.ShapeDtypeStruct((rows + 16, LANES), jnp.bfloat16) if k else jax.ShapeDtypeStruct((rows, LANES), jnp.float32)
@@ -210,6 +213,66 @@
     )(h_hi, h_lo, *blocks, *grads)
 
 
+def each(count, body):
+    if count <= 8:
+        for i in range(count):
+            body(i)
+    else:
+        lax.fori_loop(0, count, lambda i, c: (body(i), c)[1], 0)
+
+
+def pack_kernel(n, m, examples, ours, theirs, out):
+    def one(i):
+        x, t = i // n, i % n
+        rows, done = [], 0
+        while done < examples:
+            owner = min(done // m, n - 1)
+            begin = min(owner * m, examples - m)
+            both = ours[0, x, t, owner] + theirs[x, t, owner]
+            rows.append(both[done - begin :])
+            done = begin + m
+        both = jnp.concatenate(rows, 0)
+        top = column_top(both)
+        out[i] = jnp.concatenate([power(both, top), top], 0).astype(jnp.bfloat16)
+
+    each(n * n // 2, one)
+
+
+def pack(ours, theirs, n, m, examples):
+    width = ours.shape[-1]
+    return pl.pallas_call(
+        functools.partial(pack_kernel, n, m, examples),
+        in_specs=[pl.BlockSpec(memory_space=pltpu.VMEM)] * 2,
+        out_specs=pl.BlockSpec(memory_space=pltpu.VMEM),
+        out_shape=jax.ShapeDtypeStruct((n * n // 2, examples + 1, width), jnp.bfloat16),
+        compiler_params=params(40),
+    )(ours, theirs)
+
+
+def unpack_kernel(examples, scale, y_ref, out):
+    def term(i):
+        y = y_ref[i].astype(jnp.float32)
+        return root(y[:examples]) * y[examples:]
+
+    count = y_ref.shape[0]
+    if count <= 8:
+        total = sum(term(i) for i in range(count))
+    else:
+        total = lax.fori_loop(1, count, lambda i, c: c + term(i), term(0))
+    out[...] = total * scale
+
+
+def unpack(y, scale):
+    examples = y.shape[1] - 1
+    return pl.pallas_call(
+        functools.partial(unpack_kernel, examples, scale),
+        in_specs=[pl.BlockSpec(memory_space=pltpu.VMEM)],
+        out_specs=pl.BlockSpec(memory_space=pltpu.VMEM),
+        out_shape=jax.ShapeDtypeStruct((examples, y.shape[2]), jnp.float32),
+        compiler_params=params(24),
+    )(y)
+
+
 def local(n, activations, out_grads, proj_in, proj_out, hess_inv, queries):
     bits = n.bit_length() - 1
     examples = activations.shape[0] // SEQ
@@ -226,7 +289,7 @@
     all_q = {0: queries}
     all_q[n // 2] = flip(queries, n // 2)
 
-    far = list(range(n - 1, 1, -1))
+    far = list(range(2, n))
     y = project(activations, out_grads, proj_in, proj_out, far, m, 59)
     (near,) = project(activations, after(out_grads, y), proj_in, proj_out, [1], m, 59)
     (own,) = project(activations, after(out_grads, near), proj_in, proj_out, [0], m, 57)
@@ -242,22 +305,10 @@
         all_q.update({k | (1 << b): flip(v, 1 << b) for k, v in all_q.items()})
 
     out = scores_of(h_hi, h_lo, all_q, groups, n, m)
-    out = out[0] + flip(out[1], 1)
+    out = pack(out, flip(out[1], 1), n, m, examples)
     same_core = [[(2 * x + core) * n + t for x in range(n // 2) for t in range(n)] for core in range(2)]
-    out = out.reshape(n * n // 2, n, m, out.shape[-1])
     out = lax.all_to_all(out, ("dp", "tensor"), 0, 0, tiled=True, axis_index_groups=same_core)
-    total = jnp.sum(out, 0)
-    width = total.shape[-1]
-    total = total.reshape(n * m, width)
-    rows, i = [], 0
-    while i < examples:
-        owner = min(i // m, n - 1)
-        begin = min(owner * m, examples - m)
-        stop = begin + m
-        rows.append(total[owner * m + i - begin : owner * m + stop - begin])
-        i = stop
-    scale = (1.0 / math.sqrt(SEQ)) * (1.0 / math.sqrt(R * R)) / (TOP * TOP)
-    return jnp.concatenate(rows, 0)[:examples] * scale
+    return unpack(out, (1.0 / math.sqrt(SEQ)) * (1.0 / math.sqrt(R * R)) / (TOP * TOP) / TOP)
 
 
 def solution(mesh):

time: 55.2 us -> 53.7 us (0.973)
  blocking collectives: 12.9 us -> 11.3 us
  Pallas kernels: 19.1 us -> 20.1 us
  other arithmetic: 1.69 us -> 0.98 us
    all_to_all x1, blocking collectives: 12.9 us -> 11.3 us  [local(): lax.all_to_all(out, ('dp', 'tensor'), 0, 0, tiled=True, axis_index_groups...]
    pallas_call x0 -> x2, Pallas kernels: none -> 0.92 us  [the longest x1 0.76 us: unpack(): pl.pallas_call(functools.partial(unpack_kernel, examples, scale), in_spec...]
    mul x1 -> x0, other arithmetic: 0.62 us -> none  [local(): return jnp.concatenate(rows, 0)[:examples] * scale]
  transfers between devices with their start and end apart: 13 -> 13, of which waited for: 5 -> 5; matrix products, arithmetic and copies ran while one was open for 2% -> 2% of each run, Pallas kernels for 31% -> 32%
where the time goes in v5:
time: 53.7 us; the launch traced here: 53.5 us
  Pallas kernels  20.1 us (37%)
  starting transfers between devices  14.3 us (27%)
  blocking collectives  11.3 us (21%)
  waiting for transfers between devices  6.65 us (12%)
  other arithmetic  0.98 us (2%)
    pallas_call x3, Pallas kernels, project(): pl.pallas_call(functools.partial(project_kernel, masks), grid=(len(masks)...  15.9 us
    all_to_all x1, blocking collectives, local(): lax.all_to_all(out, ('dp', 'tensor'), 0, 0, tiled=True, axis_index_groups...  11.3 us
    ppermute x6, starting transfers between devices, along(): return lax.ppermute(v, 'tensor', [(i, i ^ mask) for i in range(n)])  8.62 us
    ppermute x7, starting transfers between devices, flip(): return lax.ppermute(v, 'dp', [(i, i ^ mask) for i in range(n)])  5.72 us
    ppermute x6, waiting for transfers between devices, along(): return lax.ppermute(v, 'tensor', [(i, i ^ mask) for i in range(n)])  4.27 us
    ppermute x7, waiting for transfers between devices, flip(): return lax.ppermute(v, 'dp', [(i, i ^ mask) for i in range(n)])  2.37 us
    pallas_call x1, Pallas kernels, scores_of(): pl.pallas_call(functools.partial(scores_kernel, n, m, masks), in_specs=[p...  1.83 us
  transfers between devices with their start and end apart: 13, of which 5 were waited for; matrix products, arithmetic and copies ran while one was open for 2% of the time, Pallas kernels for 32%

profile of v5, /device:TPU:0, one launch (start us, length us, event | category | flops | bytes accessed | tf_op | source)
XLA Modules:
  0.0 53.5 jit_solution(5102674308964327405)
XLA Ops:
  0.0 2.9 %collective-permute-start.3 = (bf16[384,1024]{1,0:T(8,128)(2,1)}, bf16[384,1024]{1,0:T(8,128)(2,1)S(1)}, u32[]{:S(2)}, u32[]{:S(2)}) collective-permute-start(bf16[384,1024]{1,0:T(8,128)(2,1)} %refs_0_), channel_id=1, source_target_pairs={{0,8},{4,12},{8,0},{12,4},{1,9},{5,13},{9,1},{13,5},{2,10},{6,14},... | collective-permute-start | bytes 2359304 | tf_op jit(solution)/shard_map/ppermute | solution.py:284
  2.9 6.4 %shard_map.64 = (bf16[528,128]{1,0:T(8,128)(2,1)}, bf16[528,128]{1,0:T(8,128)(2,1)}) custom-call(bf16[1920,3584]{1,0:T(8,128)(2,1)} %acts.5, bf16[1920,1024]{1,0:T(8,128)(2,1)} %outs.3, bf16[64,3584]{1,0:T(8,128)(2,1)} %p_in.5, bf16[64,1024]{1,0:T(8,128)(2,1)} %p_out.5), custom_call_target="tpu_custom_call" | custom-call | flops 1 | bytes 1 | tf_op jit(solution)/shard_map/pallas_call | solution.py:90
  9.3 2.6 %collective-permute-start = (bf16[528,128]{1,0:T(8,128)(2,1)}, bf16[528,128]{1,0:T(8,128)(2,1)S(1)}, u32[]{:S(2)}, u32[]{:S(2)}) collective-permute-start(bf16[528,128]{1,0:T(8,128)(2,1)} %get-tuple-element.16), channel_id=1, source_target_pairs={{0,2},{1,3},{2,0},{3,1},{4,6},{5,7},{6,4},{7,5},{8,10},{9,11},{10,... | collective-permute-start | bytes 405512 | tf_op jit(solution)/shard_map/ppermute | solution.py:281
  11.9 1.4 %collective-permute-start.1 = (bf16[528,128]{1,0:T(8,128)(2,1)}, bf16[528,128]{1,0:T(8,128)(2,1)S(1)}, u32[]{:S(2)}, u32[]{:S(2)}) collective-permute-start(bf16[528,128]{1,0:T(8,128)(2,1)} %get-tuple-element.17), channel_id=1, source_target_pairs={{0,3},{1,2},{2,1},{3,0},{4,7},{5,6},{6,5},{7,4},{8,11},{9,10},{10,... | collective-permute-start | bytes 405512 | tf_op jit(solution)/shard_map/ppermute | solution.py:281
  13.3 4.7 %shard_map.65 = bf16[528,128]{1,0:T(8,128)(2,1)} custom-call(bf16[1920,3584]{1,0:T(8,128)(2,1)} %acts.5, bf16[1920,1024]{1,0:T(8,128)(2,1)} %outs.3, bf16[64,3584]{1,0:T(8,128)(2,1)} %p_in.5, bf16[64,1024]{1,0:T(8,128)(2,1)} %p_out.5), custom_call_target="tpu_custom_call" | custom-call | flops 1 | bytes 1 | tf_op jit(solution)/shard_map/pallas_call | solution.py:90
  18.0 0.2 collective-permute-start.2
  18.2 4.8 %shard_map.66 = f32[512,128]{1,0:T(8,128)} custom-call(bf16[1920,3584]{1,0:T(8,128)(2,1)} %acts.5, bf16[1920,1024]{1,0:T(8,128)(2,1)} %outs.3, bf16[64,3584]{1,0:T(8,128)(2,1)} %p_in.5, bf16[64,1024]{1,0:T(8,128)(2,1)} %p_out.5), custom_call_target="tpu_custom_call" | custom-call | flops 1 | bytes 1 | tf_op jit(solution)/shard_map/pallas_call | solution.py:90
  23.0 1.0 %broadcast_multiply_fusion.own = f32[512,128]{1,0:T(8,128)S(1)} fusion(f32[512,128]{1,0:T(8,128)} %shard_map.66), kind=kLoop, calls=%fused_computation.1 | loop fusion | flops 65536 | bytes 524288 | tf_op jit(solution)/shard_map/mul | solution.py:297
  24.0 0.2 collective-permute-done.2.refs_2_
  24.2 0.0 collective-permute-done.refs_0_
  24.2 0.0 collective-permute-done.1.refs_1_
  24.2 0.9 %shard_map.67.refs_0_ = bf16[4,36,128]{2,1,0:T(8,128)(2,1)S(1)} custom-call(f32[512,128]{1,0:T(8,128)S(1)} %broadcast_multiply_fusion.own, bf16[528,128]{1,0:T(8,128)(2,1)S(1)} %collective-permute-done.refs_0_, bf16[528,128]{1,0:T(8,128)(2,1)S(1)} %collective-permute-done.1.refs_1_, bf16[528,128]{1,0:T(8,128)(2,1)S(1)} %collective-permute-done.2.refs_2_), custom_call_target="tpu_custom_call" | custom-call | flops 1 | bytes 1 | tf_op jit(solution)/shard_map/pallas_call | solution.py:142
  25.1 0.0 collective-permute-done.3.refs_1_.refs_2_
  25.1 0.1 collective-permute-start.4
  25.2 0.5 collective-permute-start.5
  25.7 0.5 collective-permute-start.6
  26.2 0.9 %collective-permute-start.8 = (bf16[36,128]{1,0:T(8,128)(2,1)S(1)}, bf16[36,128]{1,0:T(8,128)(2,1)S(1)}, u32[]{:S(2)}, u32[]{:S(2)}) collective-permute-start(bf16[36,128]{1,0:T(8,128)(2,1)S(1)} %get-tuple-element.28), channel_id=1, source_target_pairs={{0,12},{4,8},{8,4},{12,0},{1,13},{5,9},{9,5},{13,1},{2,14},{6,10},... | collective-permute-start | bytes 27656 | tf_op jit(solution)/shard_map/ppermute | solution.py:284
  27.1 0.7 %collective-permute-start.7 = (bf16[36,128]{1,0:T(8,128)(2,1)S(1)}, bf16[36,128]{1,0:T(8,128)(2,1)S(1)}, u32[]{:S(2)}, u32[]{:S(2)}) collective-permute-start(bf16[36,128]{1,0:T(8,128)(2,1)S(1)} %get-tuple-element.29), channel_id=1, source_target_pairs={{0,4},{4,0},{8,12},{12,8},{1,5},{5,1},{9,13},{13,9},{2,6},{6,2},{1... | collective-permute-start | bytes 27656 | tf_op jit(solution)/shard_map/ppermute | solution.py:284
  27.8 0.6 %shard_map.68 = (bf16[1024,1024]{1,0:T(8,128)(2,1)S(1)}, bf16[1024,1024]{1,0:T(8,128)(2,1)S(1)}) custom-call(f32[1024,1024]{1,0:T(8,128)S(1)} %copy-done, bf16[4,36,128]{2,1,0:T(8,128)(2,1)S(1)} %shard_map.67.refs_0_, bf16[384,1024]{1,0:T(8,128)(2,1)S(1)} %collective-permute-done.3.refs_1_.refs_2_), custom_call_target="tpu_custom_call" | custom-call | flops 1 | bytes 1 | tf_op jit(solution)/shard_map/pallas_call | solution.py:163
  28.4 0.9 %collective-permute-done.6 = bf16[36,128]{1,0:T(8,128)(2,1)S(1)} collective-permute-done((bf16[36,128]{1,0:T(8,128)(2,1)S(1)}, bf16[36,128]{1,0:T(8,128)(2,1)S(1)}, u32[]{:S(2)}, u32[]{:S(2)}) %collective-permute-start.6) | collective-permute-done | bytes 9248 | tf_op jit(solution)/shard_map/ppermute | solution.py:284
  29.4 0.0 collective-permute-done.8
  29.4 0.0 collective-permute-done.7
  29.4 3.6 %collective-permute-start.11 = (bf16[4,36,128]{2,1,0:T(8,128)(2,1)S(1)}, bf16[4,36,128]{2,1,0:T(8,128)(2,1)S(1)}, u32[]{:S(2)}, u32[]{:S(2)}) collective-permute-start(bf16[4,36,128]{2,1,0:T(8,128)(2,1)S(1)} %pad_maximum_fusion.refs_4_), channel_id=1, source_target_pairs={{0,3},{1,2},{2,1},{3,0},{4,7},{5,6},{6,5},{7,4},{8,11},{9,10},{10,... | collective-permute-start | bytes 110600 | tf_op jit(solution)/shard_map/ppermute | solution.py:281
  33.0 0.8 %collective-permute-start.9 = (bf16[4,36,128]{2,1,0:T(8,128)(2,1)S(1)}, bf16[4,36,128]{2,1,0:T(8,128)(2,1)S(1)}, u32[]{:S(2)}, u32[]{:S(2)}) collective-permute-start(bf16[4,36,128]{2,1,0:T(8,128)(2,1)S(1)} %pad_maximum_fusion.refs_4_), channel_id=1, source_target_pairs={{0,1},{1,0},{2,3},{3,2},{4,5},{5,4},{6,7},{7,6},{8,9},{9,8},{10,11... | collective-permute-start | bytes 110600 | tf_op jit(solution)/shard_map/ppermute | solution.py:281
  33.9 1.4 %collective-permute-done.11.refs_7_ = bf16[4,36,128]{2,1,0:T(8,128)(2,1)S(1)} collective-permute-done((bf16[4,36,128]{2,1,0:T(8,128)(2,1)S(1)}, bf16[4,36,128]{2,1,0:T(8,128)(2,1)S(1)}, u32[]{:S(2)}, u32[]{:S(2)}) %collective-permute-start.11) | collective-permute-done | bytes 36896 | tf_op jit(solution)/shard_map/ppermute | solution.py:281
  35.3 2.6 %collective-permute-done.10.refs_6_ = bf16[4,36,128]{2,1,0:T(8,128)(2,1)S(1)} collective-permute-done((bf16[4,36,128]{2,1,0:T(8,128)(2,1)S(1)}, bf16[4,36,128]{2,1,0:T(8,128)(2,1)S(1)}, u32[]{:S(2)}, u32[]{:S(2)}) %collective-permute-start.10) | collective-permute-done | bytes 36896 | tf_op jit(solution)/shard_map/ppermute | solution.py:281
  37.9 1.8 %shard_map.69.ours = f32[2,2,4,4,4,384]{5,4,3,2,1,0:T(4,128)S(1)} custom-call(bf16[1024,1024]{1,0:T(8,128)(2,1)S(1)} %get-tuple-element.22.h_hi, bf16[1024,1024]{1,0:T(8,128)(2,1)S(1)} %get-tuple-element.23.h_lo, bf16[384,1024]{1,0:T(8,128)(2,1)S(1)} %copy-done.1, bf16[384,1024]{1,0:T(8,128)(2,1)S(1)} %collective-permute-done.4.refs_1_, ...), custom_call_target="tpu_custom_call" | custom-call | tf_op jit(solution)/shard_map/pallas_call | solution.py:206
  39.8 0.1 collective-permute-start.12
  39.9 1.4 %collective-permute-done.12.theirs = f32[2,4,4,4,384]{4,3,2,1,0:T(4,128)S(1)} collective-permute-done((f32[2,4,4,4,384]{4,3,2,1,0:T(4,128)S(1)}, f32[2,4,4,4,384]{4,3,2,1,0:T(4,128)S(1)}, u32[]{:S(2)}, u32[]{:S(2)}) %collective-permute-start.12) | collective-permute-done | bytes 196640 | tf_op jit(solution)/shard_map/ppermute | solution.py:284
  41.3 0.2 shard_map.70
  41.5 11.3 %all_to_all.5.y_ref = bf16[8,16,384]{2,1,0:T(8,128)(2,1)S(1)} all-to-all(bf16[8,16,384]{2,1,0:T(8,128)(2,1)S(1)} %shard_map.70), channel_id=1, replica_groups={{0,1,2,3,8,9,10,11},{4,5,6,7,12,13,14,15},{16,17,18,19,24,25,26,27},{20..., dimensions={0} | all-to-all | bytes 196608 | tf_op jit(solution)/shard_map/all_to_all | solution.py:310
  52.7 0.8 %shard_map.71 = f32[15,384]{1,0:T(8,128)} custom-call(bf16[8,16,384]{2,1,0:T(8,128)(2,1)S(1)} %all_to_all.5.y_ref), custom_call_target="tpu_custom_call" | custom-call | tf_op jit(solution)/shard_map/pallas_call | solution.py:267
  (11 shorter events, 0.1 us)
Async XLA Ops:
  0.0 25.1 %collective-permute-start.3 = (bf16[384,1024]{1,0:T(8,128)(2,1)}, bf16[384,1024]{1,0:T(8,128)(2,1)S(1)}, u32[]{:S(2)}, u32[]{:S(2)}) collective-permute-start(bf16[384,1024]{1,0:T(8,128)(2,1)} %refs_0_), channel_id=1, source_target_pairs={{0,8},{4,12},{8,0},{12,4},{1,9},{5,13},{9,1},{13,5},{2,10},{6,14},... | collective-permute-start | bytes 2359304 | tf_op jit(solution)/shard_map/ppermute | solution.py:284
  9.3 14.8 %collective-permute-start = (bf16[528,128]{1,0:T(8,128)(2,1)}, bf16[528,128]{1,0:T(8,128)(2,1)S(1)}, u32[]{:S(2)}, u32[]{:S(2)}) collective-permute-start(bf16[528,128]{1,0:T(8,128)(2,1)} %get-tuple-element.16), channel_id=1, source_target_pairs={{0,2},{1,3},{2,0},{3,1},{4,6},{5,7},{6,4},{7,5},{8,10},{9,11},{10,... | collective-permute-start | bytes 405512 | tf_op jit(solution)/shard_map/ppermute | solution.py:281
  11.9 12.3 %collective-permute-start.1 = (bf16[528,128]{1,0:T(8,128)(2,1)}, bf16[528,128]{1,0:T(8,128)(2,1)S(1)}, u32[]{:S(2)}, u32[]{:S(2)}) collective-permute-start(bf16[528,128]{1,0:T(8,128)(2,1)} %get-tuple-element.17), channel_id=1, source_target_pairs={{0,3},{1,2},{2,1},{3,0},{4,7},{5,6},{6,5},{7,4},{8,11},{9,10},{10,... | collective-permute-start | bytes 405512 | tf_op jit(solution)/shard_map/ppermute | solution.py:281
  18.0 7.1 %copy-start.1 = (bf16[384,1024]{1,0:T(8,128)(2,1)S(1)}, bf16[384,1024]{1,0:T(8,128)(2,1)}, u32[]{:S(2)}) copy-start(bf16[384,1024]{1,0:T(8,128)(2,1)} %refs_0_) | copy-start | bytes 2359300
  18.0 6.2 %collective-permute-start.2 = (bf16[528,128]{1,0:T(8,128)(2,1)}, bf16[528,128]{1,0:T(8,128)(2,1)S(1)}, u32[]{:S(2)}, u32[]{:S(2)}) collective-permute-start(bf16[528,128]{1,0:T(8,128)(2,1)} %shard_map.65), channel_id=1, source_target_pairs={{0,1},{1,0},{2,3},{3,2},{4,5},{5,4},{6,7},{7,6},{8,9},{9,8},{10,11... | collective-permute-start | bytes 405512 | tf_op jit(solution)/shard_map/ppermute | solution.py:281
  18.2 9.6 %copy-start = (f32[1024,1024]{1,0:T(8,128)S(1)}, f32[1024,1024]{1,0:T(8,128)}, u32[]{:S(2)}) copy-start(f32[1024,1024]{1,0:T(8,128)} %h.1) | copy-start | bytes 12582916
  25.1 12.8 %collective-permute-start.4 = (bf16[384,1024]{1,0:T(8,128)(2,1)S(1)}, bf16[384,1024]{1,0:T(8,128)(2,1)S(1)}, u32[]{:S(2)}, u32[]{:S(2)}) collective-permute-start(bf16[384,1024]{1,0:T(8,128)(2,1)S(1)} %copy-done.1), channel_id=1, source_target_pairs={{0,4},{4,0},{8,12},{12,8},{1,5},{5,1},{9,13},{13,9},{2,6},{6,2},{1... | collective-permute-start | bytes 2359304 | tf_op jit(solution)/shard_map/ppermute | solution.py:284
  25.2 12.7 %collective-permute-start.5 = (bf16[384,1024]{1,0:T(8,128)(2,1)S(1)}, bf16[384,1024]{1,0:T(8,128)(2,1)S(1)}, u32[]{:S(2)}, u32[]{:S(2)}) collective-permute-start(bf16[384,1024]{1,0:T(8,128)(2,1)S(1)} %collective-permute-done.3.refs_1_.refs_2_), channel_id=1, source_target_pairs={{0,4},{4,0},{8,12},{12,8},{1,5},{5,1},{9,13},{13,9},{2,6},{6,2},{1... | collective-permute-start | bytes 2359304 | tf_op jit(solution)/shard_map/ppermute | solution.py:284
  25.7 3.7 %collective-permute-start.6 = (bf16[36,128]{1,0:T(8,128)(2,1)S(1)}, bf16[36,128]{1,0:T(8,128)(2,1)S(1)}, u32[]{:S(2)}, u32[]{:S(2)}) collective-permute-start(bf16[36,128]{1,0:T(8,128)(2,1)S(1)} %get-tuple-element.27), channel_id=1, source_target_pairs={{0,8},{4,12},{8,0},{12,4},{1,9},{5,13},{9,1},{13,5},{2,10},{6,14},... | collective-permute-start | bytes 27656 | tf_op jit(solution)/shard_map/ppermute | solution.py:284
  26.2 3.2 %collective-permute-start.8 = (bf16[36,128]{1,0:T(8,128)(2,1)S(1)}, bf16[36,128]{1,0:T(8,128)(2,1)S(1)}, u32[]{:S(2)}, u32[]{:S(2)}) collective-permute-start(bf16[36,128]{1,0:T(8,128)(2,1)S(1)} %get-tuple-element.28), channel_id=1, source_target_pairs={{0,12},{4,8},{8,4},{12,0},{1,13},{5,9},{9,5},{13,1},{2,14},{6,10},... | collective-permute-start | bytes 27656 | tf_op jit(solution)/shard_map/ppermute | solution.py:284
  27.1 2.3 %collective-permute-start.7 = (bf16[36,128]{1,0:T(8,128)(2,1)S(1)}, bf16[36,128]{1,0:T(8,128)(2,1)S(1)}, u32[]{:S(2)}, u32[]{:S(2)}) collective-permute-start(bf16[36,128]{1,0:T(8,128)(2,1)S(1)} %get-tuple-element.29), channel_id=1, source_target_pairs={{0,4},{4,0},{8,12},{12,8},{1,5},{5,1},{9,13},{13,9},{2,6},{6,2},{1... | collective-permute-start | bytes 27656 | tf_op jit(solution)/shard_map/ppermute | solution.py:284
  29.4 5.9 %collective-permute-start.11 = (bf16[4,36,128]{2,1,0:T(8,128)(2,1)S(1)}, bf16[4,36,128]{2,1,0:T(8,128)(2,1)S(1)}, u32[]{:S(2)}, u32[]{:S(2)}) collective-permute-start(bf16[4,36,128]{2,1,0:T(8,128)(2,1)S(1)} %pad_maximum_fusion.refs_4_), channel_id=1, source_target_pairs={{0,3},{1,2},{2,1},{3,0},{4,7},{5,6},{6,5},{7,4},{8,11},{9,10},{10,... | collective-permute-start | bytes 110600 | tf_op jit(solution)/shard_map/ppermute | solution.py:281
  33.0 4.9 %collective-permute-start.10 = (bf16[4,36,128]{2,1,0:T(8,128)(2,1)S(1)}, bf16[4,36,128]{2,1,0:T(8,128)(2,1)S(1)}, u32[]{:S(2)}, u32[]{:S(2)}) collective-permute-start(bf16[4,36,128]{2,1,0:T(8,128)(2,1)S(1)} %pad_maximum_fusion.refs_4_), channel_id=1, source_target_pairs={{0,2},{1,3},{2,0},{3,1},{4,6},{5,7},{6,4},{7,5},{8,10},{9,11},{10,... | collective-permute-start | bytes 110600 | tf_op jit(solution)/shard_map/ppermute | solution.py:281
  33.0 4.9 %collective-permute-start.9 = (bf16[4,36,128]{2,1,0:T(8,128)(2,1)S(1)}, bf16[4,36,128]{2,1,0:T(8,128)(2,1)S(1)}, u32[]{:S(2)}, u32[]{:S(2)}) collective-permute-start(bf16[4,36,128]{2,1,0:T(8,128)(2,1)S(1)} %pad_maximum_fusion.refs_4_), channel_id=1, source_target_pairs={{0,1},{1,0},{2,3},{3,2},{4,5},{5,4},{6,7},{7,6},{8,9},{9,8},{10,11... | collective-permute-start | bytes 110600 | tf_op jit(solution)/shard_map/ppermute | solution.py:281
  39.8 1.5 %collective-permute-start.12 = (f32[2,4,4,4,384]{4,3,2,1,0:T(4,128)S(1)}, f32[2,4,4,4,384]{4,3,2,1,0:T(4,128)S(1)}, u32[]{:S(2)}, u32[]{:S(2)}) collective-permute-start(f32[2,4,4,4,384]{4,3,2,1,0:T(4,128)S(1)} %slice_bitcast_fusion), channel_id=1, source_target_pairs={{0,4},{4,0},{8,12},{12,8},{1,5},{5,1},{9,13},{13,9},{2,6},{6,2},{1... | collective-permute-start | bytes 589832 | tf_op jit(solution)/shard_map/ppermute | solution.py:284

commit v6 on v5

--- a/solution.py
+++ b/solution.py
@@ -109,7 +109,7 @@
     return hi, (v - hi.astype(jnp.float32)).astype(jnp.bfloat16)
 
 
-def grads_kernel(n, m, bits, own, *refs):
+def grads_kernel(n, m, own, *refs):
     coded, out, z, block = refs[: n - 1], *refs[-3:]
     rows = m * SEQ
     x = own[...]
@@ -117,7 +117,6 @@
         y = ref[...].astype(jnp.float32)
         x = x + root(y[:rows]) * y[rows : rows + 1]
     half = R // n // 2
-    d = lax.axis_index("dp")
     contract = (((1,), (0,)), ((), ()))
     for e in range(m):
         xe = x[e * SEQ : (e + 1) * SEQ, :]
@@ -134,20 +133,22 @@
             top = column_top(g)
             block[pl.ds(e, half, stride=m), :] = power(g, top)
             block[pl.ds(half * m + e, 1), :] = top
-        out[bitrev(lax.bitwise_xor(d, j), bits)] = block[...].astype(jnp.bfloat16)
-
-
-def grads_of(own, coded, n, m, bits):
+        y = block[...].astype(jnp.bfloat16)
+        for t in range(n):
+            out[j * n + t] = y
+
+
+def grads_of(own, coded, wait_for, n, m):
     rows = (R // n // 2 + 1) * m
     return pl.pallas_call(
-        functools.partial(grads_kernel, n, m, bits),
-        in_specs=[pl.BlockSpec(memory_space=pltpu.VMEM)] * n,
+        functools.partial(grads_kernel, n, m),
+        in_specs=[pl.BlockSpec(memory_space=pltpu.VMEM)] * n + [pl.BlockSpec(memory_space=pl.ANY)] * len(wait_for),
         out_specs=pl.BlockSpec(memory_space=pltpu.VMEM),
-        out_shape=jax.ShapeDtypeStruct((n, rows, LANES), jnp.bfloat16),
+        out_shape=jax.ShapeDtypeStruct((n * n, rows, LANES), jnp.bfloat16),
         scratch_shapes=[pltpu.VMEM((m, SEQ, LANES), jnp.float32), pltpu.VMEM((rows, LANES), jnp.float32)],
         compiler_params=params(24),
         cost_estimate=pl.CostEstimate(flops=1, bytes_accessed=1, transcendentals=0),
-    )(own, *coded)
+    )(own, *coded, *wait_for)
 
 
 def halves_kernel(h, *refs):
@@ -172,11 +173,11 @@
 
 
 def scores_kernel(n, m, masks, h_hi, h_lo, *refs):
-    queries, grads, out, a = refs[:n], refs[n : 2 * n], refs[2 * n], refs[2 * n + 1]
+    grads, queries, out, a = refs[0], refs[1 : n + 1], refs[n + 1], refs[n + 2]
     half = R // n // 2
     rows = n * n * m
     for s in range(n * n):
-        y = grads[s // n][s % n].astype(jnp.float32)
+        y = grads[s].astype(jnp.float32)
         top = y[half * m :]
         w = root(y[: half * m]) * (1.0 / TOP)
         for r in range(half):
@@ -187,7 +188,7 @@
     low = lax.dot_general(hi, h_lo[...], contract, preferred_element_type=jnp.float32)
     hi, lo = split(top[:rows] + top[rows:] + low)
     both = jnp.concatenate([hi, lo], 0)
-    d, t = lax.axis_index("dp"), lax.axis_index("tensor")
+    d = lax.axis_index("dp")
     for mask, ref in zip(masks, queries):
         to = lax.bitwise_xor(d, mask)
         s = lax.dot_general(both, ref[...], ROWS_CONTRACT, preferred_element_type=jnp.float32)
@@ -195,8 +196,7 @@
         for p in range(n):
             for b in range(n):
                 at = (p * n + b) * m
-                back = bitrev(b, n.bit_length() - 1)
-                out[back & 1, lax.bitwise_xor(d >> 1, back >> 1), to, lax.bitwise_xor(t, p)] = s[at : at + m]
+                out[lax.bitwise_xor(d, p) & 1, p >> 1, to, b] = s[at : at + m]
 
 
 def scores_of(h_hi, h_lo, queries, grads, n, m):
@@ -205,12 +205,12 @@
     width = blocks[0].shape[0]
     return pl.pallas_call(
         functools.partial(scores_kernel, n, m, masks),
-        in_specs=[pl.BlockSpec(memory_space=pltpu.VMEM)] * (2 + 2 * n),
+        in_specs=[pl.BlockSpec(memory_space=pltpu.VMEM)] * (3 + n),
         out_specs=pl.BlockSpec(memory_space=pltpu.VMEM),
         out_shape=jax.ShapeDtypeStruct((2, n // 2, n, n, m, width), jnp.float32),
         scratch_shapes=[pltpu.VMEM((n * n * m, R // n // 2 * LANES), jnp.float32)],
         compiler_params=params(40),
-    )(h_hi, h_lo, *blocks, *grads)
+    )(h_hi, h_lo, grads, *blocks)
 
 
 def each(count, body):
@@ -294,17 +294,14 @@
     (near,) = project(activations, after(out_grads, y), proj_in, proj_out, [1], m, 59)
     (own,) = project(activations, after(out_grads, near), proj_in, proj_out, [0], m, 57)
     coded = [along(v, mask) for v, mask in zip(y, far)] + [along(near, 1)]
-    grads = grads_of(own * TOP, coded, n, m, bits)
-    h_hi, h_lo = halves(hess_inv, [grads, all_q[n // 2]])
-    parts = [flip(grads[p], bitrev(p, bits)) for p in range(1, n)]
-    first, h_hi, h_lo = lax.optimization_barrier((grads[0], h_hi, h_lo))
-    group = jnp.stack([first] + parts)
-    groups = [group] + [along(group, s) for s in range(1, n)]
+    h_hi, h_lo = halves(hess_inv, [own])
+    grads = grads_of(own * TOP, coded, [h_hi, all_q[n // 2]], n, m)
     for b in reversed(range(bits - 1)):
         all_q = dict(zip(all_q, after(tuple(all_q.values()), grads)))
         all_q.update({k | (1 << b): flip(v, 1 << b) for k, v in all_q.items()})
 
-    out = scores_of(h_hi, h_lo, all_q, groups, n, m)
+    grads_all = lax.all_to_all(grads, ("dp", "tensor"), 0, 0, tiled=True)
+    out = scores_of(h_hi, h_lo, all_q, grads_all, n, m)
     out = pack(out, flip(out[1], 1), n, m, examples)
     same_core = [[(2 * x + core) * n + t for x in range(n // 2) for t in range(n)] for core in range(2)]
     out = lax.all_to_all(out, ("dp", "tensor"), 0, 0, tiled=True, axis_index_groups=same_core)

time: 53.7 us -> 53.2 us (level)
  blocking collectives: 11.3 us -> 22.5 us
  starting transfers between devices: 14.3 us -> 7.97 us
  waiting for transfers between devices: 6.65 us -> 1.23 us
  other arithmetic: 0.98 us -> 0.02 us
  local copies, waits for them, and re-layouts: 0.03 us -> 0.98 us
    all_to_all x0 -> x1, blocking collectives: none -> 11.9 us  [local(): grads_all = lax.all_to_all(grads, ('dp', 'tensor'), 0, 0, tiled=True)]
    ppermute x6 -> x3, starting transfers between devices: 8.62 us -> 4.17 us  [along(): return lax.ppermute(v, 'tensor', [(i, i ^ mask) for i in range(n)])]
    ppermute x6 -> x3, waiting for transfers between devices: 4.27 us -> 0.01 us  [along(): return lax.ppermute(v, 'tensor', [(i, i ^ mask) for i in range(n)])]
    ppermute x7 -> x4, starting transfers between devices: 5.72 us -> 3.8 us  [flip(): return lax.ppermute(v, 'dp', [(i, i ^ mask) for i in range(n)])]
    ppermute x7 -> x4, waiting for transfers between devices: 2.37 us -> 1.22 us  [flip(): return lax.ppermute(v, 'dp', [(i, i ^ mask) for i in range(n)])]
    unnamed x4 -> x6, local copies, waits for them, and re-layouts: 0.01 us -> 0.96 us
    mul x1, other arithmetic: 0.97 us -> 0.02 us  [local(): grads = grads_of(own * TOP, coded, [h_hi, all_q[n // 2]], n, m)]
    all_to_all x1, blocking collectives: 11.3 us -> 10.6 us  [local(): lax.all_to_all(out, ('dp', 'tensor'), 0, 0, tiled=True, axis_index_groups...]
  transfers between devices with their start and end apart: 13 -> 7, of which waited for: 5 -> 1; matrix products, arithmetic and copies ran while one was open for 2% -> 0% of each run, Pallas kernels for 32% -> 31%
where the time goes in v6:
time: 53.2 us; the launch traced here: 53 us
  blocking collectives  22.5 us (42%)
  Pallas kernels  20.2 us (38%)
  starting transfers between devices  7.97 us (15%)
  waiting for transfers between devices  1.23 us (2%)
  local copies, waits for them, and re-layouts  0.98 us (2%)
    pallas_call x3, Pallas kernels, project(): pl.pallas_call(functools.partial(project_kernel, masks), grid=(len(masks)...  15.9 us
    all_to_all x1, blocking collectives, local(): grads_all = lax.all_to_all(grads, ('dp', 'tensor'), 0, 0, tiled=True)  11.9 us
    all_to_all x1, blocking collectives, local(): lax.all_to_all(out, ('dp', 'tensor'), 0, 0, tiled=True, axis_index_groups...  10.6 us
    ppermute x3, starting transfers between devices, along(): return lax.ppermute(v, 'tensor', [(i, i ^ mask) for i in range(n)])  4.17 us
    ppermute x4, starting transfers between devices, flip(): return lax.ppermute(v, 'dp', [(i, i ^ mask) for i in range(n)])  3.8 us
    pallas_call x1, Pallas kernels, scores_of(): pl.pallas_call(functools.partial(scores_kernel, n, m, masks), in_specs=[p...  1.84 us
    ppermute x4, waiting for transfers between devices, flip(): return lax.ppermute(v, 'dp', [(i, i ^ mask) for i in range(n)])  1.22 us
  transfers between devices with their start and end apart: 7, of which 1 were waited for; matrix products, arithmetic and copies ran while one was open for 0% of the time, Pallas kernels for 31%

profile of v6, /device:TPU:0, one launch (start us, length us, event | category | flops | bytes accessed | tf_op | source)
XLA Modules:
  0.0 53.0 jit_solution(12038893910606922272)
XLA Ops:
  0.0 2.9 %collective-permute-start.3 = (bf16[384,1024]{1,0:T(8,128)(2,1)}, bf16[384,1024]{1,0:T(8,128)(2,1)S(1)}, u32[]{:S(2)}, u32[]{:S(2)}) collective-permute-start(bf16[384,1024]{1,0:T(8,128)(2,1)} %refs_1_), channel_id=1, source_target_pairs={{0,8},{4,12},{8,0},{12,4},{1,9},{5,13},{9,1},{13,5},{2,10},{6,14},... | collective-permute-start | bytes 2359304 | tf_op jit(solution)/shard_map/ppermute | solution.py:284
  2.9 6.4 %shard_map.64 = (bf16[528,128]{1,0:T(8,128)(2,1)}, bf16[528,128]{1,0:T(8,128)(2,1)}) custom-call(bf16[1920,3584]{1,0:T(8,128)(2,1)} %acts.5, bf16[1920,1024]{1,0:T(8,128)(2,1)} %outs.3, bf16[64,3584]{1,0:T(8,128)(2,1)} %p_in.5, bf16[64,1024]{1,0:T(8,128)(2,1)} %p_out.5), custom_call_target="tpu_custom_call" | custom-call | flops 1 | bytes 1 | tf_op jit(solution)/shard_map/pallas_call | solution.py:90
  9.3 2.6 %collective-permute-start = (bf16[528,128]{1,0:T(8,128)(2,1)}, bf16[528,128]{1,0:T(8,128)(2,1)S(1)}, u32[]{:S(2)}, u32[]{:S(2)}) collective-permute-start(bf16[528,128]{1,0:T(8,128)(2,1)} %get-tuple-element.13), channel_id=1, source_target_pairs={{0,2},{1,3},{2,0},{3,1},{4,6},{5,7},{6,4},{7,5},{8,10},{9,11},{10,... | collective-permute-start | bytes 405512 | tf_op jit(solution)/shard_map/ppermute | solution.py:281
  11.9 1.4 %collective-permute-start.1 = (bf16[528,128]{1,0:T(8,128)(2,1)}, bf16[528,128]{1,0:T(8,128)(2,1)S(1)}, u32[]{:S(2)}, u32[]{:S(2)}) collective-permute-start(bf16[528,128]{1,0:T(8,128)(2,1)} %get-tuple-element.14), channel_id=1, source_target_pairs={{0,3},{1,2},{2,1},{3,0},{4,7},{5,6},{6,5},{7,4},{8,11},{9,10},{10,... | collective-permute-start | bytes 405512 | tf_op jit(solution)/shard_map/ppermute | solution.py:281
  13.3 4.7 %shard_map.65 = bf16[528,128]{1,0:T(8,128)(2,1)} custom-call(bf16[1920,3584]{1,0:T(8,128)(2,1)} %acts.5, bf16[1920,1024]{1,0:T(8,128)(2,1)} %outs.3, bf16[64,3584]{1,0:T(8,128)(2,1)} %p_in.5, bf16[64,1024]{1,0:T(8,128)(2,1)} %p_out.5), custom_call_target="tpu_custom_call" | custom-call | flops 1 | bytes 1 | tf_op jit(solution)/shard_map/pallas_call | solution.py:90
  18.0 0.0 copy-start
  18.0 0.2 collective-permute-start.2
  18.2 4.8 %shard_map.66.refs_0_ = f32[512,128]{1,0:T(8,128)} custom-call(bf16[1920,3584]{1,0:T(8,128)(2,1)} %acts.5, bf16[1920,1024]{1,0:T(8,128)(2,1)} %outs.3, bf16[64,3584]{1,0:T(8,128)(2,1)} %p_in.5, bf16[64,1024]{1,0:T(8,128)(2,1)} %p_out.5), custom_call_target="tpu_custom_call" | custom-call | flops 1 | bytes 1 | tf_op jit(solution)/shard_map/pallas_call | solution.py:90
  23.0 0.0 copy-done
  23.0 0.0 copy-start.1
  23.0 0.9 %copy-done.1 = f32[512,128]{1,0:T(8,128)S(1)} copy-done((f32[512,128]{1,0:T(8,128)S(1)}, f32[512,128]{1,0:T(8,128)}, u32[]{:S(2)}) %copy-start.1) | copy-done | bytes 262168
  24.0 0.0 copy-start.2
  24.0 0.6 %shard_map.67 = (bf16[1024,1024]{1,0:T(8,128)(2,1)S(1)}, bf16[1024,1024]{1,0:T(8,128)(2,1)S(1)}) custom-call(f32[1024,1024]{1,0:T(8,128)S(1)} %copy-done, f32[512,128]{1,0:T(8,128)S(1)} %copy-done.1), custom_call_target="tpu_custom_call" | custom-call | flops 1 | bytes 1 | tf_op jit(solution)/shard_map/pallas_call | solution.py:164
  24.6 0.0 collective-permute-done.2.refs_2_
  24.6 0.0 collective-permute-done.refs_0_
  24.6 0.0 collective-permute-done.1.refs_1_
  24.6 0.0 collective-permute-done.3.refs_4_.refs_3_
  24.6 0.9 %shard_map.68 = bf16[16,36,128]{2,1,0:T(8,128)(2,1)S(1)} custom-call(f32[512,128]{1,0:T(8,128)S(1)} %broadcast_multiply_fusion.own, bf16[528,128]{1,0:T(8,128)(2,1)S(1)} %collective-permute-done.refs_0_, bf16[528,128]{1,0:T(8,128)(2,1)S(1)} %collective-permute-done.1.refs_1_, bf16[528,128]{1,0:T(8,128)(2,1)S(1)} %collective-permute-done.2.refs_2_, ...), custom_call_target="tpu_custom_call" | custom-call | flops 1 | bytes 1 | tf_op jit(solution)/shard_map/pallas_call | solution.py:143
  25.6 0.0 copy-done.2
  25.6 0.1 collective-permute-start.4
  25.7 0.5 collective-permute-start.5
  26.1 11.9 %all_to_all.10.refs_0_ = bf16[16,36,128]{2,1,0:T(8,128)(2,1)S(1)} all-to-all(bf16[16,36,128]{2,1,0:T(8,128)(2,1)S(1)} %shard_map.68), channel_id=1, replica_groups=mesh['groups'=2,'dp'=4,'tensor'=4] {'dp','tensor'}, dimensions={0} | all-to-all | bytes 294912 | tf_op jit(solution)/shard_map/all_to_all | solution.py:303
  38.0 0.0 collective-permute-done.4.refs_2_
  38.0 0.0 collective-permute-done.5.refs_4_
  38.0 1.8 %shard_map.69.ours = f32[2,2,4,4,4,384]{5,4,3,2,1,0:T(4,128)S(1)} custom-call(bf16[1024,1024]{1,0:T(8,128)(2,1)S(1)} %get-tuple-element.17.refs_3_.h_hi, bf16[1024,1024]{1,0:T(8,128)(2,1)S(1)} %get-tuple-element.18.h_lo, bf16[16,36,128]{2,1,0:T(8,128)(2,1)S(1)} %all_to_all.10.refs_0_, bf16[384,1024]{1,0:T(8,128)(2,1)S(1)} %copy-done.2, ...), custom_call_target="tpu_custom_call" | custom-call | tf_op jit(solution)/shard_map/pallas_call | solution.py:206
  39.9 0.3 collective-permute-start.6
  40.2 1.2 %collective-permute-done.6.theirs = f32[2,4,4,4,384]{4,3,2,1,0:T(4,128)S(1)} collective-permute-done((f32[2,4,4,4,384]{4,3,2,1,0:T(4,128)S(1)}, f32[2,4,4,4,384]{4,3,2,1,0:T(4,128)S(1)}, u32[]{:S(2)}, u32[]{:S(2)}) %collective-permute-start.6) | collective-permute-done | bytes 196640 | tf_op jit(solution)/shard_map/ppermute | solution.py:284
  41.4 0.2 shard_map.70
  41.6 10.6 %all_to_all.11.y_ref = bf16[8,16,384]{2,1,0:T(8,128)(2,1)S(1)} all-to-all(bf16[8,16,384]{2,1,0:T(8,128)(2,1)S(1)} %shard_map.70), channel_id=1, replica_groups={{0,1,2,3,8,9,10,11},{4,5,6,7,12,13,14,15},{16,17,18,19,24,25,26,27},{20..., dimensions={0} | all-to-all | bytes 196608 | tf_op jit(solution)/shard_map/all_to_all | solution.py:307
  52.2 0.8 %shard_map.71 = f32[15,384]{1,0:T(8,128)} custom-call(bf16[8,16,384]{2,1,0:T(8,128)(2,1)S(1)} %all_to_all.11.y_ref), custom_call_target="tpu_custom_call" | custom-call | tf_op jit(solution)/shard_map/pallas_call | solution.py:267
  (2 shorter events, 0.0 us)
Async XLA Ops:
  0.0 24.6 %collective-permute-start.3 = (bf16[384,1024]{1,0:T(8,128)(2,1)}, bf16[384,1024]{1,0:T(8,128)(2,1)S(1)}, u32[]{:S(2)}, u32[]{:S(2)}) collective-permute-start(bf16[384,1024]{1,0:T(8,128)(2,1)} %refs_1_), channel_id=1, source_target_pairs={{0,8},{4,12},{8,0},{12,4},{1,9},{5,13},{9,1},{13,5},{2,10},{6,14},... | collective-permute-start | bytes 2359304 | tf_op jit(solution)/shard_map/ppermute | solution.py:284
  9.3 15.3 %collective-permute-start = (bf16[528,128]{1,0:T(8,128)(2,1)}, bf16[528,128]{1,0:T(8,128)(2,1)S(1)}, u32[]{:S(2)}, u32[]{:S(2)}) collective-permute-start(bf16[528,128]{1,0:T(8,128)(2,1)} %get-tuple-element.13), channel_id=1, source_target_pairs={{0,2},{1,3},{2,0},{3,1},{4,6},{5,7},{6,4},{7,5},{8,10},{9,11},{10,... | collective-permute-start | bytes 405512 | tf_op jit(solution)/shard_map/ppermute | solution.py:281
  11.9 12.7 %collective-permute-start.1 = (bf16[528,128]{1,0:T(8,128)(2,1)}, bf16[528,128]{1,0:T(8,128)(2,1)S(1)}, u32[]{:S(2)}, u32[]{:S(2)}) collective-permute-start(bf16[528,128]{1,0:T(8,128)(2,1)} %get-tuple-element.14), channel_id=1, source_target_pairs={{0,3},{1,2},{2,1},{3,0},{4,7},{5,6},{6,5},{7,4},{8,11},{9,10},{10,... | collective-permute-start | bytes 405512 | tf_op jit(solution)/shard_map/ppermute | solution.py:281
  18.0 5.0 %copy-start = (f32[1024,1024]{1,0:T(8,128)S(1)}, f32[1024,1024]{1,0:T(8,128)}, u32[]{:S(2)}) copy-start(f32[1024,1024]{1,0:T(8,128)} %h.1) | copy-start | bytes 12582916
  18.0 6.6 %collective-permute-start.2 = (bf16[528,128]{1,0:T(8,128)(2,1)}, bf16[528,128]{1,0:T(8,128)(2,1)S(1)}, u32[]{:S(2)}, u32[]{:S(2)}) collective-permute-start(bf16[528,128]{1,0:T(8,128)(2,1)} %shard_map.65), channel_id=1, source_target_pairs={{0,1},{1,0},{2,3},{3,2},{4,5},{5,4},{6,7},{7,6},{8,9},{9,8},{10,11... | collective-permute-start | bytes 405512 | tf_op jit(solution)/shard_map/ppermute | solution.py:281
  23.0 1.0 %copy-start.1 = (f32[512,128]{1,0:T(8,128)S(1)}, f32[512,128]{1,0:T(8,128)}, u32[]{:S(2)}) copy-start(f32[512,128]{1,0:T(8,128)} %shard_map.66.refs_0_) | copy-start | bytes 786436
  24.0 1.6 %copy-start.2 = (bf16[384,1024]{1,0:T(8,128)(2,1)S(1)}, bf16[384,1024]{1,0:T(8,128)(2,1)}, u32[]{:S(2)}) copy-start(bf16[384,1024]{1,0:T(8,128)(2,1)} %refs_1_) | copy-start | bytes 2359300
  25.6 12.5 %collective-permute-start.4 = (bf16[384,1024]{1,0:T(8,128)(2,1)S(1)}, bf16[384,1024]{1,0:T(8,128)(2,1)S(1)}, u32[]{:S(2)}, u32[]{:S(2)}) collective-permute-start(bf16[384,1024]{1,0:T(8,128)(2,1)S(1)} %copy-done.2), channel_id=1, source_target_pairs={{0,4},{4,0},{8,12},{12,8},{1,5},{5,1},{9,13},{13,9},{2,6},{6,2},{1... | collective-permute-start | bytes 2359304 | tf_op jit(solution)/shard_map/ppermute | solution.py:284
  25.7 12.4 %collective-permute-start.5 = (bf16[384,1024]{1,0:T(8,128)(2,1)S(1)}, bf16[384,1024]{1,0:T(8,128)(2,1)S(1)}, u32[]{:S(2)}, u32[]{:S(2)}) collective-permute-start(bf16[384,1024]{1,0:T(8,128)(2,1)S(1)} %collective-permute-done.3.refs_4_.refs_3_), channel_id=1, source_target_pairs={{0,4},{4,0},{8,12},{12,8},{1,5},{5,1},{9,13},{13,9},{2,6},{6,2},{1... | collective-permute-start | bytes 2359304 | tf_op jit(solution)/shard_map/ppermute | solution.py:284
  39.9 1.5 %collective-permute-start.6 = (f32[2,4,4,4,384]{4,3,2,1,0:T(4,128)S(1)}, f32[2,4,4,4,384]{4,3,2,1,0:T(4,128)S(1)}, u32[]{:S(2)}, u32[]{:S(2)}) collective-permute-start(f32[2,4,4,4,384]{4,3,2,1,0:T(4,128)S(1)} %slice_bitcast_fusion), channel_id=1, source_target_pairs={{0,4},{4,0},{8,12},{12,8},{1,5},{5,1},{9,13},{13,9},{2,6},{6,2},{1... | collective-permute-start | bytes 589832 | tf_op jit(solution)/shard_map/ppermute | solution.py:284

commit v7 on v6

--- a/solution.py
+++ b/solution.py
@@ -172,7 +172,7 @@
     )(h, *wait_for)
 
 
-def scores_kernel(n, m, masks, h_hi, h_lo, *refs):
+def scores_kernel(n, m, examples, masks, h_hi, h_lo, *refs):
     grads, queries, out, a = refs[0], refs[1 : n + 1], refs[n + 1], refs[n + 2]
     half = R // n // 2
     rows = n * n * m
@@ -194,59 +194,30 @@
         s = lax.dot_general(both, ref[...], ROWS_CONTRACT, preferred_element_type=jnp.float32)
         s = s[:rows] + s[rows:]
         for p in range(n):
-            for b in range(n):
-                at = (p * n + b) * m
-                out[lax.bitwise_xor(d, p) & 1, p >> 1, to, b] = s[at : at + m]
-
-
-def scores_of(h_hi, h_lo, queries, grads, n, m):
+            kept, done = [], 0
+            while done < examples:
+                owner = min(done // m, n - 1)
+                begin = min(owner * m, examples - m)
+                at = (p * n + owner) * m
+                kept.append(s[at + done - begin : at + m])
+                done = begin + m
+            part = jnp.concatenate(kept, 0)
+            top = column_top(part)
+            out[p * n + to] = jnp.concatenate([power(part, top), top], 0).astype(jnp.bfloat16)
+
+
+def scores_of(h_hi, h_lo, queries, grads, n, m, examples):
     masks = sorted(queries)
     blocks = [queries[k] for k in masks]
     width = blocks[0].shape[0]
     return pl.pallas_call(
-        functools.partial(scores_kernel, n, m, masks),
+        functools.partial(scores_kernel, n, m, examples, masks),
         in_specs=[pl.BlockSpec(memory_space=pltpu.VMEM)] * (3 + n),
         out_specs=pl.BlockSpec(memory_space=pltpu.VMEM),
-        out_shape=jax.ShapeDtypeStruct((2, n // 2, n, n, m, width), jnp.float32),
+        out_shape=jax.ShapeDtypeStruct((n * n, examples + 1, width), jnp.bfloat16),
         scratch_shapes=[pltpu.VMEM((n * n * m, R // n // 2 * LANES), jnp.float32)],
         compiler_params=params(40),
     )(h_hi, h_lo, grads, *blocks)
-
-
-def each(count, body):
-    if count <= 8:
-        for i in range(count):
-            body(i)
-    else:
-        lax.fori_loop(0, count, lambda i, c: (body(i), c)[1], 0)
-
-
-def pack_kernel(n, m, examples, ours, theirs, out):
-    def one(i):
-        x, t = i // n, i % n
-        rows, done = [], 0
-        while done < examples:
-            owner = min(done // m, n - 1)
-            begin = min(owner * m, examples - m)
-            both = ours[0, x, t, owner] + theirs[x, t, owner]
-            rows.append(both[done - begin :])
-            done = begin + m
-        both = jnp.concatenate(rows, 0)
-        top = column_top(both)
-        out[i] = jnp.concatenate([power(both, top), top], 0).astype(jnp.bfloat16)
-
-    each(n * n // 2, one)
-
-
-def pack(ours, theirs, n, m, examples):
-    width = ours.shape[-1]
-    return pl.pallas_call(
-        functools.partial(pack_kernel, n, m, examples),
-        in_specs=[pl.BlockSpec(memory_space=pltpu.VMEM)] * 2,
-        out_specs=pl.BlockSpec(memory_space=pltpu.VMEM),
-        out_shape=jax.ShapeDtypeStruct((n * n // 2, examples + 1, width), jnp.bfloat16),
-        compiler_params=params(40),
-    )(ours, theirs)
 
 
 def unpack_kernel(examples, scale, y_ref, out):
@@ -255,7 +226,7 @@
         return root(y[:examples]) * y[examples:]
 
     count = y_ref.shape[0]
-    if count <= 8:
+    if count <= 16:
         total = sum(term(i) for i in range(count))
     else:
         total = lax.fori_loop(1, count, lambda i, c: c + term(i), term(0))
@@ -301,10 +272,8 @@
         all_q.update({k | (1 << b): flip(v, 1 << b) for k, v in all_q.items()})
 
     grads_all = lax.all_to_all(grads, ("dp", "tensor"), 0, 0, tiled=True)
-    out = scores_of(h_hi, h_lo, all_q, grads_all, n, m)
-    out = pack(out, flip(out[1], 1), n, m, examples)
-    same_core = [[(2 * x + core) * n + t for x in range(n // 2) for t in range(n)] for core in range(2)]
-    out = lax.all_to_all(out, ("dp", "tensor"), 0, 0, tiled=True, axis_index_groups=same_core)
+    out = scores_of(h_hi, h_lo, all_q, grads_all, n, m, examples)
+    out = lax.all_to_all(out, ("dp", "tensor"), 0, 0, tiled=True)
     return unpack(out, (1.0 / math.sqrt(SEQ)) * (1.0 / math.sqrt(R * R)) / (TOP * TOP) / TOP)
 
 

time: 53.2 us -> 52.7 us (level)
  waiting for transfers between devices: 1.23 us -> 0.02 us
  blocking collectives: 22.5 us -> 23.5 us
    ppermute x4 -> x3, waiting for transfers between devices: 1.22 us -> 0.01 us  [flip(): return lax.ppermute(v, 'dp', [(i, i ^ mask) for i in range(n)])]
    all_to_all x1, blocking collectives: 10.6 us -> 11.6 us  [local(): out = lax.all_to_all(out, ('dp', 'tensor'), 0, 0, tiled=True)]
    ppermute x4 -> x3, starting transfers between devices: 3.8 us -> 3.51 us  [flip(): return lax.ppermute(v, 'dp', [(i, i ^ mask) for i in range(n)])]
    pallas_call x2 -> x1, Pallas kernels: 2 us -> 1.91 us  [scores_of(): pl.pallas_call(functools.partial(scores_kernel, n, m, examples, masks), i...]
  transfers between devices with their start and end apart: 7 -> 6, of which waited for: 1 -> 0; matrix products, arithmetic and copies ran while one was open for 0% -> 0% of each run, Pallas kernels for 31% -> 31%
where the time goes in v7:
time: 52.7 us; the launch traced here: 52.5 us
  blocking collectives  23.5 us (45%)
  Pallas kernels  20.2 us (38%)
  starting transfers between devices  7.68 us (15%)
  local copies, waits for them, and re-layouts  0.96 us (2%)
    pallas_call x3, Pallas kernels, project(): pl.pallas_call(functools.partial(project_kernel, masks), grid=(len(masks)...  15.9 us
    all_to_all x1, blocking collectives, local(): grads_all = lax.all_to_all(grads, ('dp', 'tensor'), 0, 0, tiled=True)  11.9 us
    all_to_all x1, blocking collectives, local(): out = lax.all_to_all(out, ('dp', 'tensor'), 0, 0, tiled=True)  11.6 us
    ppermute x3, starting transfers between devices, along(): return lax.ppermute(v, 'tensor', [(i, i ^ mask) for i in range(n)])  4.17 us
    ppermute x3, starting transfers between devices, flip(): return lax.ppermute(v, 'dp', [(i, i ^ mask) for i in range(n)])  3.51 us
    pallas_call x1, Pallas kernels, scores_of(): pl.pallas_call(functools.partial(scores_kernel, n, m, examples, masks), i...  1.91 us
  transfers between devices with their start and end apart: 6, of which 0 were waited for; matrix products, arithmetic and copies ran while one was open for 0% of the time, Pallas kernels for 31%

profile of v7, /device:TPU:0, one launch (start us, length us, event | category | flops | bytes accessed | tf_op | source)
XLA Modules:
  0.0 52.5 jit_solution(2337708966482716333)
XLA Ops:
  0.0 2.9 %collective-permute-start.3 = (bf16[384,1024]{1,0:T(8,128)(2,1)}, bf16[384,1024]{1,0:T(8,128)(2,1)S(1)}, u32[]{:S(2)}, u32[]{:S(2)}) collective-permute-start(bf16[384,1024]{1,0:T(8,128)(2,1)} %refs_1_), channel_id=1, source_target_pairs={{0,8},{4,12},{8,0},{12,4},{1,9},{5,13},{9,1},{13,5},{2,10},{6,14},... | collective-permute-start | bytes 2359304 | tf_op jit(solution)/shard_map/ppermute | solution.py:255
  2.9 6.4 %shard_map.64 = (bf16[528,128]{1,0:T(8,128)(2,1)}, bf16[528,128]{1,0:T(8,128)(2,1)}) custom-call(bf16[1920,3584]{1,0:T(8,128)(2,1)} %acts.5, bf16[1920,1024]{1,0:T(8,128)(2,1)} %outs.3, bf16[64,3584]{1,0:T(8,128)(2,1)} %p_in.5, bf16[64,1024]{1,0:T(8,128)(2,1)} %p_out.5), custom_call_target="tpu_custom_call" | custom-call | flops 1 | bytes 1 | tf_op jit(solution)/shard_map/pallas_call | solution.py:90
  9.3 2.6 %collective-permute-start = (bf16[528,128]{1,0:T(8,128)(2,1)}, bf16[528,128]{1,0:T(8,128)(2,1)S(1)}, u32[]{:S(2)}, u32[]{:S(2)}) collective-permute-start(bf16[528,128]{1,0:T(8,128)(2,1)} %get-tuple-element.13), channel_id=1, source_target_pairs={{0,2},{1,3},{2,0},{3,1},{4,6},{5,7},{6,4},{7,5},{8,10},{9,11},{10,... | collective-permute-start | bytes 405512 | tf_op jit(solution)/shard_map/ppermute | solution.py:252
  11.9 1.4 %collective-permute-start.1 = (bf16[528,128]{1,0:T(8,128)(2,1)}, bf16[528,128]{1,0:T(8,128)(2,1)S(1)}, u32[]{:S(2)}, u32[]{:S(2)}) collective-permute-start(bf16[528,128]{1,0:T(8,128)(2,1)} %get-tuple-element.14), channel_id=1, source_target_pairs={{0,3},{1,2},{2,1},{3,0},{4,7},{5,6},{6,5},{7,4},{8,11},{9,10},{10,... | collective-permute-start | bytes 405512 | tf_op jit(solution)/shard_map/ppermute | solution.py:252
  13.3 4.7 %shard_map.65 = bf16[528,128]{1,0:T(8,128)(2,1)} custom-call(bf16[1920,3584]{1,0:T(8,128)(2,1)} %acts.5, bf16[1920,1024]{1,0:T(8,128)(2,1)} %outs.3, bf16[64,3584]{1,0:T(8,128)(2,1)} %p_in.5, bf16[64,1024]{1,0:T(8,128)(2,1)} %p_out.5), custom_call_target="tpu_custom_call" | custom-call | flops 1 | bytes 1 | tf_op jit(solution)/shard_map/pallas_call | solution.py:90
  18.0 0.0 copy-start
  18.0 0.2 collective-permute-start.2
  18.2 4.8 %shard_map.66.refs_0_ = f32[512,128]{1,0:T(8,128)} custom-call(bf16[1920,3584]{1,0:T(8,128)(2,1)} %acts.5, bf16[1920,1024]{1,0:T(8,128)(2,1)} %outs.3, bf16[64,3584]{1,0:T(8,128)(2,1)} %p_in.5, bf16[64,1024]{1,0:T(8,128)(2,1)} %p_out.5), custom_call_target="tpu_custom_call" | custom-call | flops 1 | bytes 1 | tf_op jit(solution)/shard_map/pallas_call | solution.py:90
  23.0 0.0 copy-done
  23.0 0.0 copy-start.1
  23.0 0.9 %copy-done.1 = f32[512,128]{1,0:T(8,128)S(1)} copy-done((f32[512,128]{1,0:T(8,128)S(1)}, f32[512,128]{1,0:T(8,128)}, u32[]{:S(2)}) %copy-start.1) | copy-done | bytes 262168
  24.0 0.0 copy-start.2
  24.0 0.6 %shard_map.67 = (bf16[1024,1024]{1,0:T(8,128)(2,1)S(1)}, bf16[1024,1024]{1,0:T(8,128)(2,1)S(1)}) custom-call(f32[1024,1024]{1,0:T(8,128)S(1)} %copy-done, f32[512,128]{1,0:T(8,128)S(1)} %copy-done.1), custom_call_target="tpu_custom_call" | custom-call | flops 1 | bytes 1 | tf_op jit(solution)/shard_map/pallas_call | solution.py:164
  24.6 0.0 collective-permute-done.2.refs_2_
  24.6 0.0 collective-permute-done.refs_0_
  24.6 0.0 collective-permute-done.1.refs_1_
  24.6 0.0 collective-permute-done.3.refs_4_.refs_3_
  24.6 0.9 %shard_map.68 = bf16[16,36,128]{2,1,0:T(8,128)(2,1)S(1)} custom-call(f32[512,128]{1,0:T(8,128)S(1)} %broadcast_multiply_fusion.own, bf16[528,128]{1,0:T(8,128)(2,1)S(1)} %collective-permute-done.refs_0_, bf16[528,128]{1,0:T(8,128)(2,1)S(1)} %collective-permute-done.1.refs_1_, bf16[528,128]{1,0:T(8,128)(2,1)S(1)} %collective-permute-done.2.refs_2_, ...), custom_call_target="tpu_custom_call" | custom-call | flops 1 | bytes 1 | tf_op jit(solution)/shard_map/pallas_call | solution.py:143
  25.6 0.0 copy-done.2
  25.6 0.1 collective-permute-start.4
  25.6 0.5 collective-permute-start.5
  26.1 11.9 %all_to_all.10.refs_0_ = bf16[16,36,128]{2,1,0:T(8,128)(2,1)S(1)} all-to-all(bf16[16,36,128]{2,1,0:T(8,128)(2,1)S(1)} %shard_map.68), channel_id=1, replica_groups=mesh['groups'=2,'dp'=4,'tensor'=4] {'dp','tensor'}, dimensions={0} | all-to-all | bytes 294912 | tf_op jit(solution)/shard_map/all_to_all | solution.py:274
  38.0 0.0 collective-permute-done.4.refs_2_
  38.1 0.0 collective-permute-done.5.refs_4_
  38.1 1.9 %shard_map.69 = bf16[16,16,384]{2,1,0:T(8,128)(2,1)S(1)} custom-call(bf16[1024,1024]{1,0:T(8,128)(2,1)S(1)} %get-tuple-element.17.refs_3_.h_hi, bf16[1024,1024]{1,0:T(8,128)(2,1)S(1)} %get-tuple-element.18.h_lo, bf16[16,36,128]{2,1,0:T(8,128)(2,1)S(1)} %all_to_all.10.refs_0_, bf16[384,1024]{1,0:T(8,128)(2,1)S(1)} %copy-done.2, ...), custom_call_target="tpu_custom_call" | custom-call | tf_op jit(solution)/shard_map/pallas_call | solution.py:213
  40.0 11.6 %all_to_all.11.y_ref = bf16[16,16,384]{2,1,0:T(8,128)(2,1)S(1)} all-to-all(bf16[16,16,384]{2,1,0:T(8,128)(2,1)S(1)} %shard_map.69), channel_id=1, replica_groups=mesh['groups'=2,'dp'=4,'tensor'=4] {'dp','tensor'}, dimensions={0} | all-to-all | bytes 393216 | tf_op jit(solution)/shard_map/all_to_all | solution.py:276
  51.6 0.9 %shard_map.70 = f32[15,384]{1,0:T(8,128)} custom-call(bf16[16,16,384]{2,1,0:T(8,128)(2,1)S(1)} %all_to_all.11.y_ref), custom_call_target="tpu_custom_call" | custom-call | tf_op jit(solution)/shard_map/pallas_call | solution.py:238
  (1 shorter events, 0.0 us)
Async XLA Ops:
  0.0 24.6 %collective-permute-start.3 = (bf16[384,1024]{1,0:T(8,128)(2,1)}, bf16[384,1024]{1,0:T(8,128)(2,1)S(1)}, u32[]{:S(2)}, u32[]{:S(2)}) collective-permute-start(bf16[384,1024]{1,0:T(8,128)(2,1)} %refs_1_), channel_id=1, source_target_pairs={{0,8},{4,12},{8,0},{12,4},{1,9},{5,13},{9,1},{13,5},{2,10},{6,14},... | collective-permute-start | bytes 2359304 | tf_op jit(solution)/shard_map/ppermute | solution.py:255
  9.3 15.3 %collective-permute-start = (bf16[528,128]{1,0:T(8,128)(2,1)}, bf16[528,128]{1,0:T(8,128)(2,1)S(1)}, u32[]{:S(2)}, u32[]{:S(2)}) collective-permute-start(bf16[528,128]{1,0:T(8,128)(2,1)} %get-tuple-element.13), channel_id=1, source_target_pairs={{0,2},{1,3},{2,0},{3,1},{4,6},{5,7},{6,4},{7,5},{8,10},{9,11},{10,... | collective-permute-start | bytes 405512 | tf_op jit(solution)/shard_map/ppermute | solution.py:252
  11.9 12.7 %collective-permute-start.1 = (bf16[528,128]{1,0:T(8,128)(2,1)}, bf16[528,128]{1,0:T(8,128)(2,1)S(1)}, u32[]{:S(2)}, u32[]{:S(2)}) collective-permute-start(bf16[528,128]{1,0:T(8,128)(2,1)} %get-tuple-element.14), channel_id=1, source_target_pairs={{0,3},{1,2},{2,1},{3,0},{4,7},{5,6},{6,5},{7,4},{8,11},{9,10},{10,... | collective-permute-start | bytes 405512 | tf_op jit(solution)/shard_map/ppermute | solution.py:252
  18.0 5.0 %copy-start = (f32[1024,1024]{1,0:T(8,128)S(1)}, f32[1024,1024]{1,0:T(8,128)}, u32[]{:S(2)}) copy-start(f32[1024,1024]{1,0:T(8,128)} %h.1) | copy-start | bytes 12582916
  18.0 6.6 %collective-permute-start.2 = (bf16[528,128]{1,0:T(8,128)(2,1)}, bf16[528,128]{1,0:T(8,128)(2,1)S(1)}, u32[]{:S(2)}, u32[]{:S(2)}) collective-permute-start(bf16[528,128]{1,0:T(8,128)(2,1)} %shard_map.65), channel_id=1, source_target_pairs={{0,1},{1,0},{2,3},{3,2},{4,5},{5,4},{6,7},{7,6},{8,9},{9,8},{10,11... | collective-permute-start | bytes 405512 | tf_op jit(solution)/shard_map/ppermute | solution.py:252
  23.0 1.0 %copy-start.1 = (f32[512,128]{1,0:T(8,128)S(1)}, f32[512,128]{1,0:T(8,128)}, u32[]{:S(2)}) copy-start(f32[512,128]{1,0:T(8,128)} %shard_map.66.refs_0_) | copy-start | bytes 786436
  24.0 1.6 %copy-start.2 = (bf16[384,1024]{1,0:T(8,128)(2,1)S(1)}, bf16[384,1024]{1,0:T(8,128)(2,1)}, u32[]{:S(2)}) copy-start(bf16[384,1024]{1,0:T(8,128)(2,1)} %refs_1_) | copy-start | bytes 2359300
  25.6 12.5 %collective-permute-start.4 = (bf16[384,1024]{1,0:T(8,128)(2,1)S(1)}, bf16[384,1024]{1,0:T(8,128)(2,1)S(1)}, u32[]{:S(2)}, u32[]{:S(2)}) collective-permute-start(bf16[384,1024]{1,0:T(8,128)(2,1)S(1)} %copy-done.2), channel_id=1, source_target_pairs={{0,4},{4,0},{8,12},{12,8},{1,5},{5,1},{9,13},{13,9},{2,6},{6,2},{1... | collective-permute-start | bytes 2359304 | tf_op jit(solution)/shard_map/ppermute | solution.py:255
  25.6 12.4 %collective-permute-start.5 = (bf16[384,1024]{1,0:T(8,128)(2,1)S(1)}, bf16[384,1024]{1,0:T(8,128)(2,1)S(1)}, u32[]{:S(2)}, u32[]{:S(2)}) collective-permute-start(bf16[384,1024]{1,0:T(8,128)(2,1)S(1)} %collective-permute-done.3.refs_4_.refs_3_), channel_id=1, source_target_pairs={{0,4},{4,0},{8,12},{12,8},{1,5},{5,1},{9,13},{13,9},{2,6},{6,2},{1... | collective-permute-start | bytes 2359304 | tf_op jit(solution)/shard_map/ppermute | solution.py:255

commit v8 on v7

--- a/solution.py
+++ b/solution.py
@@ -151,28 +151,7 @@
     )(own, *coded, *wait_for)
 
 
-def halves_kernel(h, *refs):
-    hi, lo = split(h[...])
-    refs[-2][...] = hi
-    refs[-1][...] = lo
-
-
-def halves(h, wait_for):
-    rows = h.shape[0] // 4 if h.shape[0] % 64 == 0 else h.shape[0]
-    spec = pl.BlockSpec((rows, h.shape[1]), lambda i: (i, 0))
-    shape = jax.ShapeDtypeStruct(h.shape, jnp.bfloat16)
-    return pl.pallas_call(
-        halves_kernel,
-        grid=(h.shape[0] // rows,),
-        in_specs=[spec] + [pl.BlockSpec(memory_space=pl.ANY)] * len(wait_for),
-        out_specs=[spec, spec],
-        out_shape=[shape, shape],
-        compiler_params=params(24),
-        cost_estimate=pl.CostEstimate(flops=1, bytes_accessed=1, transcendentals=0),
-    )(h, *wait_for)
-
-
-def scores_kernel(n, m, examples, masks, h_hi, h_lo, *refs):
+def scores_kernel(n, m, examples, masks, h, *refs):
     grads, queries, out, a = refs[0], refs[1 : n + 1], refs[n + 1], refs[n + 2]
     half = R // n // 2
     rows = n * n * m
@@ -184,8 +163,14 @@
             a[pl.ds(s * m, m), pl.ds(r * LANES, LANES)] = w[r * m : (r + 1) * m] * top
     contract = (((1,), (0,)), ((), ()))
     hi, lo = split(a[...])
-    top = lax.dot_general(jnp.concatenate([hi, lo], 0), h_hi[...], contract, preferred_element_type=jnp.float32)
-    low = lax.dot_general(hi, h_lo[...], contract, preferred_element_type=jnp.float32)
+    left = jnp.concatenate([hi, lo], 0)
+    step = min(256, h.shape[0])
+    top, low = None, None
+    for k in range(0, h.shape[0], step):
+        h_hi, h_lo = split(h[pl.ds(k, step), :])
+        one = lax.dot_general(left[:, k : k + step], h_hi, contract, preferred_element_type=jnp.float32)
+        two = lax.dot_general(hi[:, k : k + step], h_lo, contract, preferred_element_type=jnp.float32)
+        top, low = (one, two) if top is None else (top + one, low + two)
     hi, lo = split(top[:rows] + top[rows:] + low)
     both = jnp.concatenate([hi, lo], 0)
     d = lax.axis_index("dp")
@@ -206,18 +191,18 @@
             out[p * n + to] = jnp.concatenate([power(part, top), top], 0).astype(jnp.bfloat16)
 
 
-def scores_of(h_hi, h_lo, queries, grads, n, m, examples):
+def scores_of(h, queries, grads, n, m, examples):
     masks = sorted(queries)
     blocks = [queries[k] for k in masks]
     width = blocks[0].shape[0]
     return pl.pallas_call(
         functools.partial(scores_kernel, n, m, examples, masks),
-        in_specs=[pl.BlockSpec(memory_space=pltpu.VMEM)] * (3 + n),
+        in_specs=[pl.BlockSpec(memory_space=pltpu.VMEM)] * (2 + n),
         out_specs=pl.BlockSpec(memory_space=pltpu.VMEM),
         out_shape=jax.ShapeDtypeStruct((n * n, examples + 1, width), jnp.bfloat16),
         scratch_shapes=[pltpu.VMEM((n * n * m, R // n // 2 * LANES), jnp.float32)],
         compiler_params=params(40),
-    )(h_hi, h_lo, grads, *blocks)
+    )(h, grads, *blocks)
 
 
 def unpack_kernel(examples, scale, y_ref, out):
@@ -265,14 +250,13 @@
     (near,) = project(activations, after(out_grads, y), proj_in, proj_out, [1], m, 59)
     (own,) = project(activations, after(out_grads, near), proj_in, proj_out, [0], m, 57)
     coded = [along(v, mask) for v, mask in zip(y, far)] + [along(near, 1)]
-    h_hi, h_lo = halves(hess_inv, [own])
-    grads = grads_of(own * TOP, coded, [h_hi, all_q[n // 2]], n, m)
+    grads = grads_of(own * TOP, coded, [all_q[n // 2]], n, m)
     for b in reversed(range(bits - 1)):
         all_q = dict(zip(all_q, after(tuple(all_q.values()), grads)))
         all_q.update({k | (1 << b): flip(v, 1 << b) for k, v in all_q.items()})
 
     grads_all = lax.all_to_all(grads, ("dp", "tensor"), 0, 0, tiled=True)
-    out = scores_of(h_hi, h_lo, all_q, grads_all, n, m, examples)
+    out = scores_of(hess_inv, all_q, grads_all, n, m, examples)
     out = lax.all_to_all(out, ("dp", "tensor"), 0, 0, tiled=True)
     return unpack(out, (1.0 / math.sqrt(SEQ)) * (1.0 / math.sqrt(R * R)) / (TOP * TOP) / TOP)
 

time: 52.7 us -> 52.7 us (level)
  other arithmetic: 0.02 us -> 0.97 us
  local copies, waits for them, and re-layouts: 0.96 us -> 0.01 us
    unnamed x6 -> x4, local copies, waits for them, and re-layouts: 0.96 us -> 0.01 us
    mul x1, other arithmetic: 0.02 us -> 0.97 us  [local(): grads = grads_of(own * TOP, coded, [all_q[n // 2]], n, m)]
    pallas_call x1 -> x0, Pallas kernels: 0.6 us -> none  [halves(): pl.pallas_call(halves_kernel, grid=(h.shape[0] // rows,), in_specs=[spec]...]
  transfers between devices with their start and end apart: 6 -> 6, of which waited for: 0 -> 1; matrix products, arithmetic and copies ran while one was open for 0% -> 2% of each run, Pallas kernels for 31% -> 30%
where the time goes in v8:
time: 52.7 us; the launch traced here: 52.5 us
  blocking collectives  23.9 us (45%)
  Pallas kernels  19.7 us (37%)
  starting transfers between devices  7.68 us (15%)
  other arithmetic  0.97 us (2%)
    pallas_call x3, Pallas kernels, project(): pl.pallas_call(functools.partial(project_kernel, masks), grid=(len(masks)...  15.9 us
    all_to_all x1, blocking collectives, local(): grads_all = lax.all_to_all(grads, ('dp', 'tensor'), 0, 0, tiled=True)  12.3 us
    all_to_all x1, blocking collectives, local(): out = lax.all_to_all(out, ('dp', 'tensor'), 0, 0, tiled=True)  11.6 us
    ppermute x3, starting transfers between devices, along(): return lax.ppermute(v, 'tensor', [(i, i ^ mask) for i in range(n)])  4.17 us
    ppermute x3, starting transfers between devices, flip(): return lax.ppermute(v, 'dp', [(i, i ^ mask) for i in range(n)])  3.51 us
    pallas_call x1, Pallas kernels, scores_of(): pl.pallas_call(functools.partial(scores_kernel, n, m, examples, masks), i...  2.03 us
  transfers between devices with their start and end apart: 6, of which 1 were waited for; matrix products, arithmetic and copies ran while one was open for 2% of the time, Pallas kernels for 30%

profile of v8, /device:TPU:0, one launch (start us, length us, event | category | flops | bytes accessed | tf_op | source)
XLA Modules:
  0.0 52.5 jit_solution(18073259505339025279)
XLA Ops:
  0.0 2.9 %collective-permute-start.3 = (bf16[384,1024]{1,0:T(8,128)(2,1)}, bf16[384,1024]{1,0:T(8,128)(2,1)S(1)}, u32[]{:S(2)}, u32[]{:S(2)}) collective-permute-start(bf16[384,1024]{1,0:T(8,128)(2,1)} %refs_1_), channel_id=1, source_target_pairs={{0,8},{4,12},{8,0},{12,4},{1,9},{5,13},{9,1},{13,5},{2,10},{6,14},... | collective-permute-start | bytes 2359304 | tf_op jit(solution)/shard_map/ppermute | solution.py:240
  2.9 6.4 %shard_map.64 = (bf16[528,128]{1,0:T(8,128)(2,1)}, bf16[528,128]{1,0:T(8,128)(2,1)}) custom-call(bf16[1920,3584]{1,0:T(8,128)(2,1)} %acts.5, bf16[1920,1024]{1,0:T(8,128)(2,1)} %outs.3, bf16[64,3584]{1,0:T(8,128)(2,1)} %p_in.5, bf16[64,1024]{1,0:T(8,128)(2,1)} %p_out.5), custom_call_target="tpu_custom_call" | custom-call | flops 1 | bytes 1 | tf_op jit(solution)/shard_map/pallas_call | solution.py:90
  9.3 2.6 %collective-permute-start = (bf16[528,128]{1,0:T(8,128)(2,1)}, bf16[528,128]{1,0:T(8,128)(2,1)S(1)}, u32[]{:S(2)}, u32[]{:S(2)}) collective-permute-start(bf16[528,128]{1,0:T(8,128)(2,1)} %get-tuple-element.11), channel_id=1, source_target_pairs={{0,2},{1,3},{2,0},{3,1},{4,6},{5,7},{6,4},{7,5},{8,10},{9,11},{10,... | collective-permute-start | bytes 405512 | tf_op jit(solution)/shard_map/ppermute | solution.py:237
  11.9 1.4 %collective-permute-start.1 = (bf16[528,128]{1,0:T(8,128)(2,1)}, bf16[528,128]{1,0:T(8,128)(2,1)S(1)}, u32[]{:S(2)}, u32[]{:S(2)}) collective-permute-start(bf16[528,128]{1,0:T(8,128)(2,1)} %get-tuple-element.12), channel_id=1, source_target_pairs={{0,3},{1,2},{2,1},{3,0},{4,7},{5,6},{6,5},{7,4},{8,11},{9,10},{10,... | collective-permute-start | bytes 405512 | tf_op jit(solution)/shard_map/ppermute | solution.py:237
  13.3 4.7 %shard_map.65 = bf16[528,128]{1,0:T(8,128)(2,1)} custom-call(bf16[1920,3584]{1,0:T(8,128)(2,1)} %acts.5, bf16[1920,1024]{1,0:T(8,128)(2,1)} %outs.3, bf16[64,3584]{1,0:T(8,128)(2,1)} %p_in.5, bf16[64,1024]{1,0:T(8,128)(2,1)} %p_out.5), custom_call_target="tpu_custom_call" | custom-call | flops 1 | bytes 1 | tf_op jit(solution)/shard_map/pallas_call | solution.py:90
  18.0 0.0 copy-start.1
  18.0 0.2 collective-permute-start.2
  18.2 0.0 copy-start
  18.2 4.8 %shard_map.66 = f32[512,128]{1,0:T(8,128)} custom-call(bf16[1920,3584]{1,0:T(8,128)(2,1)} %acts.5, bf16[1920,1024]{1,0:T(8,128)(2,1)} %outs.3, bf16[64,3584]{1,0:T(8,128)(2,1)} %p_in.5, bf16[64,1024]{1,0:T(8,128)(2,1)} %p_out.5), custom_call_target="tpu_custom_call" | custom-call | flops 1 | bytes 1 | tf_op jit(solution)/shard_map/pallas_call | solution.py:90
  23.0 1.0 %broadcast_multiply_fusion.own = f32[512,128]{1,0:T(8,128)S(1)} fusion(f32[512,128]{1,0:T(8,128)} %shard_map.66), kind=kLoop, calls=%fused_computation | loop fusion | flops 65536 | bytes 524288 | tf_op jit(solution)/shard_map/mul | solution.py:253
  24.0 0.2 collective-permute-done.2.refs_2_
  24.2 0.0 collective-permute-done.refs_0_
  24.2 0.0 collective-permute-done.1.refs_1_
  24.2 0.0 collective-permute-done.3.refs_3_
  24.2 0.9 %shard_map.67 = bf16[16,36,128]{2,1,0:T(8,128)(2,1)S(1)} custom-call(f32[512,128]{1,0:T(8,128)S(1)} %broadcast_multiply_fusion.own, bf16[528,128]{1,0:T(8,128)(2,1)S(1)} %collective-permute-done.refs_0_, bf16[528,128]{1,0:T(8,128)(2,1)S(1)} %collective-permute-done.1.refs_1_, bf16[528,128]{1,0:T(8,128)(2,1)S(1)} %collective-permute-done.2.refs_2_, ...), custom_call_target="tpu_custom_call" | custom-call | flops 1 | bytes 1 | tf_op jit(solution)/shard_map/pallas_call | solution.py:143
  25.1 0.0 copy-done.1
  25.1 0.1 collective-permute-start.4
  25.2 0.5 collective-permute-start.5
  25.7 12.3 %all_to_all.10.refs_0_ = bf16[16,36,128]{2,1,0:T(8,128)(2,1)S(1)} all-to-all(bf16[16,36,128]{2,1,0:T(8,128)(2,1)S(1)} %shard_map.67), channel_id=1, replica_groups=mesh['groups'=2,'dp'=4,'tensor'=4] {'dp','tensor'}, dimensions={0} | all-to-all | bytes 294912 | tf_op jit(solution)/shard_map/all_to_all | solution.py:258
  38.0 0.0 collective-permute-done.4.refs_2_
  38.0 0.0 collective-permute-done.5.refs_4_
  38.0 0.0 copy-done
  38.0 2.0 %shard_map.68 = bf16[16,16,384]{2,1,0:T(8,128)(2,1)S(1)} custom-call(f32[1024,1024]{1,0:T(8,128)S(1)} %copy-done, bf16[16,36,128]{2,1,0:T(8,128)(2,1)S(1)} %all_to_all.10.refs_0_, bf16[384,1024]{1,0:T(8,128)(2,1)S(1)} %copy-done.1, bf16[384,1024]{1,0:T(8,128)(2,1)S(1)} %collective-permute-done.4.refs_2_, ...), custom_call_target="tpu_custom_call" | custom-call | tf_op jit(solution)/shard_map/pallas_call | solution.py:198
  40.0 11.6 %all_to_all.11.y_ref = bf16[16,16,384]{2,1,0:T(8,128)(2,1)S(1)} all-to-all(bf16[16,16,384]{2,1,0:T(8,128)(2,1)S(1)} %shard_map.68), channel_id=1, replica_groups=mesh['groups'=2,'dp'=4,'tensor'=4] {'dp','tensor'}, dimensions={0} | all-to-all | bytes 393216 | tf_op jit(solution)/shard_map/all_to_all | solution.py:260
  51.6 0.9 %shard_map.69 = f32[15,384]{1,0:T(8,128)} custom-call(bf16[16,16,384]{2,1,0:T(8,128)(2,1)S(1)} %all_to_all.11.y_ref), custom_call_target="tpu_custom_call" | custom-call | tf_op jit(solution)/shard_map/pallas_call | solution.py:223
Async XLA Ops:
  0.0 24.2 %collective-permute-start.3 = (bf16[384,1024]{1,0:T(8,128)(2,1)}, bf16[384,1024]{1,0:T(8,128)(2,1)S(1)}, u32[]{:S(2)}, u32[]{:S(2)}) collective-permute-start(bf16[384,1024]{1,0:T(8,128)(2,1)} %refs_1_), channel_id=1, source_target_pairs={{0,8},{4,12},{8,0},{12,4},{1,9},{5,13},{9,1},{13,5},{2,10},{6,14},... | collective-permute-start | bytes 2359304 | tf_op jit(solution)/shard_map/ppermute | solution.py:240
  9.3 14.8 %collective-permute-start = (bf16[528,128]{1,0:T(8,128)(2,1)}, bf16[528,128]{1,0:T(8,128)(2,1)S(1)}, u32[]{:S(2)}, u32[]{:S(2)}) collective-permute-start(bf16[528,128]{1,0:T(8,128)(2,1)} %get-tuple-element.11), channel_id=1, source_target_pairs={{0,2},{1,3},{2,0},{3,1},{4,6},{5,7},{6,4},{7,5},{8,10},{9,11},{10,... | collective-permute-start | bytes 405512 | tf_op jit(solution)/shard_map/ppermute | solution.py:237
  11.9 12.3 %collective-permute-start.1 = (bf16[528,128]{1,0:T(8,128)(2,1)}, bf16[528,128]{1,0:T(8,128)(2,1)S(1)}, u32[]{:S(2)}, u32[]{:S(2)}) collective-permute-start(bf16[528,128]{1,0:T(8,128)(2,1)} %get-tuple-element.12), channel_id=1, source_target_pairs={{0,3},{1,2},{2,1},{3,0},{4,7},{5,6},{6,5},{7,4},{8,11},{9,10},{10,... | collective-permute-start | bytes 405512 | tf_op jit(solution)/shard_map/ppermute | solution.py:237
  18.0 7.1 %copy-start.1 = (bf16[384,1024]{1,0:T(8,128)(2,1)S(1)}, bf16[384,1024]{1,0:T(8,128)(2,1)}, u32[]{:S(2)}) copy-start(bf16[384,1024]{1,0:T(8,128)(2,1)} %refs_1_) | copy-start | bytes 2359300
  18.0 6.2 %collective-permute-start.2 = (bf16[528,128]{1,0:T(8,128)(2,1)}, bf16[528,128]{1,0:T(8,128)(2,1)S(1)}, u32[]{:S(2)}, u32[]{:S(2)}) collective-permute-start(bf16[528,128]{1,0:T(8,128)(2,1)} %shard_map.65), channel_id=1, source_target_pairs={{0,1},{1,0},{2,3},{3,2},{4,5},{5,4},{6,7},{7,6},{8,9},{9,8},{10,11... | collective-permute-start | bytes 405512 | tf_op jit(solution)/shard_map/ppermute | solution.py:237
  18.2 19.8 %copy-start = (f32[1024,1024]{1,0:T(8,128)S(1)}, f32[1024,1024]{1,0:T(8,128)}, u32[]{:S(2)}) copy-start(f32[1024,1024]{1,0:T(8,128)} %h.1) | copy-start | bytes 12582916
  25.1 12.9 %collective-permute-start.4 = (bf16[384,1024]{1,0:T(8,128)(2,1)S(1)}, bf16[384,1024]{1,0:T(8,128)(2,1)S(1)}, u32[]{:S(2)}, u32[]{:S(2)}) collective-permute-start(bf16[384,1024]{1,0:T(8,128)(2,1)S(1)} %copy-done.1), channel_id=1, source_target_pairs={{0,4},{4,0},{8,12},{12,8},{1,5},{5,1},{9,13},{13,9},{2,6},{6,2},{1... | collective-permute-start | bytes 2359304 | tf_op jit(solution)/shard_map/ppermute | solution.py:240
  25.2 12.8 %collective-permute-start.5 = (bf16[384,1024]{1,0:T(8,128)(2,1)S(1)}, bf16[384,1024]{1,0:T(8,128)(2,1)S(1)}, u32[]{:S(2)}, u32[]{:S(2)}) collective-permute-start(bf16[384,1024]{1,0:T(8,128)(2,1)S(1)} %collective-permute-done.3.refs_3_), channel_id=1, source_target_pairs={{0,4},{4,0},{8,12},{12,8},{1,5},{5,1},{9,13},{13,9},{2,6},{6,2},{1... | collective-permute-start | bytes 2359304 | tf_op jit(solution)/shard_map/ppermute | solution.py:240
